TPU v7x, 32 devices: a whole 2x2x4 slice. The times are simulated.
32 devices in a mesh: groups: 2 (over x), aux: 16 (over z, y, core).
Axes of the slice: x: 2, y: 2, z: 4, core: 2. Of those that a mesh axis runs over, the one named last changes fastest.
Arguments:
- integrals: bfloat16 [10240, 128, 128], P(('groups', 'aux')), parts along dimension 0, may hold values from -6 to 6
- block_index: int32 [10240, 3], P(('groups', 'aux')), parts along dimension 0, may hold values from 0 to 23, as said below
- live_count: int32 [32], P(('groups', 'aux')), parts along dimension 0, may hold values from 1 to 320, as said below
- orbitals: bfloat16 [6144, 128], P('groups'), parts along dimension 0, may hold values from -0.109375 to 0.109375
- metric: float32 [512, 256], P('groups'), parts along dimension 0, may hold values from -0.0234375 to 0.0234375
Outputs:
- exchange_applied: float32 [6144, 128], P(('groups', 'aux')), parts along dimension 0
There are 2 independent parts, one for each index of `groups`. A program takes and returns all parts, laid end to end along the dimension named above; each array names one. Nothing has to cross between parts.
Inputs may be any that keep to these rules, and one draw needn't show every extreme that they name: `block_index`: columns 1 and 2 lie in 0 to 23, column 0 in 0 to 15. `live_count`: slots from this number on hold no data.
All inputs are finite; a program needn't handle non-finite values.
Results may differ from a plain program's by a relative error of at most 0.0049.
Values may be sent and summed in bfloat16 or wider, within the bound.
No kernel may reach another device: no remote copies, remote signals or barrier semaphores. Data moves between devices by JAX's collectives and lax.ppermute only.
A program may use at most 128 MiB of HBM per device.

v0:
```python
import jax
import jax.numpy as jnp
from jax import lax
from jax.sharding import PartitionSpec as P

Q_DEV = 16


def half_transform(blocks, index, live, orbitals):
    block_size = blocks.shape[1]
    basis = orbitals.shape[0]
    occupied = orbitals.shape[1]
    nblk = basis // block_size
    slots = blocks.shape[0]
    q_local = index[:, 0]
    m_block = index[:, 1]
    n_block = index[:, 2]
    orb_blocks = orbitals.reshape(nblk, block_size, occupied)
    orb_rows = orb_blocks[n_block]
    products = jnp.einsum("bmn,bni->bmi", blocks, orb_rows, preferred_element_type=jnp.float32)
    live_mask = (jnp.arange(slots, dtype=jnp.int32) < live).astype(jnp.float32)
    products = products * live_mask[:, None, None]
    slot_ids = q_local * nblk + m_block
    slab = jnp.zeros((Q_DEV * nblk, block_size, occupied), jnp.float32).at[slot_ids].add(products)
    return slab.reshape(Q_DEV, basis, occupied).astype(jnp.bfloat16)


def body(integrals, block_index, live_count, orbitals, metric):
    slab = half_transform(integrals, block_index, live_count[0], orbitals)
    pairs = jnp.einsum("qni,nj->qij", slab, orbitals, preferred_element_type=jnp.float32)
    fitted_here = jnp.einsum(
        "qp,pij->qij",
        metric,
        lax.all_to_all(pairs, "aux", split_axis=1, concat_axis=0, tiled=True),
        precision=lax.Precision.HIGHEST,
    ).astype(jnp.bfloat16)
    fitted = lax.all_to_all(fitted_here, "aux", split_axis=0, concat_axis=1, tiled=True)
    partial_sum = jnp.einsum("qmi,qij->mj", slab, fitted, preferred_element_type=jnp.float32)
    return lax.psum_scatter(partial_sum, "aux", scatter_dimension=0, tiled=True)


def solution(mesh):
    placed = (
        P(("groups", "aux"), None, None),
        P(("groups", "aux"), None),
        P(("groups", "aux")),
        P("groups", None),
        P("groups", None),
    )
    return jax.shard_map(
        body, mesh=mesh, in_specs=placed, out_specs=P(("groups", "aux"), None), check_vma=False
    )
```

profile of v0, /device:TPU:0, one launch (start us, length us, event | category | flops | bytes accessed | tf_op | source)
XLA Modules:
  0.0 282.2 jit_solution(14444143426961658373)
XLA Ops:
  6.5 0.0 copy-start
  6.5 0.0 reduce-scatter.2.cloned.1.call-start
  7.3 0.8 fusion.9
  8.1 0.0 copy-done
  8.1 10.7 %gather_fusion = bf16[320,128,128]{2,1,0:T(8,128)(2,1)} fusion(bf16[24,128,128]{2,1,0:T(8,128)(2,1)S(1)} %bitcast.30, s32[1024]{0:T(1024)S(1)} %pad_clamp_fusion), kind=kCustom, calls=%fused_computation | custom fusion | bytes 20972800 | tf_op jit(solution)/shard_map/gather | solution.py:19
  18.8 19.0 %multiply_bitcast_fusion = f32[320,128,128]{1,2,0:T(8,128)} fusion(f32[320]{0:T(512)S(1)} %fusion.7, bf16[320,128,128]{2,1,0:T(8,128)(2,1)} %gather_fusion, bf16[320,128,128]{2,1,0:T(8,128)(2,1)} %param.5), kind=kOutput, calls=%fused_computation.2 | convolution fusion | flops 1347420160 | bytes 41944320 | tf_op jit(solution)/shard_map/bmn,bni->bmi/dot_general | solution.py:20
  37.9 21.1 %copy.25 = f32[320,128,128]{2,1,0:T(8,128)} copy(f32[320,128,128]{1,2,0:T(8,128)} %multiply_bitcast_fusion) | data formatting | bytes 41943040 | tf_op jit(solution)/shard_map/mul | solution.py:22
  59.0 11.5 %broadcast_in_dim.2 = f32[384,128,128]{2,1,0:T(8,128)} broadcast(f32[]{:T(128)} %constant.0.clone.1), dimensions={} | broadcast | bytes 25165828 | tf_op jit(solution)/shard_map/broadcast_in_dim | solution.py:24
  70.5 66.1 %scatter_fusion = f32[384,128,128]{2,1,0:T(8,128)} fusion(f32[384,128,128]{2,1,0:T(8,128)} %broadcast_in_dim.2, s32[320]{0:T(512)S(1)} %get-tuple-element.6, f32[320,128,128]{2,1,0:T(8,128)} %copy.25), kind=kCustom, calls=%fused_computation.1 | custom fusion | flops 5242880 | bytes 62915840 | tf_op jit(solution)/shard_map/scatter-add | solution.py:24
  136.6 9.5 %convert_element_type.20 = bf16[384,128,128]{2,1,0:T(8,128)(2,1)S(1)} convert(f32[384,128,128]{2,1,0:T(8,128)} %scatter_fusion) | non-fusion elementwise | flops 6291456 | bytes 37748736 | tf_op jit(solution)/shard_map/convert_element_type | solution.py:25
  146.1 0.0 copy-start.1
  146.1 0.0 copy-start.2
  146.1 4.5 %copy-done.1 = bf16[384,128,128]{2,1,0:T(8,128)(2,1)} copy-done((bf16[384,128,128]{2,1,0:T(8,128)(2,1)}, bf16[384,128,128]{2,1,0:T(8,128)(2,1)S(1)}, u32[]{:S(2)}) %copy-start.1) | copy-done | bytes 12582936
  150.7 3.5 %fusion.2 = f32[16,128,128]{2,1,0:T(8,128)S(1)} fusion(bf16[16,3072,128]{2,1,0:T(8,128)(2,1)S(1)} %bitcast.31, bf16[3072,128]{1,0:T(8,128)(2,1)S(1)} %copy-done), kind=kOutput, calls=%fused_computation.7 | convolution fusion | flops 1610612736 | bytes 14417920 | tf_op jit(solution)/shard_map/qni,nj->qij/dot_general | solution.py:30
  154.1 0.6 copy.27
  154.8 32.2 %all_to_all.36 = f32[16,128,128]{2,0,1:T(8,128)S(1)} all-to-all(f32[16,128,128]{2,0,1:T(8,128)S(1)} %copy.27), channel_id=1, replica_groups=mesh['groups'=2,'aux'=16] {'aux'}, dimensions={1} | all-to-all | bytes 2097152 | tf_op jit(solution)/shard_map/all_to_all | solution.py:34
  186.9 0.3 copy.29
  187.3 0.0 copy-done.2
  187.3 1.8 fusion
  189.1 0.3 copy.31
  189.4 19.3 %all_to_all.37 = bf16[256,8,128]{2,1,0:T(8,128)(2,1)S(1)} all-to-all(bf16[256,8,128]{2,1,0:T(8,128)(2,1)S(1)} %copy.31), channel_id=1, replica_groups=mesh['groups'=2,'aux'=16] {'aux'}, dimensions={0} | all-to-all | bytes 1048576 | tf_op jit(solution)/shard_map/all_to_all | solution.py:37
  208.7 7.6 %convolution_bitcast_fusion = f32[3072,128]{1,0:T(8,128)} fusion(bf16[16,3072,128]{2,1,0:T(8,128)(2,1)} %bitcast.32, bf16[16,16,8,128]{3,2,0,1:T(8,128)(2,1)S(1)} %bitcast.35), kind=kOutput, calls=%fused_computation.3 | convolution fusion | flops 1610612736 | bytes 14680064 | tf_op jit(solution)/shard_map/qmi,qij->mj/dot_general | solution.py:38
  216.3 0.0 reduce-scatter.2.cloned.1.call-update
  216.3 59.1 %reduce-scatter.2.cloned.1.call-done = f32[192,128]{1,0:T(8,128)} async-done(((f32[3072,128]{1,0:T(8,128)}), f32[192,128]{1,0:T(8,128)}) %reduce-scatter.2.cloned.1.call-update) | async-done | bytes 98320 | tf_op jit(solution)/shard_map/reduce_scatter | solution.py:39
  (2 shorter events, 0.0 us)
Async XLA Ops:
  6.5 1.6 copy-start
  6.5 268.8 %reduce-scatter.2.cloned.1.call-start = ((), (), s32[]{:S(2)}) async-start(), calls=%async_computation.3 | async-start | bytes 1671168 | tf_op jit(solution)/shard_map/reduce_scatter | solution.py:39
  146.1 4.6 %copy-start.1 = (bf16[384,128,128]{2,1,0:T(8,128)(2,1)}, bf16[384,128,128]{2,1,0:T(8,128)(2,1)S(1)}, u32[]{:S(2)}) copy-start(bf16[384,128,128]{2,1,0:T(8,128)(2,1)S(1)} %convert_element_type.20) | copy-start | bytes 37748740
  146.1 41.2 %copy-start.2 = (f32[256,256]{1,0:T(8,128)S(1)}, f32[256,256]{1,0:T(8,128)}, u32[]{:S(2)}) copy-start(f32[256,256]{1,0:T(8,128)} %param.9) | copy-start | bytes 786436
Sparse Core Ops, SparseCore 0:
  216.4 58.9 reduce-scatter.1
where the time goes:
time: 284 us; the launch traced here: 282 us
  other arithmetic  76.4 us (27%)
  waiting for transfers between devices  59.1 us (21%)
  blocking collectives  51.4 us (18%)
  local copies, waits for them, and re-layouts  49.1 us (17%)
  matrix products  31.9 us (11%)
  between operations  14.2 us (5%)
    scatter-add x1, other arithmetic, half_transform(): jnp.zeros((Q_DEV * nblk, block_size, occupied), jnp.float32).at[slot_ids]  66.1 us
    reduce_scatter x1, waiting for transfers between devices, body(): return lax.psum_scatter(partial_sum, 'aux', scatter_dimension=0, tiled=True)  59.1 us
    all_to_all x1, blocking collectives, body(): lax.all_to_all(pairs, 'aux', split_axis=1, concat_axis=0, tiled=True)  32.2 us
    mul x1, local copies, waits for them, and re-layouts, half_transform(): products = products * live_mask[:, None, None]  21.1 us
    all_to_all x1, blocking collectives, body(): lax.all_to_all(fitted_here, 'aux', split_axis=0, concat_axis=1, tiled=True)  19.3 us
    dot_general x1, matrix products, half_transform(): jnp.einsum('bmn,bni->bmi', blocks, orb_rows, preferred_element_type=jnp.f...  19 us
    broadcast_in_dim x1, local copies, waits for them, and re-layouts, half_transform(): jnp.zeros((Q_DEV * nblk, block_size, occupied), jnp.float32).at[slot_ids]  11.5 us
    gather x1, local copies, waits for them, and re-layouts, half_transform(): orb_rows = orb_blocks[n_block]  10.7 us
  transfers between devices with their start and end apart: 1, of which 1 were waited for; matrix products, arithmetic and copies ran while one was open for 0% of the time, Pallas kernels for 0%

commit v1 on v0

v1 whole, which is shorter than its diff:
```python
import functools

import jax
import jax.numpy as jnp
from jax import lax
from jax.experimental import pallas as pl
from jax.experimental.pallas import tpu as pltpu
from jax.sharding import PartitionSpec as P

UNROLL = 8
CHUNK = 32
F32 = jnp.float32
BF16 = jnp.bfloat16


def half_kernel(
    owners, q_dev, live_ref, code_ref, blocks_hbm, orb_ref, slab_hbm, pairs_ref,
    held, acc, slab, orb_t, in_sem, out_sem,
):
    slots, size, occupied = held.shape
    nblk = orb_ref.shape[0] // size
    chunks = slots // CHUNK
    live = live_ref[0]

    def fetch(c):
        part = pl.ds(c * CHUNK, CHUNK)
        return pltpu.make_async_copy(blocks_hbm.at[part], held.at[part], in_sem.at[c])

    for c in range(chunks):
        @pl.when(c * CHUNK < live)
        def _():
            fetch(c).start()

    @pl.loop(0, q_dev * nblk, step=2)
    def _(k):
        for u in range(2):
            acc[k + u] = jnp.zeros((size, occupied), F32)

    for b in range(nblk):
        rows = slice(b * size, (b + 1) * size)
        orb_t[:, rows] = orb_ref[rows, :].T

    @pl.loop(0, (live + CHUNK - 1) // CHUNK)
    def _(c):
        fetch(c).wait()

        @pl.loop(0, CHUNK // UNROLL)
        def _(g):
            for u in range(UNROLL):
                s = c * CHUNK + g * UNROLL + u
                code = code_ref[s]
                key = code // 256
                nb = pl.multiple_of((code % 256) * size, size)
                acc[key] += jnp.dot(held[s], orb_ref[pl.ds(nb, size), :], preferred_element_type=F32)

    def flush(t):
        return pltpu.make_async_copy(slab.at[t], slab_hbm.at[t], out_sem.at[t])

    @pl.loop(0, q_dev // 2)
    def _(t):
        total = jnp.zeros((occupied, 2 * occupied), F32)
        for b in range(0, nblk, 2):
            left = jnp.concatenate([acc[2 * t * nblk + b], acc[2 * t * nblk + b + 1]], axis=0)
            right = jnp.concatenate([acc[(2 * t + 1) * nblk + b], acc[(2 * t + 1) * nblk + b + 1]], axis=0)
            block = jnp.concatenate([left.astype(BF16), right.astype(BF16)], axis=1)
            rows = slice(b * size, (b + 2) * size)
            slab[t, rows, :] = block
            total += jnp.dot(orb_t[:, rows], block, preferred_element_type=F32)
        flush(t).start()
        for u in range(2):
            pair = total[:, u * occupied : (u + 1) * occupied]
            if owners:
                pairs_ref[:, 2 * t + u] = pair.reshape(owners, occupied // owners, occupied).astype(BF16)
            else:
                pairs_ref[2 * t + u] = pair.astype(BF16)

    @pl.loop(0, q_dev // 2)
    def _(t):
        flush(t).wait()


def half_transform(blocks, code, live, orbitals, q_dev, owners):
    slots, size, _ = blocks.shape
    basis, occupied = orbitals.shape
    nblk = basis // size
    split = (occupied // owners) % 8 == 0
    pairs_shape = (owners, q_dev, occupied // owners, occupied) if split else (q_dev, occupied, occupied)
    half = q_dev // 2
    slab, pairs = pl.pallas_call(
        functools.partial(half_kernel, owners if split else 0, q_dev),
        out_shape=(
            jax.ShapeDtypeStruct((half, basis, 2 * occupied), BF16),
            jax.ShapeDtypeStruct(pairs_shape, BF16),
        ),
        in_specs=[
            pl.BlockSpec(memory_space=pltpu.SMEM),
            pl.BlockSpec(memory_space=pltpu.SMEM),
            pl.BlockSpec(memory_space=pl.ANY),
            pl.BlockSpec(memory_space=pltpu.VMEM),
        ],
        out_specs=(pl.BlockSpec(memory_space=pl.ANY), pl.BlockSpec(memory_space=pltpu.VMEM)),
        scratch_shapes=[
            pltpu.VMEM((slots, size, size), BF16),
            pltpu.VMEM((q_dev * nblk + 1, size, occupied), F32),
            pltpu.VMEM((half, basis, 2 * occupied), BF16),
            pltpu.VMEM((occupied, basis), BF16),
            pltpu.SemaphoreType.DMA((slots // CHUNK,)),
            pltpu.SemaphoreType.DMA((half,)),
        ],
        compiler_params=pltpu.CompilerParams(vmem_limit_bytes=60 * 2**20),
        cost_estimate=pl.CostEstimate(
            flops=2 * slots * size * size * occupied + 2 * q_dev * basis * occupied * occupied,
            bytes_accessed=2 * slots * size * size + 2 * q_dev * basis * occupied,
            transcendentals=0,
        ),
        name="half_transform_pairs",
    )(live, code, blocks, orbitals)
    if not split:
        pairs = pairs.reshape(q_dev, owners, occupied // owners, occupied).transpose(1, 0, 2, 3)
    return slab, pairs


def exchange_kernel(mine, me_ref, slab_hbm, fitted_ref, out_ref, slab, fitted, sem):
    half, rows, _ = slab.shape
    parts, each, occupied = out_ref.shape
    me = me_ref[0]

    def fetch(h):
        owner = (2 * h + mine) ^ me
        there = pl.ds(pl.multiple_of(owner * each, each), each)
        here = pl.ds(h * each, each)
        return pltpu.make_async_copy(slab_hbm.at[:, there, :], slab.at[:, here, :], sem.at[h])

    for h in range(parts):
        fetch(h).start()

    for q in range(2 * half):
        if len(fitted_ref.shape) == 4:
            block = fitted_ref[:, q].astype(F32).reshape(occupied, occupied)
        else:
            block = fitted_ref[q].astype(F32)
        fitted[q * occupied : (q + 1) * occupied, :] = block.T.astype(BF16)

    for h in range(parts):
        fetch(h).wait()
        here = slice(h * each, (h + 1) * each)
        rows_all = jnp.concatenate([slab[t, here, :] for t in range(half)], axis=1)
        out_ref[h] = jnp.dot(rows_all, fitted[...], preferred_element_type=F32).astype(out_ref.dtype)


def exchange_rows(slab, fitted, me, owners, mine, dtype):
    half, basis, width = slab.shape
    occupied = width // 2
    each = basis // owners
    return pl.pallas_call(
        functools.partial(exchange_kernel, mine),
        out_shape=jax.ShapeDtypeStruct((owners // 2, each, occupied), dtype),
        in_specs=[
            pl.BlockSpec(memory_space=pltpu.SMEM),
            pl.BlockSpec(memory_space=pl.ANY),
            pl.BlockSpec(memory_space=pltpu.VMEM),
        ],
        out_specs=pl.BlockSpec(memory_space=pltpu.VMEM),
        scratch_shapes=[
            pltpu.VMEM((half, basis // 2, width), BF16),
            pltpu.VMEM((half * width, occupied), BF16),
            pltpu.SemaphoreType.DMA((owners // 2,)),
        ],
        compiler_params=pltpu.CompilerParams(vmem_limit_bytes=32 * 2**20),
        cost_estimate=pl.CostEstimate(
            flops=half * width * basis * occupied, bytes_accessed=half * width * basis, transcendentals=0
        ),
        name="exchange_rows",
    )(me, slab, fitted)


def body(owners, integrals, block_index, live_count, orbitals, metric):
    slots, size, _ = integrals.shape
    basis, occupied = orbitals.shape
    nblk = basis // size
    naux = metric.shape[1]
    q_dev = naux // owners
    each = basis // owners
    me = lax.axis_index("aux").astype(jnp.int32)

    key = block_index[:, 0] * nblk + block_index[:, 1]
    alive = jnp.arange(slots, dtype=jnp.int32) < live_count[0]
    code = jnp.where(alive, key, q_dev * nblk) * 256 + block_index[:, 2]

    slab, pairs = half_transform(integrals, code, live_count, orbitals, q_dev, owners)

    held = lax.all_to_all(pairs, "aux", split_axis=0, concat_axis=0, tiled=True)
    held = held.reshape(naux, occupied // owners, occupied).astype(F32)
    fitted = jnp.einsum("qp,pji->qji", metric, held, precision=lax.Precision.HIGHEST).astype(BF16)
    fitted = fitted.reshape(owners, q_dev, occupied // owners, occupied)
    fitted = lax.all_to_all(fitted, "aux", split_axis=0, concat_axis=0, tiled=True)
    if (occupied // owners) % 8:
        fitted = fitted.transpose(1, 0, 2, 3).reshape(q_dev, occupied, occupied)

    def swap(x, bit):
        return lax.ppermute(x, "aux", [(d, d ^ bit) for d in range(owners)])

    mine = me.reshape(1)
    away = exchange_rows(slab, fitted, mine, owners, 1, BF16)
    arrived = swap(away, 1)
    near = exchange_rows(slab, fitted, mine, owners, 0, F32)
    arrived = arrived.reshape(owners // 4, 2, each, occupied)
    near = near.reshape(owners // 4, 2, each, occupied)
    away = (near[:, 1] + arrived[:, 1].astype(F32)).astype(BF16)
    arrived_y = swap(away, 2)
    near = near[:, 0] + arrived[:, 0].astype(F32) + arrived_y.astype(F32)
    total = near[0]
    for k in range(1, owners // 4):
        total = total + swap(near[k].astype(BF16), 4 * k).astype(F32)
    return total


def solution(mesh):
    placed = (
        P(("groups", "aux"), None, None),
        P(("groups", "aux"), None),
        P(("groups", "aux")),
        P("groups", None),
        P("groups", None),
    )
    return jax.shard_map(
        functools.partial(body, mesh.shape["aux"]),
        mesh=mesh, in_specs=placed, out_specs=P(("groups", "aux"), None), check_vma=False,
    )
```

time: 284 us -> 90.7 us (0.32)
  other arithmetic: 76.4 us -> 2.19 us
  local copies, waits for them, and re-layouts: 49.1 us -> 5.7 us
  waiting for transfers between devices: 59.1 us -> 25.6 us
  matrix products: 31.9 us -> 0.69 us
  blocking collectives: 51.4 us -> 27.9 us
  Pallas kernels: 0 us -> 18.2 us
  between operations: 14.2 us -> 0.77 us
  starting transfers between devices: 0.01 us -> 9.2 us
    scatter-add x1 -> x0, other arithmetic: 66.1 us -> none  [half_transform(): jnp.zeros((Q_DEV * nblk, block_size, occupied), jnp.float32).at[slot_ids]]
    reduce_scatter x1 -> x0, waiting for transfers between devices: 59.1 us -> none  [body(): return lax.psum_scatter(partial_sum, 'aux', scatter_dimension=0, tiled=True)]
    dot_general x4 -> x1, matrix products: 31.9 us -> 0.69 us  [body(): jnp.einsum('qp,pji->qji', metric, held, precision=lax.Precision.HIGHEST)]
    all_to_all x2 -> x1, blocking collectives: 51.4 us -> 27.9 us  [body(): held = lax.all_to_all(pairs, 'aux', split_axis=0, concat_axis=0, tiled=True)]
    mul x1 -> x0, local copies, waits for them, and re-layouts: 21.1 us -> none  [half_transform(): products = products * live_mask[:, None, None]]
    pallas_call x0 -> x3, Pallas kernels: none -> 18.2 us  [the longest x1 11 us: half_transform(): pl.pallas_call(functools.partial(half_kernel, owners if split else 0, q_d...]
    all_to_all x0 -> x1, waiting for transfers between devices: none -> 14.5 us  [body(): lax.all_to_all(fitted, 'aux', split_axis=0, concat_axis=0, tiled=True)]
    broadcast_in_dim x1 -> x0, local copies, waits for them, and re-layouts: 11.5 us -> none  [half_transform(): jnp.zeros((Q_DEV * nblk, block_size, occupied), jnp.float32).at[slot_ids]]
  transfers between devices with their start and end apart: 1 -> 6, of which waited for: 1 -> 5; matrix products, arithmetic and copies ran while one was open for 0% -> 0% of each run, Pallas kernels for 0% -> 4%
where the time goes in v1:
time: 90.7 us; the launch traced here: 90.2 us
  blocking collectives  27.9 us (31%)
  waiting for transfers between devices  25.6 us (28%)
  Pallas kernels  18.2 us (20%)
  starting transfers between devices  9.2 us (10%)
  local copies, waits for them, and re-layouts  5.7 us (6%)
  other arithmetic  2.19 us (2%)
    all_to_all x1, blocking collectives, body(): held = lax.all_to_all(pairs, 'aux', split_axis=0, concat_axis=0, tiled=True)  27.9 us
    all_to_all x1, waiting for transfers between devices, body(): lax.all_to_all(fitted, 'aux', split_axis=0, concat_axis=0, tiled=True)  14.5 us
    ppermute x5, waiting for transfers between devices, swap(): return lax.ppermute(x, 'aux', [(d, d ^ bit) for d in range(owners)])  11.1 us
    pallas_call x1, Pallas kernels, half_transform(): pl.pallas_call(functools.partial(half_kernel, owners if split else 0, q_d...  11 us
    pallas_call x2, Pallas kernels, exchange_rows(): pl.pallas_call(functools.partial(exchange_kernel, mine), out_shape=jax.Sh...  7.2 us
    ppermute x5, starting transfers between devices, swap(): return lax.ppermute(x, 'aux', [(d, d ^ bit) for d in range(owners)])  5.1 us
    unnamed x4, local copies, waits for them, and re-layouts  4.58 us
    all_to_all x1, starting transfers between devices, body(): lax.all_to_all(fitted, 'aux', split_axis=0, concat_axis=0, tiled=True)  4.1 us
  transfers between devices with their start and end apart: 6, of which 5 were waited for; matrix products, arithmetic and copies ran while one was open for 0% of the time, Pallas kernels for 4%

profile of v1, /device:TPU:0, one launch (start us, length us, event | category | flops | bytes accessed | tf_op | source)
XLA Modules:
  0.0 90.2 jit_solution(10679824305660021490)
XLA Ops:
  0.0 0.0 copy-start
  0.7 0.8 add_reduce_fusion
  1.5 0.6 multiply_add_fusion.code_ref
  2.1 11.0 %half_transform_pairs.1 = (bf16[8,3072,256]{2,1,0:T(8,128)(2,1)}, bf16[16,16,8,128]{3,2,1,0:T(8,128)(2,1)}) custom-call(s32[1]{0:T(128)} %copy.18.live_ref, s32[320]{0:T(512)} %multiply_add_fusion.code_ref, bf16[320,128,128]{2,1,0:T(8,128)(2,1)} %blocks_hbm.1, bf16[3072,128]{1,0:T(8,128)(2,1)} %orb_ref.1), custom_call_target="tpu_custom_call" | custom-call | flops 2952790016 | bytes 23068672 | tf_op jit(solution)/shard_map/half_transform_pairs/pallas_call | solution.py:89
  13.1 27.9 %all_to_all.10 = bf16[16,16,8,128]{3,2,1,0:T(8,128)(2,1)S(1)} all-to-all(bf16[16,16,8,128]{3,2,1,0:T(8,128)(2,1)} %get-tuple-element.8), channel_id=1, replica_groups=mesh['groups'=2,'aux'=16] {'aux'}, dimensions={0} | all-to-all | bytes 1048576 | tf_op jit(solution)/shard_map/all_to_all | solution.py:192
  41.0 0.0 copy-done
  41.0 0.7 fusion
  41.7 1.1 %copy.7 = bf16[256,8,128]{2,1,0:T(8,128)(2,1)} copy(bf16[256,8,128]{0,2,1:T(8,128)(2,1)S(1)} %fusion) | data formatting | bytes 1048576 | tf_op jit(solution)/shard_map/convert_element_type | solution.py:194
  42.8 4.1 %all-to-all-start.1 = ((bf16[16,16,8,128]{3,2,1,0:T(8,128)(2,1)}), bf16[16,16,8,128]{3,2,1,0:T(8,128)(2,1)S(1)}, u32[]{:S(2)}, u32[]{:S(2)}) async-start(bf16[16,16,8,128]{3,2,1,0:T(8,128)(2,1)} %bitcast.5), calls=%async_computation.1 | async-start | bytes 1048576 | tf_op jit(solution)/shard_map/all_to_all | solution.py:196
  46.9 14.5 %all-to-all-done.1.fitted_ref = bf16[16,16,8,128]{3,2,1,0:T(8,128)(2,1)S(1)} async-done(((bf16[16,16,8,128]{3,2,1,0:T(8,128)(2,1)}), bf16[16,16,8,128]{3,2,1,0:T(8,128)(2,1)S(1)}, u32[]{:S(2)}, u32[]{:S(2)}) %all-to-all-start.1) | async-done | bytes 524320 | tf_op jit(solution)/shard_map/all_to_all | solution.py:196
  61.4 0.0 copy-start.1
  61.4 4.6 %copy-done.1 = bf16[8,3072,256]{2,1,0:T(8,128)(2,1)S(1)} copy-done((bf16[8,3072,256]{2,1,0:T(8,128)(2,1)S(1)}, bf16[8,3072,256]{2,1,0:T(8,128)(2,1)}, u32[]{:S(2)}) %copy-start.1) | copy-done | bytes 12582936
  66.0 3.6 %exchange_rows.3 = bf16[8,192,128]{2,1,0:T(8,128)(2,1)S(1)} custom-call(s32[1]{0:T(128)} %bitcast.me_ref, bf16[8,3072,256]{2,1,0:T(8,128)(2,1)S(1)} %copy-done.1, bf16[16,16,8,128]{3,2,1,0:T(8,128)(2,1)S(1)} %all-to-all-done.1.fitted_ref), custom_call_target="tpu_custom_call" | custom-call | flops 805306368 | bytes 6291456 | tf_op jit(solution)/shard_map/exchange_rows/pallas_call | solution.py:155
  69.6 0.1 collective-permute-start
  69.7 3.6 %exchange_rows.2 = f32[8,192,128]{2,1,0:T(8,128)S(1)} custom-call(s32[1]{0:T(128)} %bitcast.me_ref, bf16[8,3072,256]{2,1,0:T(8,128)(2,1)S(1)} %copy-done.1, bf16[16,16,8,128]{3,2,1,0:T(8,128)(2,1)S(1)} %all-to-all-done.1.fitted_ref), custom_call_target="tpu_custom_call" | custom-call | flops 805306368 | bytes 6291456 | tf_op jit(solution)/shard_map/exchange_rows/pallas_call | solution.py:155
  73.3 0.0 collective-permute-done
  73.3 1.2 %collective-permute-start.1 = (bf16[4,192,128]{2,1,0:T(8,128)(2,1)S(1)}, bf16[4,192,128]{2,1,0:T(8,128)(2,1)S(1)}, u32[]{:S(2)}, u32[]{:S(2)}) collective-permute-start(bf16[4,192,128]{2,1,0:T(8,128)(2,1)S(1)} %fusion.8), channel_id=1, source_target_pairs={{0,2},{1,3},{2,0},{3,1},{4,6},{5,7},{6,4},{7,5},{8,10},{9,11},{10,... | collective-permute-start | bytes 589832 | tf_op jit(solution)/shard_map/ppermute | solution.py:201
  74.5 6.1 %collective-permute-done.1 = bf16[4,192,128]{2,1,0:T(8,128)(2,1)S(1)} collective-permute-done((bf16[4,192,128]{2,1,0:T(8,128)(2,1)S(1)}, bf16[4,192,128]{2,1,0:T(8,128)(2,1)S(1)}, u32[]{:S(2)}, u32[]{:S(2)}) %collective-permute-start.1) | collective-permute-done | bytes 196640 | tf_op jit(solution)/shard_map/ppermute | solution.py:201
  80.7 0.1 fusion.12
  80.8 1.3 %collective-permute-start.2 = (bf16[192,128]{1,0:T(8,128)(2,1)S(1)}, bf16[192,128]{1,0:T(8,128)(2,1)S(1)}, u32[]{:S(2)}, u32[]{:S(2)}) collective-permute-start(bf16[192,128]{1,0:T(8,128)(2,1)S(1)} %get-tuple-element.13), channel_id=1, source_target_pairs={{0,4},{1,5},{2,6},{3,7},{4,0},{5,1},{6,2},{7,3},{8,12},{9,13},{10,... | collective-permute-start | bytes 147464 | tf_op jit(solution)/shard_map/ppermute | solution.py:201
  82.1 2.5 %collective-permute-start.4 = (bf16[192,128]{1,0:T(8,128)(2,1)S(1)}, bf16[192,128]{1,0:T(8,128)(2,1)S(1)}, u32[]{:S(2)}, u32[]{:S(2)}) collective-permute-start(bf16[192,128]{1,0:T(8,128)(2,1)S(1)} %get-tuple-element.14), channel_id=1, source_target_pairs={{0,12},{1,13},{2,14},{3,15},{4,8},{5,9},{6,10},{7,11},{8,4},{9,5},... | collective-permute-start | bytes 147464 | tf_op jit(solution)/shard_map/ppermute | solution.py:201
  84.6 0.0 collective-permute-start.3
  84.6 0.3 collective-permute-done.2
  84.9 3.1 %collective-permute-done.4 = bf16[192,128]{1,0:T(8,128)(2,1)S(1)} collective-permute-done((bf16[192,128]{1,0:T(8,128)(2,1)S(1)}, bf16[192,128]{1,0:T(8,128)(2,1)S(1)}, u32[]{:S(2)}, u32[]{:S(2)}) %collective-permute-start.4) | collective-permute-done | bytes 49184 | tf_op jit(solution)/shard_map/ppermute | solution.py:201
  88.0 1.6 %collective-permute-done.3 = bf16[192,128]{1,0:T(8,128)(2,1)S(1)} collective-permute-done((bf16[192,128]{1,0:T(8,128)(2,1)S(1)}, bf16[192,128]{1,0:T(8,128)(2,1)S(1)}, u32[]{:S(2)}, u32[]{:S(2)}) %collective-permute-start.3) | collective-permute-done | bytes 49184 | tf_op jit(solution)/shard_map/ppermute | solution.py:201
  89.6 0.7 fusion.11
  (2 shorter events, 0.1 us)
Async XLA Ops:
  0.0 41.0 %copy-start = (f32[256,256]{1,0:T(8,128)S(1)}, f32[256,256]{1,0:T(8,128)}, u32[]{:S(2)}) copy-start(f32[256,256]{1,0:T(8,128)} %param.9) | copy-start | bytes 786436
  42.8 18.6 %all-to-all-start.1 = ((bf16[16,16,8,128]{3,2,1,0:T(8,128)(2,1)}), bf16[16,16,8,128]{3,2,1,0:T(8,128)(2,1)S(1)}, u32[]{:S(2)}, u32[]{:S(2)}) async-start(bf16[16,16,8,128]{3,2,1,0:T(8,128)(2,1)} %bitcast.5), calls=%async_computation.1 | async-start | bytes 1048576 | tf_op jit(solution)/shard_map/all_to_all | solution.py:196
  61.4 4.6 %copy-start.1 = (bf16[8,3072,256]{2,1,0:T(8,128)(2,1)S(1)}, bf16[8,3072,256]{2,1,0:T(8,128)(2,1)}, u32[]{:S(2)}) copy-start(bf16[8,3072,256]{2,1,0:T(8,128)(2,1)} %get-tuple-element.7.slab_hbm) | copy-start | bytes 37748740
  69.6 3.7 %collective-permute-start = (bf16[8,192,128]{2,1,0:T(8,128)(2,1)S(1)}, bf16[8,192,128]{2,1,0:T(8,128)(2,1)S(1)}, u32[]{:S(2)}, u32[]{:S(2)}) collective-permute-start(bf16[8,192,128]{2,1,0:T(8,128)(2,1)S(1)} %exchange_rows.3), channel_id=1, source_target_pairs={{0,1},{1,0},{2,3},{3,2},{4,5},{5,4},{6,7},{7,6},{8,9},{9,8},{10,11... | collective-permute-start | bytes 1179656 | tf_op jit(solution)/shard_map/ppermute | solution.py:201
  73.3 7.3 %collective-permute-start.1 = (bf16[4,192,128]{2,1,0:T(8,128)(2,1)S(1)}, bf16[4,192,128]{2,1,0:T(8,128)(2,1)S(1)}, u32[]{:S(2)}, u32[]{:S(2)}) collective-permute-start(bf16[4,192,128]{2,1,0:T(8,128)(2,1)S(1)} %fusion.8), channel_id=1, source_target_pairs={{0,2},{1,3},{2,0},{3,1},{4,6},{5,7},{6,4},{7,5},{8,10},{9,11},{10,... | collective-permute-start | bytes 589832 | tf_op jit(solution)/shard_map/ppermute | solution.py:201
  80.8 4.2 %collective-permute-start.2 = (bf16[192,128]{1,0:T(8,128)(2,1)S(1)}, bf16[192,128]{1,0:T(8,128)(2,1)S(1)}, u32[]{:S(2)}, u32[]{:S(2)}) collective-permute-start(bf16[192,128]{1,0:T(8,128)(2,1)S(1)} %get-tuple-element.13), channel_id=1, source_target_pairs={{0,4},{1,5},{2,6},{3,7},{4,0},{5,1},{6,2},{7,3},{8,12},{9,13},{10,... | collective-permute-start | bytes 147464 | tf_op jit(solution)/shard_map/ppermute | solution.py:201
  82.1 5.9 %collective-permute-start.4 = (bf16[192,128]{1,0:T(8,128)(2,1)S(1)}, bf16[192,128]{1,0:T(8,128)(2,1)S(1)}, u32[]{:S(2)}, u32[]{:S(2)}) collective-permute-start(bf16[192,128]{1,0:T(8,128)(2,1)S(1)} %get-tuple-element.14), channel_id=1, source_target_pairs={{0,12},{1,13},{2,14},{3,15},{4,8},{5,9},{6,10},{7,11},{8,4},{9,5},... | collective-permute-start | bytes 147464 | tf_op jit(solution)/shard_map/ppermute | solution.py:201
  84.6 5.0 %collective-permute-start.3 = (bf16[192,128]{1,0:T(8,128)(2,1)S(1)}, bf16[192,128]{1,0:T(8,128)(2,1)S(1)}, u32[]{:S(2)}, u32[]{:S(2)}) collective-permute-start(bf16[192,128]{1,0:T(8,128)(2,1)S(1)} %get-tuple-element.15), channel_id=1, source_target_pairs={{0,8},{1,9},{2,10},{3,11},{4,12},{5,13},{6,14},{7,15},{8,0},{9,1},... | collective-permute-start | bytes 147464 | tf_op jit(solution)/shard_map/ppermute | solution.py:201

commit v2 on v1

v2 whole, which is shorter than its diff:
```python
import functools

import jax
import jax.numpy as jnp
from jax import lax
from jax.experimental import pallas as pl
from jax.experimental.pallas import tpu as pltpu
from jax.sharding import PartitionSpec as P

UNROLL = 8
CHUNK = 32
F32 = jnp.float32
BF16 = jnp.bfloat16


def rank_slots(live, index_ref, keys, meta, nblk, nkeys):
    slots = index_ref.shape[1]
    wide = keys.shape[1]
    keys[...] = jnp.full(keys.shape, nkeys, F32)
    key = index_ref[0:1, :] * nblk + index_ref[1:2, :]
    alive = lax.broadcasted_iota(jnp.int32, (1, slots), 1) < live
    keys[0:1, 0:slots] = jnp.where(alive, key, nkeys).astype(F32)
    row = jnp.broadcast_to(keys[0:1, :], (wide, wide))
    column = row.T
    before = lax.broadcasted_iota(jnp.int32, (wide, wide), 0) < lax.broadcasted_iota(jnp.int32, (wide, wide), 1)
    rank = jnp.sum(jnp.where((column == row) & before, 1.0, 0.0), axis=0, keepdims=True)
    pair = jnp.floor(rank * 0.5)
    odd = rank - 2.0 * pair
    opens = jnp.broadcast_to(1.0 - odd, (wide, wide)).T
    group = jnp.sum(jnp.where(column < row, opens, 0.0), axis=0, keepdims=True) + pair
    lives = keys[0:1, :] < nkeys
    place = jnp.where(lives, 2.0 * group + odd, 2.0 * slots + 2 * UNROLL)
    count = jnp.sum(jnp.where(lives, 1.0 - odd, 0.0), axis=1, keepdims=True)
    last = jnp.max(jnp.where(lives, keys[0:1, :], 0.0), axis=1, keepdims=True)
    meta[0:1, :] = place.astype(jnp.int32)
    meta[1:2, 0:slots] = lax.broadcasted_iota(jnp.int32, (1, slots), 1) * 256 + index_ref[2:3, :]
    meta[2:3, :] = (2.0 * keys[0:1, :] + jnp.where(rank < 2.0, 1.0, 0.0)).astype(jnp.int32)
    meta[3:4, :] = jnp.broadcast_to(count, (1, wide)).astype(jnp.int32)
    meta[4:5, :] = jnp.broadcast_to(last, (1, wide)).astype(jnp.int32)


def half_kernel(
    owners, q_dev, live_ref, index_hbm, blocks_hbm, orb_hbm, slab, pairs_ref,
    index_ref, held, orb_ref, orb_t, keys, meta, facts, group_slot, group_key, in_sem, meta_sem,
):
    slots, size, _ = blocks_hbm.shape
    occupied = orb_ref.shape[1]
    nblk = orb_ref.shape[0] // size
    nkeys = q_dev * nblk
    chunks = slots // CHUNK

    def fetch(c):
        part = pl.ds(c * CHUNK, CHUNK)
        return pltpu.make_async_copy(blocks_hbm.at[part], held.at[part], in_sem.at[c])

    small = [
        pltpu.make_async_copy(source, target, meta_sem.at[1 + k])
        for k, (source, target) in enumerate([(index_hbm, index_ref), (orb_hbm, orb_ref)])
    ]
    for copy in small:
        copy.start()
    for c in range(chunks):
        fetch(c).start()

    small[0].wait()
    rank_slots(live_ref[0], index_ref, keys, meta, nblk, nkeys)
    copy = pltpu.make_async_copy(meta, facts, meta_sem.at[0])
    copy.start()

    nothing = slots * 256
    held[slots] = jnp.zeros((size, size), BF16)

    @pl.loop(0, nkeys, step=4)
    def _(k):
        for u in range(4):
            slab[k + u] = jnp.zeros((size, occupied), BF16)

    @pl.loop(0, 2 * slots, step=16)
    def _(k):
        for u in range(16):
            group_slot[k + u] = nothing

    for u in range(2 * UNROLL):
        group_slot[2 * slots + u] = nothing

    small[1].wait()
    for b in range(nblk):
        rows = slice(b * size, (b + 1) * size)
        orb_t[:, rows] = orb_ref[rows, :].T

    copy.wait()
    groups = facts[3, 0]

    @pl.loop(0, slots, step=8)
    def _(k):
        for u in range(8):
            place = facts[0, k + u]
            group_slot[place] = facts[1, k + u]
            group_key[place // 2] = facts[2, k + u]

    for u in range(UNROLL):
        group_key[groups + u] = 2 * facts[4, 0]

    for c in range(chunks):
        fetch(c).wait()

    def step(g, total):
        for u in range(UNROLL):
            first, second = group_slot[2 * (g * UNROLL + u)], group_slot[2 * (g * UNROLL + u) + 1]
            code = group_key[g * UNROLL + u]
            blocks = jnp.concatenate([held[first // 256], held[second // 256]], axis=1)
            orbs = jnp.concatenate(
                [orb_ref[pl.ds(pl.multiple_of((s % 256) * size, size), size), :] for s in (first, second)], axis=0
            )
            product = jnp.dot(blocks, orbs, preferred_element_type=F32)
            total = jnp.where(code % 2 == 1, product, total + product)
            slab[code // 2] = total.astype(BF16)
        return total

    lax.fori_loop(0, (groups + UNROLL - 1) // UNROLL, step, jnp.zeros((size, occupied), F32))

    @pl.loop(0, q_dev // 2)
    def _(t):
        total = jnp.zeros((occupied, 2 * occupied), F32)
        for b in range(0, nblk, 2):
            block = jnp.concatenate(
                [
                    jnp.concatenate([slab[(2 * t + u) * nblk + b], slab[(2 * t + u) * nblk + b + 1]], axis=0)
                    for u in range(2)
                ],
                axis=1,
            )
            total += jnp.dot(orb_t[:, b * size : (b + 2) * size], block, preferred_element_type=F32)
        for u in range(2):
            pair = total[:, u * occupied : (u + 1) * occupied].T
            if owners:
                pairs_ref[:, 2 * t + u] = pair.reshape(owners, occupied // owners, occupied).astype(BF16)
            else:
                pairs_ref[2 * t + u] = pair.astype(BF16)


def half_transform(blocks, index, live, orbitals, q_dev, owners):
    slots, size, _ = blocks.shape
    basis, occupied = orbitals.shape
    nblk = basis // size
    split = (occupied // owners) % 8 == 0
    pairs_shape = (owners, q_dev, occupied // owners, occupied) if split else (q_dev, occupied, occupied)
    wide = -(-slots // 128) * 128
    slab, pairs = pl.pallas_call(
        functools.partial(half_kernel, owners if split else 0, q_dev),
        out_shape=(
            pltpu.VMEM((q_dev * nblk, size, occupied), BF16),
            jax.ShapeDtypeStruct(pairs_shape, BF16),
        ),
        in_specs=[pl.BlockSpec(memory_space=pltpu.SMEM)] + [pl.BlockSpec(memory_space=pl.ANY)] * 3,
        out_specs=(pl.BlockSpec(memory_space=pltpu.VMEM), pl.BlockSpec(memory_space=pltpu.VMEM)),
        scratch_shapes=[
            pltpu.VMEM(index.shape, jnp.int32),
            pltpu.VMEM((slots + 1, size, size), BF16),
            pltpu.VMEM((basis, occupied), BF16),
            pltpu.VMEM((occupied, basis), BF16),
            pltpu.VMEM((8, wide), F32),
            pltpu.VMEM((8, wide), jnp.int32),
            pltpu.SMEM((8, wide), jnp.int32),
            pltpu.SMEM((2 * slots + 2 * UNROLL + 2,), jnp.int32),
            pltpu.SMEM((slots + UNROLL + 1,), jnp.int32),
            pltpu.SemaphoreType.DMA((slots // CHUNK,)),
            pltpu.SemaphoreType.DMA((3,)),
        ],
        compiler_params=pltpu.CompilerParams(vmem_limit_bytes=36 * 2**20),
        cost_estimate=pl.CostEstimate(
            flops=2 * slots * size * size * occupied + 2 * q_dev * basis * occupied * occupied,
            bytes_accessed=2 * slots * size * size + 2 * q_dev * basis * occupied,
            transcendentals=0,
        ),
        name="half_transform_pairs",
    )(live, *(pltpu.with_memory_space_constraint(x, pltpu.HBM) for x in (index, blocks, orbitals)))
    if not split:
        pairs = pairs.reshape(q_dev, owners, occupied // owners, occupied).transpose(1, 0, 2, 3)
    return slab.reshape(q_dev, basis, occupied), pairs


def exchange_kernel(mine, me_ref, slab, fitted_ref, out_ref, fitted):
    q_dev = slab.shape[0]
    parts, each, occupied = out_ref.shape
    me = me_ref[0]

    for q in range(q_dev):
        if len(fitted_ref.shape) == 4:
            block = fitted_ref[:, q].astype(F32).reshape(occupied, occupied).astype(BF16)
        else:
            block = fitted_ref[q]
        fitted[q * occupied : (q + 1) * occupied, :] = block

    @pl.loop(0, parts)
    def _(h):
        owner = (2 * h + mine) ^ me
        rows = pl.ds(pl.multiple_of(owner * each, each), each)
        every = jnp.concatenate([slab[q, rows, :] for q in range(q_dev)], axis=1)
        out_ref[h] = jnp.dot(every, fitted[...], preferred_element_type=F32).astype(out_ref.dtype)


def exchange_rows(slab, fitted, me, owners, mine, dtype):
    q_dev, basis, occupied = slab.shape
    each = basis // owners
    return pl.pallas_call(
        functools.partial(exchange_kernel, mine),
        out_shape=jax.ShapeDtypeStruct((owners // 2, each, occupied), dtype),
        in_specs=[
            pl.BlockSpec(memory_space=pltpu.SMEM),
            pl.BlockSpec(memory_space=pltpu.VMEM),
            pl.BlockSpec(memory_space=pltpu.VMEM),
        ],
        out_specs=pl.BlockSpec(memory_space=pltpu.VMEM),
        scratch_shapes=[pltpu.VMEM((q_dev * occupied, occupied), BF16)],
        compiler_params=pltpu.CompilerParams(vmem_limit_bytes=24 * 2**20),
        cost_estimate=pl.CostEstimate(
            flops=q_dev * occupied * basis * occupied, bytes_accessed=q_dev * occupied * basis, transcendentals=0
        ),
        name="exchange_rows",
    )(me, pltpu.with_memory_space_constraint(slab, pltpu.VMEM), fitted)


def body(owners, integrals, block_index, live_count, orbitals, metric):
    basis, occupied = orbitals.shape
    naux = metric.shape[1]
    q_dev = naux // owners
    me = lax.axis_index("aux").astype(jnp.int32)

    slab, pairs = half_transform(integrals, block_index.T, live_count, orbitals, q_dev, owners)

    held = lax.all_to_all(pairs, "aux", split_axis=0, concat_axis=0, tiled=True)
    held = held.reshape(naux, occupied // owners, occupied).astype(F32)
    fitted = jnp.einsum("qp,pij->qij", metric, held, precision=lax.Precision.HIGHEST).astype(BF16)
    fitted = fitted.reshape(owners, q_dev, occupied // owners, occupied)
    fitted = lax.all_to_all(fitted, "aux", split_axis=0, concat_axis=0, tiled=True)
    if (occupied // owners) % 8:
        fitted = fitted.transpose(1, 0, 2, 3).reshape(q_dev, occupied, occupied)

    def swap(x, bit):
        return lax.ppermute(x, "aux", [(d, d ^ bit) for d in range(owners)])

    mine = me.reshape(1)
    away = exchange_rows(slab, fitted, mine, owners, 1, BF16)
    arrived = swap(away, 1)
    near = exchange_rows(slab, fitted, mine, owners, 0, F32) + arrived.astype(F32)
    total = near[0]
    for k in range(1, owners // 2):
        total = total + swap(near[k].astype(BF16), 2 * k).astype(F32)
    return total


def solution(mesh):
    placed = (
        P(("groups", "aux"), None, None),
        P(("groups", "aux"), None),
        P(("groups", "aux")),
        P("groups", None),
        P("groups", None),
    )
    return jax.shard_map(
        functools.partial(body, mesh.shape["aux"]),
        mesh=mesh, in_specs=placed, out_specs=P(("groups", "aux"), None), check_vma=False,
    )
```

time: 90.7 us -> 95 us (1.047)
  Pallas kernels: 18.2 us -> 27.7 us
  blocking collectives: 27.9 us -> 20.1 us
  waiting for transfers between devices: 25.6 us -> 18.1 us
  starting transfers between devices: 9.2 us -> 15.4 us
  local copies, waits for them, and re-layouts: 5.7 us -> 10.2 us
  other arithmetic: 2.19 us -> 0.81 us
    pallas_call x1, Pallas kernels: 11 us -> 21.9 us  [half_transform(): pl.pallas_call(functools.partial(half_kernel, owners if split else 0, q_d...]
    all_to_all x1, blocking collectives: 27.9 us -> 20.1 us  [body(): held = lax.all_to_all(pairs, 'aux', split_axis=0, concat_axis=0, tiled=True)]
    ppermute x5 -> x8, waiting for transfers between devices: 11.1 us -> 3.62 us  [swap(): return lax.ppermute(x, 'aux', [(d, d ^ bit) for d in range(owners)])]
    ppermute x5 -> x8, starting transfers between devices: 5.1 us -> 11.3 us  [swap(): return lax.ppermute(x, 'aux', [(d, d ^ bit) for d in range(owners)])]
    unnamed x4 -> x6, local copies, waits for them, and re-layouts: 4.58 us -> 9.1 us
    add x3 -> x1, other arithmetic: 2.07 us -> 0.69 us  [body(): total = total + swap(near[k].astype(BF16), 2 * k).astype(F32)]
    pallas_call x2, Pallas kernels: 7.2 us -> 5.87 us  [exchange_rows(): pl.pallas_call(functools.partial(exchange_kernel, mine), out_shape=jax.Sh...]
  transfers between devices with their start and end apart: 6 -> 9, of which waited for: 5 -> 5; matrix products, arithmetic and copies ran while one was open for 0% -> 0% of each run, Pallas kernels for 4% -> 3%
where the time goes in v2:
time: 95 us; the launch traced here: 93.8 us
  Pallas kernels  27.7 us (29%)
  blocking collectives  20.1 us (21%)
  waiting for transfers between devices  18.1 us (19%)
  starting transfers between devices  15.4 us (16%)
  local copies, waits for them, and re-layouts  10.2 us (11%)
    pallas_call x1, Pallas kernels, half_transform(): pl.pallas_call(functools.partial(half_kernel, owners if split else 0, q_d...  21.9 us
    all_to_all x1, blocking collectives, body(): held = lax.all_to_all(pairs, 'aux', split_axis=0, concat_axis=0, tiled=True)  20.1 us
    all_to_all x1, waiting for transfers between devices, body(): lax.all_to_all(fitted, 'aux', split_axis=0, concat_axis=0, tiled=True)  14.5 us
    ppermute x8, starting transfers between devices, swap(): return lax.ppermute(x, 'aux', [(d, d ^ bit) for d in range(owners)])  11.3 us
    unnamed x6, local copies, waits for them, and re-layouts  9.1 us
    pallas_call x2, Pallas kernels, exchange_rows(): pl.pallas_call(functools.partial(exchange_kernel, mine), out_shape=jax.Sh...  5.87 us
    all_to_all x1, starting transfers between devices, body(): lax.all_to_all(fitted, 'aux', split_axis=0, concat_axis=0, tiled=True)  4.1 us
    ppermute x8, waiting for transfers between devices, swap(): return lax.ppermute(x, 'aux', [(d, d ^ bit) for d in range(owners)])  3.62 us
  transfers between devices with their start and end apart: 9, of which 5 were waited for; matrix products, arithmetic and copies ran while one was open for 0% of the time, Pallas kernels for 3%

profile of v2, /device:TPU:0, one launch (start us, length us, event | category | flops | bytes accessed | tf_op | source)
XLA Modules:
  0.0 93.8 jit_solution(15981349709140517769)
XLA Ops:
  0.0 0.0 copy-start
  0.7 21.9 %half_transform_pairs.1 = (bf16[384,128,128]{2,1,0:T(8,128)(2,1)S(1)}, bf16[16,16,8,128]{3,2,1,0:T(8,128)(2,1)S(1)}) custom-call(s32[1]{0:T(128)S(6)} %copy.10.live_ref, s32[3,320]{1,0:T(4,128)} %bitcast.43, bf16[320,128,128]{2,1,0:T(8,128)(2,1)} %blocks_hbm.1, bf16[3072,128]{1,0:T(8,128)(2,1)} %orb_hbm.1), custom_call_target="tpu_custom_call" | custom-call | flops 2952790016 | bytes 23068672 | tf_op jit(solution)/shard_map/half_transform_pairs/pallas_call | solution.py:149
  22.6 0.0 copy-start.1
  22.6 4.5 %copy-done.1 = bf16[384,128,128]{2,1,0:T(8,128)(2,1)} copy-done((bf16[384,128,128]{2,1,0:T(8,128)(2,1)}, bf16[384,128,128]{2,1,0:T(8,128)(2,1)S(1)}, u32[]{:S(2)}) %copy-start.1) | copy-done | bytes 12582936
  27.1 20.1 %all_to_all.10 = bf16[16,16,8,128]{3,2,1,0:T(8,128)(2,1)S(1)} all-to-all(bf16[16,16,8,128]{3,2,1,0:T(8,128)(2,1)S(1)} %get-tuple-element.8), channel_id=1, replica_groups=mesh['groups'=2,'aux'=16] {'aux'}, dimensions={0} | all-to-all | bytes 1048576 | tf_op jit(solution)/shard_map/all_to_all | solution.py:232
  47.2 0.0 copy-done
  47.2 0.7 fusion
  47.9 1.1 %copy.7 = bf16[256,8,128]{2,1,0:T(8,128)(2,1)} copy(bf16[256,8,128]{0,2,1:T(8,128)(2,1)S(1)} %fusion) | data formatting | bytes 1048576 | tf_op jit(solution)/shard_map/convert_element_type | solution.py:234
  49.0 4.1 %all-to-all-start.1 = ((bf16[16,16,8,128]{3,2,1,0:T(8,128)(2,1)}), bf16[16,16,8,128]{3,2,1,0:T(8,128)(2,1)S(1)}, u32[]{:S(2)}, u32[]{:S(2)}) async-start(bf16[16,16,8,128]{3,2,1,0:T(8,128)(2,1)} %bitcast.6), calls=%async_computation.1 | async-start | bytes 1048576 | tf_op jit(solution)/shard_map/all_to_all | solution.py:236
  53.1 14.5 %all-to-all-done.1.fitted_ref = bf16[16,16,8,128]{3,2,1,0:T(8,128)(2,1)S(1)} async-done(((bf16[16,16,8,128]{3,2,1,0:T(8,128)(2,1)}), bf16[16,16,8,128]{3,2,1,0:T(8,128)(2,1)S(1)}, u32[]{:S(2)}, u32[]{:S(2)}) %all-to-all-start.1) | async-done | bytes 524320 | tf_op jit(solution)/shard_map/all_to_all | solution.py:236
  67.6 0.0 copy-start.2
  67.6 4.6 %copy-done.2 = bf16[384,128,128]{2,1,0:T(8,128)(2,1)S(1)} copy-done((bf16[384,128,128]{2,1,0:T(8,128)(2,1)S(1)}, bf16[384,128,128]{2,1,0:T(8,128)(2,1)}, u32[]{:S(2)}) %copy-start.2) | copy-done | bytes 12582936
  72.1 2.9 %exchange_rows.3 = bf16[8,192,128]{2,1,0:T(8,128)(2,1)S(1)} custom-call(s32[1]{0:T(128)} %bitcast.me_ref, bf16[16,3072,128]{2,1,0:T(8,128)(2,1)S(1)} %bitcast.40, bf16[16,16,8,128]{3,2,1,0:T(8,128)(2,1)S(1)} %all-to-all-done.1.fitted_ref), custom_call_target="tpu_custom_call" | custom-call | flops 805306368 | bytes 6291456 | tf_op jit(solution)/shard_map/exchange_rows/pallas_call | solution.py:206
  75.1 0.1 collective-permute-start
  75.2 2.9 %exchange_rows.2 = f32[8,192,128]{2,1,0:T(8,128)S(1)} custom-call(s32[1]{0:T(128)} %bitcast.me_ref, bf16[16,3072,128]{2,1,0:T(8,128)(2,1)S(1)} %bitcast.41, bf16[16,16,8,128]{3,2,1,0:T(8,128)(2,1)S(1)} %all-to-all-done.1.fitted_ref), custom_call_target="tpu_custom_call" | custom-call | flops 805306368 | bytes 6291456 | tf_op jit(solution)/shard_map/exchange_rows/pallas_call | solution.py:206
  78.1 0.0 collective-permute-done
  78.1 0.1 fusion.10
  78.3 1.2 %collective-permute-start.1 = (bf16[192,128]{1,0:T(8,128)(2,1)S(1)}, bf16[192,128]{1,0:T(8,128)(2,1)S(1)}, u32[]{:S(2)}, u32[]{:S(2)}) collective-permute-start(bf16[192,128]{1,0:T(8,128)(2,1)S(1)} %get-tuple-element.11), channel_id=1, source_target_pairs={{0,2},{1,3},{2,0},{3,1},{4,6},{5,7},{6,4},{7,5},{8,10},{9,11},{10,... | collective-permute-start | bytes 147464 | tf_op jit(solution)/shard_map/ppermute | solution.py:241
  79.5 2.2 %collective-permute-start.7 = (bf16[192,128]{1,0:T(8,128)(2,1)S(1)}, bf16[192,128]{1,0:T(8,128)(2,1)S(1)}, u32[]{:S(2)}, u32[]{:S(2)}) collective-permute-start(bf16[192,128]{1,0:T(8,128)(2,1)S(1)} %get-tuple-element.12), channel_id=1, source_target_pairs={{0,14},{1,15},{2,12},{3,13},{4,10},{5,11},{6,8},{7,9},{8,6},{9,7},... | collective-permute-start | bytes 147464 | tf_op jit(solution)/shard_map/ppermute | solution.py:241
  81.7 1.9 %collective-permute-start.6 = (bf16[192,128]{1,0:T(8,128)(2,1)S(1)}, bf16[192,128]{1,0:T(8,128)(2,1)S(1)}, u32[]{:S(2)}, u32[]{:S(2)}) collective-permute-start(bf16[192,128]{1,0:T(8,128)(2,1)S(1)} %get-tuple-element.13), channel_id=1, source_target_pairs={{0,12},{1,13},{2,14},{3,15},{4,8},{5,9},{6,10},{7,11},{8,4},{9,5},... | collective-permute-start | bytes 147464 | tf_op jit(solution)/shard_map/ppermute | solution.py:241
  83.6 0.0 collective-permute-start.5
  83.6 3.5 %collective-permute-start.4 = (bf16[192,128]{1,0:T(8,128)(2,1)S(1)}, bf16[192,128]{1,0:T(8,128)(2,1)S(1)}, u32[]{:S(2)}, u32[]{:S(2)}) collective-permute-start(bf16[192,128]{1,0:T(8,128)(2,1)S(1)} %get-tuple-element.15), channel_id=1, source_target_pairs={{0,8},{1,9},{2,10},{3,11},{4,12},{5,13},{6,14},{7,15},{8,0},{9,1},... | collective-permute-start | bytes 147464 | tf_op jit(solution)/shard_map/ppermute | solution.py:241
  87.1 0.0 collective-permute-done.1
  87.1 0.2 collective-permute-start.3
  87.4 0.0 collective-permute-done.7
  87.4 2.1 %collective-permute-start.2 = (bf16[192,128]{1,0:T(8,128)(2,1)S(1)}, bf16[192,128]{1,0:T(8,128)(2,1)S(1)}, u32[]{:S(2)}, u32[]{:S(2)}) collective-permute-start(bf16[192,128]{1,0:T(8,128)(2,1)S(1)} %get-tuple-element.17), channel_id=1, source_target_pairs={{0,4},{1,5},{2,6},{3,7},{4,0},{5,1},{6,2},{7,3},{8,12},{9,13},{10,... | collective-permute-start | bytes 147464 | tf_op jit(solution)/shard_map/ppermute | solution.py:241
  89.5 0.0 collective-permute-done.6
  89.5 1.4 %collective-permute-done.5 = bf16[192,128]{1,0:T(8,128)(2,1)S(1)} collective-permute-done((bf16[192,128]{1,0:T(8,128)(2,1)S(1)}, bf16[192,128]{1,0:T(8,128)(2,1)S(1)}, u32[]{:S(2)}, u32[]{:S(2)}) %collective-permute-start.5) | collective-permute-done | bytes 49184 | tf_op jit(solution)/shard_map/ppermute | solution.py:241
  90.9 1.4 %collective-permute-done.4 = bf16[192,128]{1,0:T(8,128)(2,1)S(1)} collective-permute-done((bf16[192,128]{1,0:T(8,128)(2,1)S(1)}, bf16[192,128]{1,0:T(8,128)(2,1)S(1)}, u32[]{:S(2)}, u32[]{:S(2)}) %collective-permute-start.4) | collective-permute-done | bytes 49184 | tf_op jit(solution)/shard_map/ppermute | solution.py:241
  92.3 0.6 collective-permute-done.3
  92.9 0.2 collective-permute-done.2
  93.1 0.7 fusion.9
  (1 shorter events, 0.0 us)
Async XLA Ops:
  0.0 47.2 %copy-start = (f32[256,256]{1,0:T(8,128)S(1)}, f32[256,256]{1,0:T(8,128)}, u32[]{:S(2)}) copy-start(f32[256,256]{1,0:T(8,128)} %param.9) | copy-start | bytes 786436
  22.6 4.5 %copy-start.1 = (bf16[384,128,128]{2,1,0:T(8,128)(2,1)}, bf16[384,128,128]{2,1,0:T(8,128)(2,1)S(1)}, u32[]{:S(2)}) copy-start(bf16[384,128,128]{2,1,0:T(8,128)(2,1)S(1)} %get-tuple-element.7) | copy-start | bytes 37748740
  49.0 18.6 %all-to-all-start.1 = ((bf16[16,16,8,128]{3,2,1,0:T(8,128)(2,1)}), bf16[16,16,8,128]{3,2,1,0:T(8,128)(2,1)S(1)}, u32[]{:S(2)}, u32[]{:S(2)}) async-start(bf16[16,16,8,128]{3,2,1,0:T(8,128)(2,1)} %bitcast.6), calls=%async_computation.1 | async-start | bytes 1048576 | tf_op jit(solution)/shard_map/all_to_all | solution.py:236
  67.6 4.6 %copy-start.2 = (bf16[384,128,128]{2,1,0:T(8,128)(2,1)S(1)}, bf16[384,128,128]{2,1,0:T(8,128)(2,1)}, u32[]{:S(2)}) copy-start(bf16[384,128,128]{2,1,0:T(8,128)(2,1)} %copy-done.1) | copy-start | bytes 37748740
  75.1 3.0 %collective-permute-start = (bf16[8,192,128]{2,1,0:T(8,128)(2,1)S(1)}, bf16[8,192,128]{2,1,0:T(8,128)(2,1)S(1)}, u32[]{:S(2)}, u32[]{:S(2)}) collective-permute-start(bf16[8,192,128]{2,1,0:T(8,128)(2,1)S(1)} %exchange_rows.3), channel_id=1, source_target_pairs={{0,1},{1,0},{2,3},{3,2},{4,5},{5,4},{6,7},{7,6},{8,9},{9,8},{10,11... | collective-permute-start | bytes 1179656 | tf_op jit(solution)/shard_map/ppermute | solution.py:241
  78.3 8.9 %collective-permute-start.1 = (bf16[192,128]{1,0:T(8,128)(2,1)S(1)}, bf16[192,128]{1,0:T(8,128)(2,1)S(1)}, u32[]{:S(2)}, u32[]{:S(2)}) collective-permute-start(bf16[192,128]{1,0:T(8,128)(2,1)S(1)} %get-tuple-element.11), channel_id=1, source_target_pairs={{0,2},{1,3},{2,0},{3,1},{4,6},{5,7},{6,4},{7,5},{8,10},{9,11},{10,... | collective-permute-start | bytes 147464 | tf_op jit(solution)/shard_map/ppermute | solution.py:241
  79.5 7.9 %collective-permute-start.7 = (bf16[192,128]{1,0:T(8,128)(2,1)S(1)}, bf16[192,128]{1,0:T(8,128)(2,1)S(1)}, u32[]{:S(2)}, u32[]{:S(2)}) collective-permute-start(bf16[192,128]{1,0:T(8,128)(2,1)S(1)} %get-tuple-element.12), channel_id=1, source_target_pairs={{0,14},{1,15},{2,12},{3,13},{4,10},{5,11},{6,8},{7,9},{8,6},{9,7},... | collective-permute-start | bytes 147464 | tf_op jit(solution)/shard_map/ppermute | solution.py:241
  81.7 7.8 %collective-permute-start.6 = (bf16[192,128]{1,0:T(8,128)(2,1)S(1)}, bf16[192,128]{1,0:T(8,128)(2,1)S(1)}, u32[]{:S(2)}, u32[]{:S(2)}) collective-permute-start(bf16[192,128]{1,0:T(8,128)(2,1)S(1)} %get-tuple-element.13), channel_id=1, source_target_pairs={{0,12},{1,13},{2,14},{3,15},{4,8},{5,9},{6,10},{7,11},{8,4},{9,5},... | collective-permute-start | bytes 147464 | tf_op jit(solution)/shard_map/ppermute | solution.py:241
  83.6 7.3 %collective-permute-start.5 = (bf16[192,128]{1,0:T(8,128)(2,1)S(1)}, bf16[192,128]{1,0:T(8,128)(2,1)S(1)}, u32[]{:S(2)}, u32[]{:S(2)}) collective-permute-start(bf16[192,128]{1,0:T(8,128)(2,1)S(1)} %get-tuple-element.14), channel_id=1, source_target_pairs={{0,10},{1,11},{2,8},{3,9},{4,14},{5,15},{6,12},{7,13},{8,2},{9,3},... | collective-permute-start | bytes 147464 | tf_op jit(solution)/shard_map/ppermute | solution.py:241
  83.6 8.7 %collective-permute-start.4 = (bf16[192,128]{1,0:T(8,128)(2,1)S(1)}, bf16[192,128]{1,0:T(8,128)(2,1)S(1)}, u32[]{:S(2)}, u32[]{:S(2)}) collective-permute-start(bf16[192,128]{1,0:T(8,128)(2,1)S(1)} %get-tuple-element.15), channel_id=1, source_target_pairs={{0,8},{1,9},{2,10},{3,11},{4,12},{5,13},{6,14},{7,15},{8,0},{9,1},... | collective-permute-start | bytes 147464 | tf_op jit(solution)/shard_map/ppermute | solution.py:241
  87.1 5.7 %collective-permute-start.3 = (bf16[192,128]{1,0:T(8,128)(2,1)S(1)}, bf16[192,128]{1,0:T(8,128)(2,1)S(1)}, u32[]{:S(2)}, u32[]{:S(2)}) collective-permute-start(bf16[192,128]{1,0:T(8,128)(2,1)S(1)} %get-tuple-element.16), channel_id=1, source_target_pairs={{0,6},{1,7},{2,4},{3,5},{4,2},{5,3},{6,0},{7,1},{8,14},{9,15},{10,... | collective-permute-start | bytes 147464 | tf_op jit(solution)/shard_map/ppermute | solution.py:241
  87.4 5.7 %collective-permute-start.2 = (bf16[192,128]{1,0:T(8,128)(2,1)S(1)}, bf16[192,128]{1,0:T(8,128)(2,1)S(1)}, u32[]{:S(2)}, u32[]{:S(2)}) collective-permute-start(bf16[192,128]{1,0:T(8,128)(2,1)S(1)} %get-tuple-element.17), channel_id=1, source_target_pairs={{0,4},{1,5},{2,6},{3,7},{4,0},{5,1},{6,2},{7,3},{8,12},{9,13},{10,... | collective-permute-start | bytes 147464 | tf_op jit(solution)/shard_map/ppermute | solution.py:241

commit v3 on v2

--- a/solution.py
+++ b/solution.py
@@ -20,13 +20,13 @@
     key = index_ref[0:1, :] * nblk + index_ref[1:2, :]
     alive = lax.broadcasted_iota(jnp.int32, (1, slots), 1) < live
     keys[0:1, 0:slots] = jnp.where(alive, key, nkeys).astype(F32)
-    row = jnp.broadcast_to(keys[0:1, :], (wide, wide))
-    column = row.T
+    row = keys[0:1, :]
+    column = keys[...].T[:, 0:1]
     before = lax.broadcasted_iota(jnp.int32, (wide, wide), 0) < lax.broadcasted_iota(jnp.int32, (wide, wide), 1)
     rank = jnp.sum(jnp.where((column == row) & before, 1.0, 0.0), axis=0, keepdims=True)
     pair = jnp.floor(rank * 0.5)
     odd = rank - 2.0 * pair
-    opens = jnp.broadcast_to(1.0 - odd, (wide, wide)).T
+    opens = jnp.broadcast_to(1.0 - odd, (8, wide)).T[:, 0:1]
     group = jnp.sum(jnp.where(column < row, opens, 0.0), axis=0, keepdims=True) + pair
     lives = keys[0:1, :] < nkeys
     place = jnp.where(lives, 2.0 * group + odd, 2.0 * slots + 2 * UNROLL)
@@ -62,26 +62,26 @@
     for c in range(chunks):
         fetch(c).start()
 
+    nothing = slots * 256
+    held[slots] = jnp.zeros((size, size), BF16)
+
+    @pl.loop(0, nkeys, step=8)
+    def _(k):
+        for u in range(8):
+            slab[k + u] = jnp.zeros((size, occupied), BF16)
+
+    @pl.loop(0, 2 * slots, step=16)
+    def _(k):
+        for u in range(16):
+            group_slot[k + u] = nothing
+
+    for u in range(2 * UNROLL):
+        group_slot[2 * slots + u] = nothing
+
     small[0].wait()
     rank_slots(live_ref[0], index_ref, keys, meta, nblk, nkeys)
     copy = pltpu.make_async_copy(meta, facts, meta_sem.at[0])
     copy.start()
-
-    nothing = slots * 256
-    held[slots] = jnp.zeros((size, size), BF16)
-
-    @pl.loop(0, nkeys, step=4)
-    def _(k):
-        for u in range(4):
-            slab[k + u] = jnp.zeros((size, occupied), BF16)
-
-    @pl.loop(0, 2 * slots, step=16)
-    def _(k):
-        for u in range(16):
-            group_slot[k + u] = nothing
-
-    for u in range(2 * UNROLL):
-        group_slot[2 * slots + u] = nothing
 
     small[1].wait()
     for b in range(nblk):
@@ -96,7 +96,7 @@
         for u in range(8):
             place = facts[0, k + u]
             group_slot[place] = facts[1, k + u]
-            group_key[place // 2] = facts[2, k + u]
+            group_key[place >> 1] = facts[2, k + u]
 
     for u in range(UNROLL):
         group_key[groups + u] = 2 * facts[4, 0]
@@ -108,29 +108,23 @@
         for u in range(UNROLL):
             first, second = group_slot[2 * (g * UNROLL + u)], group_slot[2 * (g * UNROLL + u) + 1]
             code = group_key[g * UNROLL + u]
-            blocks = jnp.concatenate([held[first // 256], held[second // 256]], axis=1)
+            blocks = jnp.concatenate([held[first >> 8], held[second >> 8]], axis=1)
             orbs = jnp.concatenate(
-                [orb_ref[pl.ds(pl.multiple_of((s % 256) * size, size), size), :] for s in (first, second)], axis=0
+                [orb_ref[pl.ds(pl.multiple_of((s & 255) * size, size), size), :] for s in (first, second)], axis=0
             )
             product = jnp.dot(blocks, orbs, preferred_element_type=F32)
-            total = jnp.where(code % 2 == 1, product, total + product)
-            slab[code // 2] = total.astype(BF16)
+            total = jnp.where((code & 1) == 1, product, total + product)
+            slab[code >> 1] = total.astype(BF16)
         return total
 
     lax.fori_loop(0, (groups + UNROLL - 1) // UNROLL, step, jnp.zeros((size, occupied), F32))
 
     @pl.loop(0, q_dev // 2)
     def _(t):
-        total = jnp.zeros((occupied, 2 * occupied), F32)
-        for b in range(0, nblk, 2):
-            block = jnp.concatenate(
-                [
-                    jnp.concatenate([slab[(2 * t + u) * nblk + b], slab[(2 * t + u) * nblk + b + 1]], axis=0)
-                    for u in range(2)
-                ],
-                axis=1,
-            )
-            total += jnp.dot(orb_t[:, b * size : (b + 2) * size], block, preferred_element_type=F32)
+        block = jnp.concatenate(
+            [slab[pl.ds((2 * t + u) * nblk, nblk)].reshape(nblk * size, occupied) for u in range(2)], axis=1
+        )
+        total = jnp.dot(orb_t[...], block, preferred_element_type=F32)
         for u in range(2):
             pair = total[:, u * occupied : (u + 1) * occupied].T
             if owners:
@@ -180,11 +174,41 @@
     return slab.reshape(q_dev, basis, occupied), pairs
 
 
-def exchange_kernel(mine, me_ref, slab, fitted_ref, out_ref, fitted):
-    q_dev = slab.shape[0]
-    parts, each, occupied = out_ref.shape
-    me = me_ref[0]
-
+def metric_kernel(metric_ref, held_ref, out_ref, spread, mixed):
+    naux, each, occupied = held_ref.shape
+    metric = metric_ref[...]
+    high = metric.astype(BF16)
+    low = (metric - high.astype(F32)).astype(BF16)
+    spread[...] = held_ref[...].astype(F32).reshape(naux * each, occupied)
+    for r in range(each):
+        pairs = spread[pl.ds(r, naux, stride=each), :].astype(BF16)
+        fitted = jnp.dot(high, pairs, preferred_element_type=F32) + jnp.dot(low, pairs, preferred_element_type=F32)
+        mixed[pl.ds(r, naux, stride=each), :] = fitted
+    out_ref[...] = mixed[...].reshape(naux, each, occupied).astype(BF16)
+
+
+def apply_metric(metric, held):
+    naux, each, occupied = held.shape
+    if each % 8:
+        fitted = jnp.einsum("qp,pij->qij", metric, held.astype(F32), precision=lax.Precision.HIGHEST)
+        return fitted.astype(BF16)
+    return pl.pallas_call(
+        metric_kernel,
+        out_shape=jax.ShapeDtypeStruct(held.shape, BF16),
+        in_specs=[pl.BlockSpec(memory_space=pltpu.VMEM)] * 2,
+        out_specs=pl.BlockSpec(memory_space=pltpu.VMEM),
+        scratch_shapes=[pltpu.VMEM((naux * each, occupied), F32)] * 2,
+        compiler_params=pltpu.CompilerParams(vmem_limit_bytes=12 * 2**20),
+        cost_estimate=pl.CostEstimate(
+            flops=4 * naux * naux * each * occupied, bytes_accessed=4 * naux * each * occupied, transcendentals=0
+        ),
+        name="apply_metric",
+    )(metric, held)
+
+
+def gather_fitted(fitted_ref, fitted):
+    q_dev = fitted.shape[0] // fitted.shape[1]
+    occupied = fitted.shape[1]
     for q in range(q_dev):
         if len(fitted_ref.shape) == 4:
             block = fitted_ref[:, q].astype(F32).reshape(occupied, occupied).astype(BF16)
@@ -192,46 +216,69 @@
             block = fitted_ref[q]
         fitted[q * occupied : (q + 1) * occupied, :] = block
 
-    @pl.loop(0, parts)
-    def _(h):
-        owner = (2 * h + mine) ^ me
-        rows = pl.ds(pl.multiple_of(owner * each, each), each)
-        every = jnp.concatenate([slab[q, rows, :] for q in range(q_dev)], axis=1)
-        out_ref[h] = jnp.dot(every, fitted[...], preferred_element_type=F32).astype(out_ref.dtype)
-
-
-def exchange_rows(slab, fitted, me, owners, mine, dtype):
+
+def exchange_kernel(start, together, more, slab, fitted_ref, *refs):
+    refs = list(refs)
+    more_ref = refs.pop(0) if more else None
+    out_ref = refs.pop(0)
+    if start == 3:
+        fitted = refs.pop(0)
+        gather_fitted(fitted_ref, fitted)
+    else:
+        fitted = fitted_ref
+    q_dev = slab.shape[0]
+    parts, each, occupied = out_ref.shape
+    me = lax.axis_index("aux").astype(jnp.int32)
+
+    @pl.loop(0, parts // together)
+    def _(g):
+        rows = []
+        for u in range(together):
+            owner = (4 * (g * together + u) + start) ^ me
+            rows.append(pl.ds(pl.multiple_of(owner * each, each), each))
+        every = jnp.concatenate(
+            [jnp.concatenate([slab[q, r, :] for r in rows], axis=0) for q in range(q_dev)], axis=1
+        )
+        sums = jnp.dot(every, fitted[...], preferred_element_type=F32)
+        for u in range(together):
+            part = sums[u * each : (u + 1) * each]
+            if more:
+                part = part + more_ref[g * together + u].astype(F32)
+            out_ref[g * together + u] = part.astype(out_ref.dtype)
+
+
+def exchange_rows(slab, fitted, owners, start, dtype, more=None):
     q_dev, basis, occupied = slab.shape
     each = basis // owners
+    parts = owners // 4
+    out = [jax.ShapeDtypeStruct((parts, each, occupied), dtype)]
+    if start == 3:
+        out.append(jax.ShapeDtypeStruct((q_dev * occupied, occupied), BF16))
+    operands = [pltpu.with_memory_space_constraint(slab, pltpu.VMEM), fitted] + ([] if more is None else [more])
     return pl.pallas_call(
-        functools.partial(exchange_kernel, mine),
-        out_shape=jax.ShapeDtypeStruct((owners // 2, each, occupied), dtype),
-        in_specs=[
-            pl.BlockSpec(memory_space=pltpu.SMEM),
-            pl.BlockSpec(memory_space=pltpu.VMEM),
-            pl.BlockSpec(memory_space=pltpu.VMEM),
-        ],
-        out_specs=pl.BlockSpec(memory_space=pltpu.VMEM),
-        scratch_shapes=[pltpu.VMEM((q_dev * occupied, occupied), BF16)],
+        functools.partial(exchange_kernel, start, 2 if parts % 2 == 0 else 1, more is not None),
+        out_shape=out,
+        in_specs=[pl.BlockSpec(memory_space=pltpu.VMEM)] * len(operands),
+        out_specs=[pl.BlockSpec(memory_space=pltpu.VMEM)] * len(out),
         compiler_params=pltpu.CompilerParams(vmem_limit_bytes=24 * 2**20),
         cost_estimate=pl.CostEstimate(
-            flops=q_dev * occupied * basis * occupied, bytes_accessed=q_dev * occupied * basis, transcendentals=0
+            flops=2 * q_dev * occupied * basis * occupied // 4,
+            bytes_accessed=q_dev * occupied * basis // 2,
+            transcendentals=0,
         ),
         name="exchange_rows",
-    )(me, pltpu.with_memory_space_constraint(slab, pltpu.VMEM), fitted)
+    )(*operands)
 
 
 def body(owners, integrals, block_index, live_count, orbitals, metric):
     basis, occupied = orbitals.shape
     naux = metric.shape[1]
     q_dev = naux // owners
-    me = lax.axis_index("aux").astype(jnp.int32)
 
     slab, pairs = half_transform(integrals, block_index.T, live_count, orbitals, q_dev, owners)
 
     held = lax.all_to_all(pairs, "aux", split_axis=0, concat_axis=0, tiled=True)
-    held = held.reshape(naux, occupied // owners, occupied).astype(F32)
-    fitted = jnp.einsum("qp,pij->qij", metric, held, precision=lax.Precision.HIGHEST).astype(BF16)
+    fitted = apply_metric(metric, held.reshape(naux, occupied // owners, occupied))
     fitted = fitted.reshape(owners, q_dev, occupied // owners, occupied)
     fitted = lax.all_to_all(fitted, "aux", split_axis=0, concat_axis=0, tiled=True)
     if (occupied // owners) % 8:
@@ -240,13 +287,17 @@
     def swap(x, bit):
         return lax.ppermute(x, "aux", [(d, d ^ bit) for d in range(owners)])
 
-    mine = me.reshape(1)
-    away = exchange_rows(slab, fitted, mine, owners, 1, BF16)
-    arrived = swap(away, 1)
-    near = exchange_rows(slab, fitted, mine, owners, 0, F32) + arrived.astype(F32)
+    away, fitted = exchange_rows(slab, fitted, owners, 3, BF16)
+    far = swap(away, 1)
+    (away,) = exchange_rows(slab, fitted, owners, 1, BF16)
+    near = swap(away, 1)
+    (away,) = exchange_rows(slab, fitted, owners, 2, BF16, far)
+    far = swap(away, 2)
+    (near,) = exchange_rows(slab, fitted, owners, 0, F32, near)
+    near = near + far.astype(F32)
     total = near[0]
-    for k in range(1, owners // 2):
-        total = total + swap(near[k].astype(BF16), 2 * k).astype(F32)
+    for k in range(1, owners // 4):
+        total = total + swap(near[k].astype(BF16), 4 * k).astype(F32)
     return total
 
 

time: 95 us -> 81.7 us (0.86)
  blocking collectives: 20.1 us -> 46.4 us
  Pallas kernels: 27.7 us -> 16.5 us
  starting transfers between devices: 15.4 us -> 5.17 us
  local copies, waits for them, and re-layouts: 10.2 us -> 0.96 us
  waiting for transfers between devices: 18.1 us -> 10.1 us
    all_to_all x0 -> x1, blocking collectives: none -> 18.4 us  [body(): lax.all_to_all(fitted, 'aux', split_axis=0, concat_axis=0, tiled=True)]
    all_to_all x1 -> x0, waiting for transfers between devices: 14.5 us -> none  [body(): lax.all_to_all(fitted, 'aux', split_axis=0, concat_axis=0, tiled=True)]
    pallas_call x1, Pallas kernels: 21.9 us -> 11 us  [half_transform(): pl.pallas_call(functools.partial(half_kernel, owners if split else 0, q_d...]
    unnamed x6 -> x2, local copies, waits for them, and re-layouts: 9.1 us -> 0.95 us
    all_to_all x1, blocking collectives: 20.1 us -> 28.1 us  [body(): held = lax.all_to_all(pairs, 'aux', split_axis=0, concat_axis=0, tiled=True)]
    ppermute x8 -> x6, waiting for transfers between devices: 3.62 us -> 10.1 us  [swap(): return lax.ppermute(x, 'aux', [(d, d ^ bit) for d in range(owners)])]
    ppermute x8 -> x6, starting transfers between devices: 11.3 us -> 5.17 us  [swap(): return lax.ppermute(x, 'aux', [(d, d ^ bit) for d in range(owners)])]
    all_to_all x1 -> x0, starting transfers between devices: 4.1 us -> none  [body(): lax.all_to_all(fitted, 'aux', split_axis=0, concat_axis=0, tiled=True)]
  transfers between devices with their start and end apart: 9 -> 6, of which waited for: 5 -> 4; matrix products, arithmetic and copies ran while one was open for 0% -> 0% of each run, Pallas kernels for 3% -> 4%
where the time goes in v3:
time: 81.7 us; the launch traced here: 80.6 us
  blocking collectives  46.4 us (57%)
  Pallas kernels  16.5 us (20%)
  waiting for transfers between devices  10.1 us (12%)
  starting transfers between devices  5.17 us (6%)
  local copies, waits for them, and re-layouts  0.96 us (1%)
    all_to_all x1, blocking collectives, body(): held = lax.all_to_all(pairs, 'aux', split_axis=0, concat_axis=0, tiled=True)  28.1 us
    all_to_all x1, blocking collectives, body(): lax.all_to_all(fitted, 'aux', split_axis=0, concat_axis=0, tiled=True)  18.4 us
    pallas_call x1, Pallas kernels, half_transform(): pl.pallas_call(functools.partial(half_kernel, owners if split else 0, q_d...  11 us
    ppermute x6, waiting for transfers between devices, swap(): return lax.ppermute(x, 'aux', [(d, d ^ bit) for d in range(owners)])  10.1 us
    ppermute x6, starting transfers between devices, swap(): return lax.ppermute(x, 'aux', [(d, d ^ bit) for d in range(owners)])  5.17 us
    pallas_call x4, Pallas kernels, exchange_rows(): pl.pallas_call(functools.partial(exchange_kernel, start, 2 if parts % 2 =...  4.68 us
  transfers between devices with their start and end apart: 6, of which 4 were waited for; matrix products, arithmetic and copies ran while one was open for 0% of the time, Pallas kernels for 4%

profile of v3, /device:TPU:0, one launch (start us, length us, event | category | flops | bytes accessed | tf_op | source)
XLA Modules:
  0.0 80.6 jit_solution(16480241346356241647)
XLA Ops:
  0.7 11.0 %half_transform_pairs.1 = (bf16[384,128,128]{2,1,0:T(8,128)(2,1)S(1)}, bf16[16,16,8,128]{3,2,1,0:T(8,128)(2,1)S(1)}) custom-call(s32[1]{0:T(128)S(6)} %copy.6.live_ref, s32[3,320]{1,0:T(4,128)} %bitcast.24, bf16[320,128,128]{2,1,0:T(8,128)(2,1)} %blocks_hbm.1, bf16[3072,128]{1,0:T(8,128)(2,1)} %orb_hbm.1), custom_call_target="tpu_custom_call" | custom-call | flops 2952790016 | bytes 23068672 | tf_op jit(solution)/shard_map/half_transform_pairs/pallas_call | solution.py:143
  11.7 28.1 %all_to_all.10 = bf16[16,16,8,128]{3,2,1,0:T(8,128)(2,1)S(1)} all-to-all(bf16[16,16,8,128]{3,2,1,0:T(8,128)(2,1)S(1)} %get-tuple-element.10), channel_id=1, replica_groups=mesh['groups'=2,'aux'=16] {'aux'}, dimensions={0} | all-to-all | bytes 1048576 | tf_op jit(solution)/shard_map/all_to_all | solution.py:280
  39.7 0.0 copy-start
  39.7 0.9 %copy-done = f32[256,256]{1,0:T(8,128)S(1)} copy-done((f32[256,256]{1,0:T(8,128)S(1)}, f32[256,256]{1,0:T(8,128)}, u32[]{:S(2)}) %copy-start) | copy-done | bytes 262168
  40.7 0.8 %apply_metric.1 = bf16[256,8,128]{2,1,0:T(8,128)(2,1)S(1)} custom-call(f32[256,256]{1,0:T(8,128)S(1)} %copy-done, bf16[256,8,128]{2,1,0:T(8,128)(2,1)S(1)} %bitcast.22), custom_call_target="tpu_custom_call" | custom-call | flops 268435456 | bytes 1048576 | tf_op jit(solution)/shard_map/apply_metric/pallas_call | solution.py:195
  41.5 18.4 %all_to_all.11.fitted_ref = bf16[16,16,8,128]{3,2,1,0:T(8,128)(2,1)S(1)} all-to-all(bf16[16,16,8,128]{3,2,1,0:T(8,128)(2,1)S(1)} %bitcast.23), channel_id=1, replica_groups=mesh['groups'=2,'aux'=16] {'aux'}, dimensions={0} | all-to-all | bytes 1048576 | tf_op jit(solution)/shard_map/all_to_all | solution.py:283
  59.9 1.2 %exchange_rows.4 = (bf16[4,192,128]{2,1,0:T(8,128)(2,1)S(1)}, bf16[2048,128]{1,0:T(8,128)(2,1)S(1)}) custom-call(bf16[16,3072,128]{2,1,0:T(8,128)(2,1)S(1)} %bitcast.18, bf16[16,16,8,128]{3,2,1,0:T(8,128)(2,1)S(1)} %all_to_all.11.fitted_ref), custom_call_target="tpu_custom_call" | custom-call | flops 402653184 | bytes 3145728 | tf_op jit(solution)/shard_map/exchange_rows/pallas_call | solution.py:258
  61.1 0.1 collective-permute-start.1
  61.2 1.1 %exchange_rows.5 = bf16[4,192,128]{2,1,0:T(8,128)(2,1)S(1)} custom-call(bf16[16,3072,128]{2,1,0:T(8,128)(2,1)S(1)} %bitcast.19, bf16[2048,128]{1,0:T(8,128)(2,1)S(1)} %get-tuple-element.11.fitted_ref), custom_call_target="tpu_custom_call" | custom-call | flops 402653184 | bytes 3145728 | tf_op jit(solution)/shard_map/exchange_rows/pallas_call | solution.py:258
  62.4 0.6 collective-permute-start
  62.9 0.0 collective-permute-done.1.refs_0_
  62.9 1.2 %exchange_rows.7 = bf16[4,192,128]{2,1,0:T(8,128)(2,1)S(1)} custom-call(bf16[16,3072,128]{2,1,0:T(8,128)(2,1)S(1)} %bitcast.20, bf16[2048,128]{1,0:T(8,128)(2,1)S(1)} %get-tuple-element.11.fitted_ref, bf16[4,192,128]{2,1,0:T(8,128)(2,1)S(1)} %collective-permute-done.1.refs_0_), custom_call_target="tpu_custom_call" | custom-call | flops 402653184 | bytes 3145728 | tf_op jit(solution)/shard_map/exchange_rows/pallas_call | solution.py:258
  64.1 0.8 collective-permute-start.2
  64.8 0.0 collective-permute-done.refs_0_
  64.8 1.2 %exchange_rows.6 = f32[4,192,128]{2,1,0:T(8,128)S(1)} custom-call(bf16[16,3072,128]{2,1,0:T(8,128)(2,1)S(1)} %bitcast.21, bf16[2048,128]{1,0:T(8,128)(2,1)S(1)} %get-tuple-element.11.fitted_ref, bf16[4,192,128]{2,1,0:T(8,128)(2,1)S(1)} %collective-permute-done.refs_0_), custom_call_target="tpu_custom_call" | custom-call | flops 402653184 | bytes 3145728 | tf_op jit(solution)/shard_map/exchange_rows/pallas_call | solution.py:258
  66.0 5.0 %collective-permute-done.2 = bf16[4,192,128]{2,1,0:T(8,128)(2,1)S(1)} collective-permute-done((bf16[4,192,128]{2,1,0:T(8,128)(2,1)S(1)}, bf16[4,192,128]{2,1,0:T(8,128)(2,1)S(1)}, u32[]{:S(2)}, u32[]{:S(2)}) %collective-permute-start.2) | collective-permute-done | bytes 196640 | tf_op jit(solution)/shard_map/ppermute | solution.py:288
  71.0 0.1 fusion.3
  71.1 1.8 %collective-permute-start.3 = (bf16[192,128]{1,0:T(8,128)(2,1)S(1)}, bf16[192,128]{1,0:T(8,128)(2,1)S(1)}, u32[]{:S(2)}, u32[]{:S(2)}) collective-permute-start(bf16[192,128]{1,0:T(8,128)(2,1)S(1)} %get-tuple-element.15), channel_id=1, source_target_pairs={{0,4},{1,5},{2,6},{3,7},{4,0},{5,1},{6,2},{7,3},{8,12},{9,13},{10,... | collective-permute-start | bytes 147464 | tf_op jit(solution)/shard_map/ppermute | solution.py:288
  72.9 2.0 %collective-permute-start.5 = (bf16[192,128]{1,0:T(8,128)(2,1)S(1)}, bf16[192,128]{1,0:T(8,128)(2,1)S(1)}, u32[]{:S(2)}, u32[]{:S(2)}) collective-permute-start(bf16[192,128]{1,0:T(8,128)(2,1)S(1)} %get-tuple-element.16), channel_id=1, source_target_pairs={{0,12},{1,13},{2,14},{3,15},{4,8},{5,9},{6,10},{7,11},{8,4},{9,5},... | collective-permute-start | bytes 147464 | tf_op jit(solution)/shard_map/ppermute | solution.py:288
  74.9 0.0 collective-permute-start.4
  74.9 0.4 collective-permute-done.3
  75.2 3.5 %collective-permute-done.5 = bf16[192,128]{1,0:T(8,128)(2,1)S(1)} collective-permute-done((bf16[192,128]{1,0:T(8,128)(2,1)S(1)}, bf16[192,128]{1,0:T(8,128)(2,1)S(1)}, u32[]{:S(2)}, u32[]{:S(2)}) %collective-permute-start.5) | collective-permute-done | bytes 49184 | tf_op jit(solution)/shard_map/ppermute | solution.py:288
  78.8 1.2 %collective-permute-done.4 = bf16[192,128]{1,0:T(8,128)(2,1)S(1)} collective-permute-done((bf16[192,128]{1,0:T(8,128)(2,1)S(1)}, bf16[192,128]{1,0:T(8,128)(2,1)S(1)}, u32[]{:S(2)}, u32[]{:S(2)}) %collective-permute-start.4) | collective-permute-done | bytes 49184 | tf_op jit(solution)/shard_map/ppermute | solution.py:288
  80.0 0.7 fusion.2
  (1 shorter events, 0.0 us)
Async XLA Ops:
  39.7 1.0 %copy-start = (f32[256,256]{1,0:T(8,128)S(1)}, f32[256,256]{1,0:T(8,128)}, u32[]{:S(2)}) copy-start(f32[256,256]{1,0:T(8,128)} %metric_ref.1) | copy-start | bytes 786436
  61.1 1.8 %collective-permute-start.1 = (bf16[4,192,128]{2,1,0:T(8,128)(2,1)S(1)}, bf16[4,192,128]{2,1,0:T(8,128)(2,1)S(1)}, u32[]{:S(2)}, u32[]{:S(2)}) collective-permute-start(bf16[4,192,128]{2,1,0:T(8,128)(2,1)S(1)} %get-tuple-element.12), channel_id=1, source_target_pairs={{0,1},{1,0},{2,3},{3,2},{4,5},{5,4},{6,7},{7,6},{8,9},{9,8},{10,11... | collective-permute-start | bytes 589832 | tf_op jit(solution)/shard_map/ppermute | solution.py:288
  62.4 2.5 %collective-permute-start = (bf16[4,192,128]{2,1,0:T(8,128)(2,1)S(1)}, bf16[4,192,128]{2,1,0:T(8,128)(2,1)S(1)}, u32[]{:S(2)}, u32[]{:S(2)}) collective-permute-start(bf16[4,192,128]{2,1,0:T(8,128)(2,1)S(1)} %exchange_rows.5), channel_id=1, source_target_pairs={{0,1},{1,0},{2,3},{3,2},{4,5},{5,4},{6,7},{7,6},{8,9},{9,8},{10,11... | collective-permute-start | bytes 589832 | tf_op jit(solution)/shard_map/ppermute | solution.py:288
  64.1 6.9 %collective-permute-start.2 = (bf16[4,192,128]{2,1,0:T(8,128)(2,1)S(1)}, bf16[4,192,128]{2,1,0:T(8,128)(2,1)S(1)}, u32[]{:S(2)}, u32[]{:S(2)}) collective-permute-start(bf16[4,192,128]{2,1,0:T(8,128)(2,1)S(1)} %exchange_rows.7), channel_id=1, source_target_pairs={{0,2},{1,3},{2,0},{3,1},{4,6},{5,7},{6,4},{7,5},{8,10},{9,11},{10,... | collective-permute-start | bytes 589832 | tf_op jit(solution)/shard_map/ppermute | solution.py:288
  71.1 4.2 %collective-permute-start.3 = (bf16[192,128]{1,0:T(8,128)(2,1)S(1)}, bf16[192,128]{1,0:T(8,128)(2,1)S(1)}, u32[]{:S(2)}, u32[]{:S(2)}) collective-permute-start(bf16[192,128]{1,0:T(8,128)(2,1)S(1)} %get-tuple-element.15), channel_id=1, source_target_pairs={{0,4},{1,5},{2,6},{3,7},{4,0},{5,1},{6,2},{7,3},{8,12},{9,13},{10,... | collective-permute-start | bytes 147464 | tf_op jit(solution)/shard_map/ppermute | solution.py:288
  72.9 5.9 %collective-permute-start.5 = (bf16[192,128]{1,0:T(8,128)(2,1)S(1)}, bf16[192,128]{1,0:T(8,128)(2,1)S(1)}, u32[]{:S(2)}, u32[]{:S(2)}) collective-permute-start(bf16[192,128]{1,0:T(8,128)(2,1)S(1)} %get-tuple-element.16), channel_id=1, source_target_pairs={{0,12},{1,13},{2,14},{3,15},{4,8},{5,9},{6,10},{7,11},{8,4},{9,5},... | collective-permute-start | bytes 147464 | tf_op jit(solution)/shard_map/ppermute | solution.py:288
  74.9 5.1 %collective-permute-start.4 = (bf16[192,128]{1,0:T(8,128)(2,1)S(1)}, bf16[192,128]{1,0:T(8,128)(2,1)S(1)}, u32[]{:S(2)}, u32[]{:S(2)}) collective-permute-start(bf16[192,128]{1,0:T(8,128)(2,1)S(1)} %get-tuple-element.17), channel_id=1, source_target_pairs={{0,8},{1,9},{2,10},{3,11},{4,12},{5,13},{6,14},{7,15},{8,0},{9,1},... | collective-permute-start | bytes 147464 | tf_op jit(solution)/shard_map/ppermute | solution.py:288

commit v4 on v3

--- a/solution.py
+++ b/solution.py
@@ -13,35 +13,43 @@
 BF16 = jnp.bfloat16
 
 
-def rank_slots(live, index_ref, keys, meta, nblk, nkeys):
+def rank_slots(live, index_ref, rows, meta, nblk, nkeys):
     slots = index_ref.shape[1]
-    wide = keys.shape[1]
-    keys[...] = jnp.full(keys.shape, nkeys, F32)
+    wide = rows.shape[1]
+    many = meta.shape[1]
+    nothing = float(slots * 256)
+    rows[...] = jnp.full(rows.shape, nkeys, F32)
     key = index_ref[0:1, :] * nblk + index_ref[1:2, :]
-    alive = lax.broadcasted_iota(jnp.int32, (1, slots), 1) < live
-    keys[0:1, 0:slots] = jnp.where(alive, key, nkeys).astype(F32)
-    row = keys[0:1, :]
-    column = keys[...].T[:, 0:1]
+    slot = lax.broadcasted_iota(jnp.int32, (1, slots), 1)
+    rows[0:1, 0:slots] = jnp.where(slot < live, key, nkeys).astype(F32)
+    rows[1:2, 0:slots] = (slot * 256 + index_ref[2:3, :]).astype(F32)
+    row = rows[0:1, :]
+    column = rows[...].T[:, 0:1]
     before = lax.broadcasted_iota(jnp.int32, (wide, wide), 0) < lax.broadcasted_iota(jnp.int32, (wide, wide), 1)
     rank = jnp.sum(jnp.where((column == row) & before, 1.0, 0.0), axis=0, keepdims=True)
     pair = jnp.floor(rank * 0.5)
     odd = rank - 2.0 * pair
     opens = jnp.broadcast_to(1.0 - odd, (8, wide)).T[:, 0:1]
     group = jnp.sum(jnp.where(column < row, opens, 0.0), axis=0, keepdims=True) + pair
-    lives = keys[0:1, :] < nkeys
-    place = jnp.where(lives, 2.0 * group + odd, 2.0 * slots + 2 * UNROLL)
+    lives = row < nkeys
     count = jnp.sum(jnp.where(lives, 1.0 - odd, 0.0), axis=1, keepdims=True)
-    last = jnp.max(jnp.where(lives, keys[0:1, :], 0.0), axis=1, keepdims=True)
-    meta[0:1, :] = place.astype(jnp.int32)
-    meta[1:2, 0:slots] = lax.broadcasted_iota(jnp.int32, (1, slots), 1) * 256 + index_ref[2:3, :]
-    meta[2:3, :] = (2.0 * keys[0:1, :] + jnp.where(rank < 2.0, 1.0, 0.0)).astype(jnp.int32)
-    meta[3:4, :] = jnp.broadcast_to(count, (1, wide)).astype(jnp.int32)
-    meta[4:5, :] = jnp.broadcast_to(last, (1, wide)).astype(jnp.int32)
+    last = 2.0 * jnp.max(jnp.where(lives, row, 0.0), axis=1, keepdims=True)
+    rows[1:2, :] = rows[1:2, :] - nothing
+    rows[2:3, :] = jnp.where(lives, 2.0 * group + odd, -1.0)
+    rows[3:4, :] = jnp.where(lives & (odd == 0.0), group, -1.0)
+    rows[4:5, :] = 2.0 * row + jnp.where(rank < 2.0, 1.0, 0.0) - last
+    columns = rows[...].T
+    place = lax.broadcasted_iota(jnp.int32, (1, many), 1).astype(F32)
+    members = jnp.sum(jnp.where(columns[:, 2:3] == place, columns[:, 1:2], 0.0), axis=0, keepdims=True)
+    keys = jnp.sum(jnp.where(columns[:, 3:4] == place[:, :wide], columns[:, 4:5], 0.0), axis=0, keepdims=True)
+    meta[0:1, :] = (members + nothing).astype(jnp.int32)
+    meta[1:2, 0:wide] = (keys + last).astype(jnp.int32)
+    meta[2:3, :] = jnp.broadcast_to(count, (1, many)).astype(jnp.int32)
 
 
 def half_kernel(
-    owners, q_dev, live_ref, index_hbm, blocks_hbm, orb_hbm, slab, pairs_ref,
-    index_ref, held, orb_ref, orb_t, keys, meta, facts, group_slot, group_key, in_sem, meta_sem,
+    owners, q_dev, live_ref, index_hbm, blocks_hbm, orb_hbm, metric_hbm, slab, pairs_ref, split_ref,
+    index_ref, held, orb_ref, metric_ref, orb_t, rows, meta, facts, in_sem, small_sem,
 ):
     slots, size, _ = blocks_hbm.shape
     occupied = orb_ref.shape[1]
@@ -53,61 +61,51 @@
         part = pl.ds(c * CHUNK, CHUNK)
         return pltpu.make_async_copy(blocks_hbm.at[part], held.at[part], in_sem.at[c])
 
+    def clear(first, last):
+        @pl.loop(first, last, step=8)
+        def _(k):
+            for u in range(8):
+                slab[k + u] = jnp.zeros((size, occupied), BF16)
+
     small = [
-        pltpu.make_async_copy(source, target, meta_sem.at[1 + k])
-        for k, (source, target) in enumerate([(index_hbm, index_ref), (orb_hbm, orb_ref)])
+        pltpu.make_async_copy(source, target, small_sem.at[1 + k])
+        for k, (source, target) in enumerate(
+            [(index_hbm, index_ref), (orb_hbm, orb_ref), (metric_hbm, metric_ref)]
+        )
     ]
     for copy in small:
         copy.start()
     for c in range(chunks):
         fetch(c).start()
 
-    nothing = slots * 256
     held[slots] = jnp.zeros((size, size), BF16)
-
-    @pl.loop(0, nkeys, step=8)
-    def _(k):
-        for u in range(8):
-            slab[k + u] = jnp.zeros((size, occupied), BF16)
-
-    @pl.loop(0, 2 * slots, step=16)
-    def _(k):
-        for u in range(16):
-            group_slot[k + u] = nothing
-
-    for u in range(2 * UNROLL):
-        group_slot[2 * slots + u] = nothing
+    clear(0, nkeys // 2)
 
     small[0].wait()
-    rank_slots(live_ref[0], index_ref, keys, meta, nblk, nkeys)
-    copy = pltpu.make_async_copy(meta, facts, meta_sem.at[0])
+    rank_slots(live_ref[0], index_ref, rows, meta, nblk, nkeys)
+    copy = pltpu.make_async_copy(meta, facts, small_sem.at[0])
     copy.start()
 
+    clear(nkeys // 2, nkeys)
     small[1].wait()
     for b in range(nblk):
-        rows = slice(b * size, (b + 1) * size)
-        orb_t[:, rows] = orb_ref[rows, :].T
+        part = slice(b * size, (b + 1) * size)
+        orb_t[:, part] = orb_ref[part, :].T
+    small[2].wait()
+    metric = metric_ref[...]
+    high = metric.astype(BF16)
+    split_ref[0] = high
+    split_ref[1] = (metric - high.astype(F32)).astype(BF16)
 
     copy.wait()
-    groups = facts[3, 0]
-
-    @pl.loop(0, slots, step=8)
-    def _(k):
-        for u in range(8):
-            place = facts[0, k + u]
-            group_slot[place] = facts[1, k + u]
-            group_key[place >> 1] = facts[2, k + u]
-
-    for u in range(UNROLL):
-        group_key[groups + u] = 2 * facts[4, 0]
-
+    groups = facts[2, 0]
     for c in range(chunks):
         fetch(c).wait()
 
     def step(g, total):
         for u in range(UNROLL):
-            first, second = group_slot[2 * (g * UNROLL + u)], group_slot[2 * (g * UNROLL + u) + 1]
-            code = group_key[g * UNROLL + u]
+            first, second = facts[0, 2 * (g * UNROLL + u)], facts[0, 2 * (g * UNROLL + u) + 1]
+            code = facts[1, g * UNROLL + u]
             blocks = jnp.concatenate([held[first >> 8], held[second >> 8]], axis=1)
             orbs = jnp.concatenate(
                 [orb_ref[pl.ds(pl.multiple_of((s & 255) * size, size), size), :] for s in (first, second)], axis=0
@@ -133,33 +131,34 @@
                 pairs_ref[2 * t + u] = pair.astype(BF16)
 
 
-def half_transform(blocks, index, live, orbitals, q_dev, owners):
+def half_transform(blocks, index, live, orbitals, metric, q_dev, owners):
     slots, size, _ = blocks.shape
     basis, occupied = orbitals.shape
     nblk = basis // size
     split = (occupied // owners) % 8 == 0
     pairs_shape = (owners, q_dev, occupied // owners, occupied) if split else (q_dev, occupied, occupied)
-    wide = -(-slots // 128) * 128
-    slab, pairs = pl.pallas_call(
+    wide = -(-(slots + UNROLL) // 128) * 128
+    many = -(-2 * (slots + UNROLL) // 128) * 128
+    slab, pairs, metric_split = pl.pallas_call(
         functools.partial(half_kernel, owners if split else 0, q_dev),
         out_shape=(
             pltpu.VMEM((q_dev * nblk, size, occupied), BF16),
             jax.ShapeDtypeStruct(pairs_shape, BF16),
+            pltpu.VMEM((2,) + metric.shape, BF16),
         ),
-        in_specs=[pl.BlockSpec(memory_space=pltpu.SMEM)] + [pl.BlockSpec(memory_space=pl.ANY)] * 3,
-        out_specs=(pl.BlockSpec(memory_space=pltpu.VMEM), pl.BlockSpec(memory_space=pltpu.VMEM)),
+        in_specs=[pl.BlockSpec(memory_space=pltpu.SMEM)] + [pl.BlockSpec(memory_space=pl.ANY)] * 4,
+        out_specs=(pl.BlockSpec(memory_space=pltpu.VMEM),) * 3,
         scratch_shapes=[
             pltpu.VMEM(index.shape, jnp.int32),
             pltpu.VMEM((slots + 1, size, size), BF16),
             pltpu.VMEM((basis, occupied), BF16),
+            pltpu.VMEM(metric.shape, F32),
             pltpu.VMEM((occupied, basis), BF16),
             pltpu.VMEM((8, wide), F32),
-            pltpu.VMEM((8, wide), jnp.int32),
-            pltpu.SMEM((8, wide), jnp.int32),
-            pltpu.SMEM((2 * slots + 2 * UNROLL + 2,), jnp.int32),
-            pltpu.SMEM((slots + UNROLL + 1,), jnp.int32),
+            pltpu.VMEM((8, many), jnp.int32),
+            pltpu.SMEM((8, many), jnp.int32),
             pltpu.SemaphoreType.DMA((slots // CHUNK,)),
-            pltpu.SemaphoreType.DMA((3,)),
+            pltpu.SemaphoreType.DMA((4,)),
         ],
         compiler_params=pltpu.CompilerParams(vmem_limit_bytes=36 * 2**20),
         cost_estimate=pl.CostEstimate(
@@ -168,32 +167,38 @@
             transcendentals=0,
         ),
         name="half_transform_pairs",
-    )(live, *(pltpu.with_memory_space_constraint(x, pltpu.HBM) for x in (index, blocks, orbitals)))
+    )(live, *(pltpu.with_memory_space_constraint(x, pltpu.HBM) for x in (index, blocks, orbitals, metric)))
     if not split:
         pairs = pairs.reshape(q_dev, owners, occupied // owners, occupied).transpose(1, 0, 2, 3)
-    return slab.reshape(q_dev, basis, occupied), pairs
-
-
-def metric_kernel(metric_ref, held_ref, out_ref, spread, mixed):
+    return slab.reshape(q_dev, basis, occupied), pairs, metric_split
+
+
+def metric_kernel(order, split_ref, held_ref, out_ref, spread, mixed):
     naux, each, occupied = held_ref.shape
-    metric = metric_ref[...]
-    high = metric.astype(BF16)
-    low = (metric - high.astype(F32)).astype(BF16)
-    spread[...] = held_ref[...].astype(F32).reshape(naux * each, occupied)
+    q_dev = naux // len(order)
+    for k, d in enumerate(order):
+        block = held_ref[k * q_dev : (k + 1) * q_dev].astype(F32)
+        spread[d * q_dev * each : (d + 1) * q_dev * each, :] = block.reshape(q_dev * each, occupied)
     for r in range(each):
         pairs = spread[pl.ds(r, naux, stride=each), :].astype(BF16)
-        fitted = jnp.dot(high, pairs, preferred_element_type=F32) + jnp.dot(low, pairs, preferred_element_type=F32)
+        fitted = jnp.dot(split_ref[0], pairs, preferred_element_type=F32)
+        fitted = fitted + jnp.dot(split_ref[1], pairs, preferred_element_type=F32)
         mixed[pl.ds(r, naux, stride=each), :] = fitted
-    out_ref[...] = mixed[...].reshape(naux, each, occupied).astype(BF16)
-
-
-def apply_metric(metric, held):
+    for k, d in enumerate(order):
+        block = mixed[d * q_dev * each : (d + 1) * q_dev * each, :]
+        out_ref[k * q_dev : (k + 1) * q_dev] = block.reshape(q_dev, each, occupied).astype(BF16)
+
+
+def apply_metric(metric, metric_split, held, order):
     naux, each, occupied = held.shape
     if each % 8:
-        fitted = jnp.einsum("qp,pij->qij", metric, held.astype(F32), precision=lax.Precision.HIGHEST)
-        return fitted.astype(BF16)
+        q_dev = naux // len(order)
+        back = [order.index(d) for d in range(len(order))]
+        held = held.reshape(len(order), q_dev, each, occupied)[jnp.array(back)].reshape(held.shape)
+        fitted = jnp.einsum("qp,pij->qij", metric, held.astype(F32), precision=lax.Precision.HIGHEST).astype(BF16)
+        return fitted.reshape(len(order), q_dev, each, occupied)[jnp.array(order)].reshape(held.shape)
     return pl.pallas_call(
-        metric_kernel,
+        functools.partial(metric_kernel, order),
         out_shape=jax.ShapeDtypeStruct(held.shape, BF16),
         in_specs=[pl.BlockSpec(memory_space=pltpu.VMEM)] * 2,
         out_specs=pl.BlockSpec(memory_space=pltpu.VMEM),
@@ -203,7 +208,7 @@
             flops=4 * naux * naux * each * occupied, bytes_accessed=4 * naux * each * occupied, transcendentals=0
         ),
         name="apply_metric",
-    )(metric, held)
+    )(pltpu.with_memory_space_constraint(metric_split, pltpu.VMEM), held)
 
 
 def gather_fitted(fitted_ref, fitted):
@@ -256,7 +261,7 @@
         out.append(jax.ShapeDtypeStruct((q_dev * occupied, occupied), BF16))
     operands = [pltpu.with_memory_space_constraint(slab, pltpu.VMEM), fitted] + ([] if more is None else [more])
     return pl.pallas_call(
-        functools.partial(exchange_kernel, start, 2 if parts % 2 == 0 else 1, more is not None),
+        functools.partial(exchange_kernel, start, 4 if parts % 4 == 0 else 1, more is not None),
         out_shape=out,
         in_specs=[pl.BlockSpec(memory_space=pltpu.VMEM)] * len(operands),
         out_specs=[pl.BlockSpec(memory_space=pltpu.VMEM)] * len(out),
@@ -275,12 +280,15 @@
     naux = metric.shape[1]
     q_dev = naux // owners
 
-    slab, pairs = half_transform(integrals, block_index.T, live_count, orbitals, q_dev, owners)
-
-    held = lax.all_to_all(pairs, "aux", split_axis=0, concat_axis=0, tiled=True)
-    fitted = apply_metric(metric, held.reshape(naux, occupied // owners, occupied))
-    fitted = fitted.reshape(owners, q_dev, occupied // owners, occupied)
-    fitted = lax.all_to_all(fitted, "aux", split_axis=0, concat_axis=0, tiled=True)
+    slab, pairs, metric_split = half_transform(integrals, block_index.T, live_count, orbitals, metric, q_dev, owners)
+
+    order = [4 * a + b for b in range(4) for a in range(owners // 4)]
+    trade = functools.partial(
+        lax.all_to_all, axis_name="aux", split_axis=0, concat_axis=0, tiled=True, axis_index_groups=[order]
+    )
+    held = trade(pairs).reshape(naux, occupied // owners, occupied)
+    fitted = apply_metric(metric, metric_split, held, order)
+    fitted = trade(fitted.reshape(owners, q_dev, occupied // owners, occupied))
     if (occupied // owners) % 8:
         fitted = fitted.transpose(1, 0, 2, 3).reshape(q_dev, occupied, occupied)
 

time: 81.7 us -> 78.9 us (0.966)
  blocking collectives: 46.4 us -> 39.5 us
  Pallas kernels: 16.5 us -> 23.3 us
  local copies, waits for them, and re-layouts: 0.96 us -> 0.01 us
  waiting for transfers between devices: 10.1 us -> 9.23 us
    pallas_call x1, Pallas kernels: 11 us -> 18.5 us  [half_transform(): pl.pallas_call(functools.partial(half_kernel, owners if split else 0, q_d...]
    all_to_all x2, blocking collectives: 46.4 us -> 39.5 us  [the longest x1 20.6 us: body(): held = trade(pairs).reshape(naux, occupied // owners, occupied)]
    unnamed x2 -> x0, local copies, waits for them, and re-layouts: 0.95 us -> none
    ppermute x6, waiting for transfers between devices: 10.1 us -> 9.23 us  [swap(): return lax.ppermute(x, 'aux', [(d, d ^ bit) for d in range(owners)])]
where the time goes in v4:
time: 78.9 us; the launch traced here: 78.3 us
  blocking collectives  39.5 us (50%)
  Pallas kernels  23.3 us (30%)
  waiting for transfers between devices  9.23 us (12%)
  starting transfers between devices  4.8 us (6%)
    all_to_all x1, blocking collectives, body(): held = trade(pairs).reshape(naux, occupied // owners, occupied)  20.6 us
    all_to_all x1, blocking collectives, body(): fitted = trade(fitted.reshape(owners, q_dev, occupied // owners, occupied))  18.9 us
    pallas_call x1, Pallas kernels, half_transform(): pl.pallas_call(functools.partial(half_kernel, owners if split else 0, q_d...  18.5 us
    ppermute x6, waiting for transfers between devices, swap(): return lax.ppermute(x, 'aux', [(d, d ^ bit) for d in range(owners)])  9.23 us
    ppermute x6, starting transfers between devices, swap(): return lax.ppermute(x, 'aux', [(d, d ^ bit) for d in range(owners)])  4.8 us
    pallas_call x4, Pallas kernels, exchange_rows(): pl.pallas_call(functools.partial(exchange_kernel, start, 4 if parts % 4 =...  3.98 us
  transfers between devices with their start and end apart: 6, of which 4 were waited for; matrix products, arithmetic and copies ran while one was open for 0% of the time, Pallas kernels for 4%

profile of v4, /device:TPU:0, one launch (start us, length us, event | category | flops | bytes accessed | tf_op | source)
XLA Modules:
  0.0 78.3 jit_solution(11152038138646850358)
XLA Ops:
  0.7 18.5 %half_transform_pairs.1 = (bf16[384,128,128]{2,1,0:T(8,128)(2,1)S(1)}, bf16[16,16,8,128]{3,2,1,0:T(8,128)(2,1)S(1)}, bf16[2,256,256]{2,1,0:T(8,128)(2,1)S(1)}) custom-call(s32[1]{0:T(128)S(6)} %copy.6.live_ref, s32[3,320]{1,0:T(4,128)} %bitcast.24, bf16[320,128,128]{2,1,0:T(8,128)(2,1)} %blocks_hbm.1, bf16[3072,128]{1,0:T(8,128)(2,1)} %orb_hbm.1, ...), custom_call_target="tpu_custom_call" | custom-call | flops 2952790016 | bytes 23068672 | tf_op jit(solution)/shard_map/half_transform_pairs/pallas_call | solution.py:142
  19.2 20.6 %all_to_all.10 = bf16[16,16,8,128]{3,2,1,0:T(8,128)(2,1)S(1)} all-to-all(bf16[16,16,8,128]{3,2,1,0:T(8,128)(2,1)S(1)} %get-tuple-element.12), channel_id=1, replica_groups={{0,4,8,12,1,5,9,13,2,6,10,14,3,7,11,15},{16,20,24,28,17,21,25,29,18,22,..., dimensions={0} | all-to-all | bytes 1048576 | tf_op jit(solution)/shard_map/all_to_all | solution.py:289
  39.8 0.8 %apply_metric.1 = bf16[256,8,128]{2,1,0:T(8,128)(2,1)S(1)} custom-call(bf16[2,256,256]{2,1,0:T(8,128)(2,1)S(1)} %get-tuple-element.11.split_ref, bf16[256,8,128]{2,1,0:T(8,128)(2,1)S(1)} %bitcast.22), custom_call_target="tpu_custom_call" | custom-call | flops 268435456 | bytes 1048576 | tf_op jit(solution)/shard_map/apply_metric/pallas_call | solution.py:200
  40.6 18.9 %all_to_all.11.fitted_ref = bf16[16,16,8,128]{3,2,1,0:T(8,128)(2,1)S(1)} all-to-all(bf16[16,16,8,128]{3,2,1,0:T(8,128)(2,1)S(1)} %bitcast.23), channel_id=1, replica_groups={{0,4,8,12,1,5,9,13,2,6,10,14,3,7,11,15},{16,20,24,28,17,21,25,29,18,22,..., dimensions={0} | all-to-all | bytes 1048576 | tf_op jit(solution)/shard_map/all_to_all | solution.py:291
  59.5 1.0 %exchange_rows.4 = (bf16[4,192,128]{2,1,0:T(8,128)(2,1)S(1)}, bf16[2048,128]{1,0:T(8,128)(2,1)S(1)}) custom-call(bf16[16,3072,128]{2,1,0:T(8,128)(2,1)S(1)} %bitcast.18, bf16[16,16,8,128]{3,2,1,0:T(8,128)(2,1)S(1)} %all_to_all.11.fitted_ref), custom_call_target="tpu_custom_call" | custom-call | flops 402653184 | bytes 3145728 | tf_op jit(solution)/shard_map/exchange_rows/pallas_call | solution.py:263
  60.5 0.1 collective-permute-start.1
  60.6 1.0 %exchange_rows.5 = bf16[4,192,128]{2,1,0:T(8,128)(2,1)S(1)} custom-call(bf16[16,3072,128]{2,1,0:T(8,128)(2,1)S(1)} %bitcast.19, bf16[2048,128]{1,0:T(8,128)(2,1)S(1)} %get-tuple-element.13.fitted_ref), custom_call_target="tpu_custom_call" | custom-call | flops 402653184 | bytes 3145728 | tf_op jit(solution)/shard_map/exchange_rows/pallas_call | solution.py:263
  61.6 0.6 collective-permute-start
  62.1 0.0 collective-permute-done.1.refs_0_
  62.1 1.0 %exchange_rows.7 = bf16[4,192,128]{2,1,0:T(8,128)(2,1)S(1)} custom-call(bf16[16,3072,128]{2,1,0:T(8,128)(2,1)S(1)} %bitcast.20, bf16[2048,128]{1,0:T(8,128)(2,1)S(1)} %get-tuple-element.13.fitted_ref, bf16[4,192,128]{2,1,0:T(8,128)(2,1)S(1)} %collective-permute-done.1.refs_0_), custom_call_target="tpu_custom_call" | custom-call | flops 402653184 | bytes 3145728 | tf_op jit(solution)/shard_map/exchange_rows/pallas_call | solution.py:263
  63.1 0.6 collective-permute-start.2
  63.8 0.0 collective-permute-done.refs_0_
  63.8 1.0 %exchange_rows.6 = f32[4,192,128]{2,1,0:T(8,128)S(1)} custom-call(bf16[16,3072,128]{2,1,0:T(8,128)(2,1)S(1)} %bitcast.21, bf16[2048,128]{1,0:T(8,128)(2,1)S(1)} %get-tuple-element.13.fitted_ref, bf16[4,192,128]{2,1,0:T(8,128)(2,1)S(1)} %collective-permute-done.refs_0_), custom_call_target="tpu_custom_call" | custom-call | flops 402653184 | bytes 3145728 | tf_op jit(solution)/shard_map/exchange_rows/pallas_call | solution.py:263
  64.7 5.3 %collective-permute-done.2 = bf16[4,192,128]{2,1,0:T(8,128)(2,1)S(1)} collective-permute-done((bf16[4,192,128]{2,1,0:T(8,128)(2,1)S(1)}, bf16[4,192,128]{2,1,0:T(8,128)(2,1)S(1)}, u32[]{:S(2)}, u32[]{:S(2)}) %collective-permute-start.2) | collective-permute-done | bytes 196640 | tf_op jit(solution)/shard_map/ppermute | solution.py:296
  70.0 0.1 fusion.3
  70.1 0.1 collective-permute-start.3
  70.2 1.7 %collective-permute-start.5 = (bf16[192,128]{1,0:T(8,128)(2,1)S(1)}, bf16[192,128]{1,0:T(8,128)(2,1)S(1)}, u32[]{:S(2)}, u32[]{:S(2)}) collective-permute-start(bf16[192,128]{1,0:T(8,128)(2,1)S(1)} %get-tuple-element.18), channel_id=1, source_target_pairs={{0,12},{1,13},{2,14},{3,15},{4,8},{5,9},{6,10},{7,11},{8,4},{9,5},... | collective-permute-start | bytes 147464 | tf_op jit(solution)/shard_map/ppermute | solution.py:296
  71.9 1.8 %collective-permute-start.4 = (bf16[192,128]{1,0:T(8,128)(2,1)S(1)}, bf16[192,128]{1,0:T(8,128)(2,1)S(1)}, u32[]{:S(2)}, u32[]{:S(2)}) collective-permute-start(bf16[192,128]{1,0:T(8,128)(2,1)S(1)} %get-tuple-element.19), channel_id=1, source_target_pairs={{0,8},{1,9},{2,10},{3,11},{4,12},{5,13},{6,14},{7,15},{8,0},{9,1},... | collective-permute-start | bytes 147464 | tf_op jit(solution)/shard_map/ppermute | solution.py:296
  73.7 1.2 %collective-permute-done.3 = bf16[192,128]{1,0:T(8,128)(2,1)S(1)} collective-permute-done((bf16[192,128]{1,0:T(8,128)(2,1)S(1)}, bf16[192,128]{1,0:T(8,128)(2,1)S(1)}, u32[]{:S(2)}, u32[]{:S(2)}) %collective-permute-start.3) | collective-permute-done | bytes 49184 | tf_op jit(solution)/shard_map/ppermute | solution.py:296
  74.8 1.4 %collective-permute-done.5 = bf16[192,128]{1,0:T(8,128)(2,1)S(1)} collective-permute-done((bf16[192,128]{1,0:T(8,128)(2,1)S(1)}, bf16[192,128]{1,0:T(8,128)(2,1)S(1)}, u32[]{:S(2)}, u32[]{:S(2)}) %collective-permute-start.5) | collective-permute-done | bytes 49184 | tf_op jit(solution)/shard_map/ppermute | solution.py:296
  76.2 1.4 %collective-permute-done.4 = bf16[192,128]{1,0:T(8,128)(2,1)S(1)} collective-permute-done((bf16[192,128]{1,0:T(8,128)(2,1)S(1)}, bf16[192,128]{1,0:T(8,128)(2,1)S(1)}, u32[]{:S(2)}, u32[]{:S(2)}) %collective-permute-start.4) | collective-permute-done | bytes 49184 | tf_op jit(solution)/shard_map/ppermute | solution.py:296
  77.6 0.7 fusion.2
  (1 shorter events, 0.0 us)
Async XLA Ops:
  60.5 1.6 %collective-permute-start.1 = (bf16[4,192,128]{2,1,0:T(8,128)(2,1)S(1)}, bf16[4,192,128]{2,1,0:T(8,128)(2,1)S(1)}, u32[]{:S(2)}, u32[]{:S(2)}) collective-permute-start(bf16[4,192,128]{2,1,0:T(8,128)(2,1)S(1)} %get-tuple-element.14), channel_id=1, source_target_pairs={{0,1},{1,0},{2,3},{3,2},{4,5},{5,4},{6,7},{7,6},{8,9},{9,8},{10,11... | collective-permute-start | bytes 589832 | tf_op jit(solution)/shard_map/ppermute | solution.py:296
  61.6 2.2 %collective-permute-start = (bf16[4,192,128]{2,1,0:T(8,128)(2,1)S(1)}, bf16[4,192,128]{2,1,0:T(8,128)(2,1)S(1)}, u32[]{:S(2)}, u32[]{:S(2)}) collective-permute-start(bf16[4,192,128]{2,1,0:T(8,128)(2,1)S(1)} %exchange_rows.5), channel_id=1, source_target_pairs={{0,1},{1,0},{2,3},{3,2},{4,5},{5,4},{6,7},{7,6},{8,9},{9,8},{10,11... | collective-permute-start | bytes 589832 | tf_op jit(solution)/shard_map/ppermute | solution.py:296
  63.1 6.9 %collective-permute-start.2 = (bf16[4,192,128]{2,1,0:T(8,128)(2,1)S(1)}, bf16[4,192,128]{2,1,0:T(8,128)(2,1)S(1)}, u32[]{:S(2)}, u32[]{:S(2)}) collective-permute-start(bf16[4,192,128]{2,1,0:T(8,128)(2,1)S(1)} %exchange_rows.7), channel_id=1, source_target_pairs={{0,2},{1,3},{2,0},{3,1},{4,6},{5,7},{6,4},{7,5},{8,10},{9,11},{10,... | collective-permute-start | bytes 589832 | tf_op jit(solution)/shard_map/ppermute | solution.py:296
  70.1 4.7 %collective-permute-start.3 = (bf16[192,128]{1,0:T(8,128)(2,1)S(1)}, bf16[192,128]{1,0:T(8,128)(2,1)S(1)}, u32[]{:S(2)}, u32[]{:S(2)}) collective-permute-start(bf16[192,128]{1,0:T(8,128)(2,1)S(1)} %get-tuple-element.17), channel_id=1, source_target_pairs={{0,4},{1,5},{2,6},{3,7},{4,0},{5,1},{6,2},{7,3},{8,12},{9,13},{10,... | collective-permute-start | bytes 147464 | tf_op jit(solution)/shard_map/ppermute | solution.py:296
  70.2 6.1 %collective-permute-start.5 = (bf16[192,128]{1,0:T(8,128)(2,1)S(1)}, bf16[192,128]{1,0:T(8,128)(2,1)S(1)}, u32[]{:S(2)}, u32[]{:S(2)}) collective-permute-start(bf16[192,128]{1,0:T(8,128)(2,1)S(1)} %get-tuple-element.18), channel_id=1, source_target_pairs={{0,12},{1,13},{2,14},{3,15},{4,8},{5,9},{6,10},{7,11},{8,4},{9,5},... | collective-permute-start | bytes 147464 | tf_op jit(solution)/shard_map/ppermute | solution.py:296
  71.9 5.8 %collective-permute-start.4 = (bf16[192,128]{1,0:T(8,128)(2,1)S(1)}, bf16[192,128]{1,0:T(8,128)(2,1)S(1)}, u32[]{:S(2)}, u32[]{:S(2)}) collective-permute-start(bf16[192,128]{1,0:T(8,128)(2,1)S(1)} %get-tuple-element.19), channel_id=1, source_target_pairs={{0,8},{1,9},{2,10},{3,11},{4,12},{5,13},{6,14},{7,15},{8,0},{9,1},... | collective-permute-start | bytes 147464 | tf_op jit(solution)/shard_map/ppermute | solution.py:296

commit v5 on v4

--- a/solution.py
+++ b/solution.py
@@ -16,7 +16,6 @@
 def rank_slots(live, index_ref, rows, meta, nblk, nkeys):
     slots = index_ref.shape[1]
     wide = rows.shape[1]
-    many = meta.shape[1]
     nothing = float(slots * 256)
     rows[...] = jnp.full(rows.shape, nkeys, F32)
     key = index_ref[0:1, :] * nblk + index_ref[1:2, :]
@@ -26,25 +25,20 @@
     row = rows[0:1, :]
     column = rows[...].T[:, 0:1]
     before = lax.broadcasted_iota(jnp.int32, (wide, wide), 0) < lax.broadcasted_iota(jnp.int32, (wide, wide), 1)
-    rank = jnp.sum(jnp.where((column == row) & before, 1.0, 0.0), axis=0, keepdims=True)
-    pair = jnp.floor(rank * 0.5)
-    odd = rank - 2.0 * pair
-    opens = jnp.broadcast_to(1.0 - odd, (8, wide)).T[:, 0:1]
-    group = jnp.sum(jnp.where(column < row, opens, 0.0), axis=0, keepdims=True) + pair
+    same = (column == row) & before
+    rank = jnp.sum(jnp.where(same, 1.0, 0.0), axis=0, keepdims=True)
+    place = jnp.sum(jnp.where(same | (column < row), 1.0, 0.0), axis=0, keepdims=True)
     lives = row < nkeys
-    count = jnp.sum(jnp.where(lives, 1.0 - odd, 0.0), axis=1, keepdims=True)
     last = 2.0 * jnp.max(jnp.where(lives, row, 0.0), axis=1, keepdims=True)
     rows[1:2, :] = rows[1:2, :] - nothing
-    rows[2:3, :] = jnp.where(lives, 2.0 * group + odd, -1.0)
-    rows[3:4, :] = jnp.where(lives & (odd == 0.0), group, -1.0)
-    rows[4:5, :] = 2.0 * row + jnp.where(rank < 2.0, 1.0, 0.0) - last
+    rows[2:3, :] = jnp.where(lives, place, -1.0)
+    rows[3:4, :] = 2.0 * row + jnp.where(rank == 0.0, 1.0, 0.0) - last
     columns = rows[...].T
-    place = lax.broadcasted_iota(jnp.int32, (1, many), 1).astype(F32)
-    members = jnp.sum(jnp.where(columns[:, 2:3] == place, columns[:, 1:2], 0.0), axis=0, keepdims=True)
-    keys = jnp.sum(jnp.where(columns[:, 3:4] == place[:, :wide], columns[:, 4:5], 0.0), axis=0, keepdims=True)
+    found = columns[:, 2:3] == lax.broadcasted_iota(jnp.int32, (1, wide), 1).astype(F32)
+    members = jnp.sum(jnp.where(found, columns[:, 1:2], 0.0), axis=0, keepdims=True)
+    keys = jnp.sum(jnp.where(found, columns[:, 3:4], 0.0), axis=0, keepdims=True)
     meta[0:1, :] = (members + nothing).astype(jnp.int32)
-    meta[1:2, 0:wide] = (keys + last).astype(jnp.int32)
-    meta[2:3, :] = jnp.broadcast_to(count, (1, many)).astype(jnp.int32)
+    meta[1:2, :] = (keys + last).astype(jnp.int32)
 
 
 def half_kernel(
@@ -94,30 +88,26 @@
     small[2].wait()
     metric = metric_ref[...]
     high = metric.astype(BF16)
-    split_ref[0] = high
-    split_ref[1] = (metric - high.astype(F32)).astype(BF16)
+    naux = metric.shape[0]
+    split_ref[0:naux, :] = high
+    split_ref[naux : 2 * naux, :] = (metric - high.astype(F32)).astype(BF16)
 
     copy.wait()
-    groups = facts[2, 0]
     for c in range(chunks):
         fetch(c).wait()
 
     def step(g, total):
         for u in range(UNROLL):
-            first, second = facts[0, 2 * (g * UNROLL + u)], facts[0, 2 * (g * UNROLL + u) + 1]
-            code = facts[1, g * UNROLL + u]
-            blocks = jnp.concatenate([held[first >> 8], held[second >> 8]], axis=1)
-            orbs = jnp.concatenate(
-                [orb_ref[pl.ds(pl.multiple_of((s & 255) * size, size), size), :] for s in (first, second)], axis=0
-            )
-            product = jnp.dot(blocks, orbs, preferred_element_type=F32)
+            slot, code = facts[0, g * UNROLL + u], facts[1, g * UNROLL + u]
+            orbs = orb_ref[pl.ds(pl.multiple_of((slot & 255) * size, size), size), :]
+            product = jnp.dot(held[slot >> 8], orbs, preferred_element_type=F32)
             total = jnp.where((code & 1) == 1, product, total + product)
             slab[code >> 1] = total.astype(BF16)
         return total
 
-    lax.fori_loop(0, (groups + UNROLL - 1) // UNROLL, step, jnp.zeros((size, occupied), F32))
-
-    @pl.loop(0, q_dev // 2)
+    lax.fori_loop(0, (live_ref[0] + UNROLL - 1) // UNROLL, step, jnp.zeros((size, occupied), F32))
+
+    @pl.loop(0, q_dev // 2, unroll=2)
     def _(t):
         block = jnp.concatenate(
             [slab[pl.ds((2 * t + u) * nblk, nblk)].reshape(nblk * size, occupied) for u in range(2)], axis=1
@@ -138,13 +128,12 @@
     split = (occupied // owners) % 8 == 0
     pairs_shape = (owners, q_dev, occupied // owners, occupied) if split else (q_dev, occupied, occupied)
     wide = -(-(slots + UNROLL) // 128) * 128
-    many = -(-2 * (slots + UNROLL) // 128) * 128
     slab, pairs, metric_split = pl.pallas_call(
         functools.partial(half_kernel, owners if split else 0, q_dev),
         out_shape=(
             pltpu.VMEM((q_dev * nblk, size, occupied), BF16),
             jax.ShapeDtypeStruct(pairs_shape, BF16),
-            pltpu.VMEM((2,) + metric.shape, BF16),
+            pltpu.VMEM((2 * metric.shape[0], metric.shape[1]), BF16),
         ),
         in_specs=[pl.BlockSpec(memory_space=pltpu.SMEM)] + [pl.BlockSpec(memory_space=pl.ANY)] * 4,
         out_specs=(pl.BlockSpec(memory_space=pltpu.VMEM),) * 3,
@@ -155,8 +144,8 @@
             pltpu.VMEM(metric.shape, F32),
             pltpu.VMEM((occupied, basis), BF16),
             pltpu.VMEM((8, wide), F32),
-            pltpu.VMEM((8, many), jnp.int32),
-            pltpu.SMEM((8, many), jnp.int32),
+            pltpu.VMEM((8, wide), jnp.int32),
+            pltpu.SMEM((8, wide), jnp.int32),
             pltpu.SemaphoreType.DMA((slots // CHUNK,)),
             pltpu.SemaphoreType.DMA((4,)),
         ],
@@ -173,32 +162,25 @@
     return slab.reshape(q_dev, basis, occupied), pairs, metric_split
 
 
-def metric_kernel(order, split_ref, held_ref, out_ref, spread, mixed):
+def metric_kernel(split_ref, held_ref, out_ref, spread, mixed):
     naux, each, occupied = held_ref.shape
-    q_dev = naux // len(order)
-    for k, d in enumerate(order):
-        block = held_ref[k * q_dev : (k + 1) * q_dev].astype(F32)
-        spread[d * q_dev * each : (d + 1) * q_dev * each, :] = block.reshape(q_dev * each, occupied)
-    for r in range(each):
-        pairs = spread[pl.ds(r, naux, stride=each), :].astype(BF16)
-        fitted = jnp.dot(split_ref[0], pairs, preferred_element_type=F32)
-        fitted = fitted + jnp.dot(split_ref[1], pairs, preferred_element_type=F32)
-        mixed[pl.ds(r, naux, stride=each), :] = fitted
-    for k, d in enumerate(order):
-        block = mixed[d * q_dev * each : (d + 1) * q_dev * each, :]
-        out_ref[k * q_dev : (k + 1) * q_dev] = block.reshape(q_dev, each, occupied).astype(BF16)
-
-
-def apply_metric(metric, metric_split, held, order):
+    spread[...] = held_ref[...].astype(F32).reshape(naux * each, occupied)
+    for r in range(0, each, 2):
+        both = [spread[pl.ds(r + u, naux, stride=each), :].astype(BF16) for u in range(2)]
+        parts = jnp.dot(split_ref[...], jnp.concatenate(both, axis=1), preferred_element_type=F32)
+        fitted = parts[:naux] + parts[naux:]
+        for u in range(2):
+            mixed[pl.ds(r + u, naux, stride=each), :] = fitted[:, u * occupied : (u + 1) * occupied]
+    out_ref[...] = mixed[...].reshape(naux, each, occupied).astype(BF16)
+
+
+def apply_metric(metric, metric_split, held):
     naux, each, occupied = held.shape
     if each % 8:
-        q_dev = naux // len(order)
-        back = [order.index(d) for d in range(len(order))]
-        held = held.reshape(len(order), q_dev, each, occupied)[jnp.array(back)].reshape(held.shape)
-        fitted = jnp.einsum("qp,pij->qij", metric, held.astype(F32), precision=lax.Precision.HIGHEST).astype(BF16)
-        return fitted.reshape(len(order), q_dev, each, occupied)[jnp.array(order)].reshape(held.shape)
+        fitted = jnp.einsum("qp,pij->qij", metric, held.astype(F32), precision=lax.Precision.HIGHEST)
+        return fitted.astype(BF16)
     return pl.pallas_call(
-        functools.partial(metric_kernel, order),
+        metric_kernel,
         out_shape=jax.ShapeDtypeStruct(held.shape, BF16),
         in_specs=[pl.BlockSpec(memory_space=pltpu.VMEM)] * 2,
         out_specs=pl.BlockSpec(memory_space=pltpu.VMEM),
@@ -282,12 +264,9 @@
 
     slab, pairs, metric_split = half_transform(integrals, block_index.T, live_count, orbitals, metric, q_dev, owners)
 
-    order = [4 * a + b for b in range(4) for a in range(owners // 4)]
-    trade = functools.partial(
-        lax.all_to_all, axis_name="aux", split_axis=0, concat_axis=0, tiled=True, axis_index_groups=[order]
-    )
+    trade = functools.partial(lax.all_to_all, axis_name="aux", split_axis=0, concat_axis=0, tiled=True)
     held = trade(pairs).reshape(naux, occupied // owners, occupied)
-    fitted = apply_metric(metric, metric_split, held, order)
+    fitted = apply_metric(metric, metric_split, held)
     fitted = trade(fitted.reshape(owners, q_dev, occupied // owners, occupied))
     if (occupied // owners) % 8:
         fitted = fitted.transpose(1, 0, 2, 3).reshape(q_dev, occupied, occupied)

time: 78.9 us -> 77.4 us (0.981); the launches traced: 78.3 us -> 78.4 us
  Pallas kernels: 23.3 us -> 13.1 us
  blocking collectives: 39.5 us -> 48.3 us
  waiting for transfers between devices: 9.23 us -> 10.3 us
    pallas_call x1, Pallas kernels: 18.5 us -> 8.55 us  [half_transform(): pl.pallas_call(functools.partial(half_kernel, owners if split else 0, q_d...]
    all_to_all x1, blocking collectives: 20.6 us -> 30 us  [body(): held = trade(pairs).reshape(naux, occupied // owners, occupied)]
    ppermute x6, waiting for transfers between devices: 9.23 us -> 10.3 us  [swap(): return lax.ppermute(x, 'aux', [(d, d ^ bit) for d in range(owners)])]
where the time goes in v5:
time: 77.4 us; the launch traced here: 78.4 us
  blocking collectives  48.3 us (62%)
  Pallas kernels  13.1 us (17%)
  waiting for transfers between devices  10.3 us (13%)
  starting transfers between devices  5.17 us (7%)
    all_to_all x1, blocking collectives, body(): held = trade(pairs).reshape(naux, occupied // owners, occupied)  30 us
    all_to_all x1, blocking collectives, body(): fitted = trade(fitted.reshape(owners, q_dev, occupied // owners, occupied))  18.4 us
    ppermute x6, waiting for transfers between devices, swap(): return lax.ppermute(x, 'aux', [(d, d ^ bit) for d in range(owners)])  10.3 us
    pallas_call x1, Pallas kernels, half_transform(): pl.pallas_call(functools.partial(half_kernel, owners if split else 0, q_d...  8.55 us
    ppermute x6, starting transfers between devices, swap(): return lax.ppermute(x, 'aux', [(d, d ^ bit) for d in range(owners)])  5.17 us
    pallas_call x4, Pallas kernels, exchange_rows(): pl.pallas_call(functools.partial(exchange_kernel, start, 4 if parts % 4 =...  3.98 us
  transfers between devices with their start and end apart: 6, of which 4 were waited for; matrix products, arithmetic and copies ran while one was open for 0% of the time, Pallas kernels for 4%

profile of v5, /device:TPU:0, one launch (start us, length us, event | category | flops | bytes accessed | tf_op | source)
XLA Modules:
  0.0 78.4 jit_solution(7912115017824638287)
XLA Ops:
  0.7 8.6 %half_transform_pairs.1 = (bf16[384,128,128]{2,1,0:T(8,128)(2,1)S(1)}, bf16[16,16,8,128]{3,2,1,0:T(8,128)(2,1)S(1)}, bf16[512,256]{1,0:T(8,128)(2,1)S(1)}) custom-call(s32[1]{0:T(128)S(6)} %copy.6.live_ref, s32[3,320]{1,0:T(4,128)} %bitcast.24, bf16[320,128,128]{2,1,0:T(8,128)(2,1)} %blocks_hbm.1, bf16[3072,128]{1,0:T(8,128)(2,1)} %orb_hbm.1, ...), custom_call_target="tpu_custom_call" | custom-call | flops 2952790016 | bytes 23068672 | tf_op jit(solution)/shard_map/half_transform_pairs/pallas_call | solution.py:131
  9.2 30.0 %all_to_all.10 = bf16[16,16,8,128]{3,2,1,0:T(8,128)(2,1)S(1)} all-to-all(bf16[16,16,8,128]{3,2,1,0:T(8,128)(2,1)S(1)} %get-tuple-element.12), channel_id=1, replica_groups=mesh['groups'=2,'aux'=16] {'aux'}, dimensions={0} | all-to-all | bytes 1048576 | tf_op jit(solution)/shard_map/all_to_all | solution.py:268
  39.2 0.6 apply_metric.1
  39.8 18.4 %all_to_all.11.fitted_ref = bf16[16,16,8,128]{3,2,1,0:T(8,128)(2,1)S(1)} all-to-all(bf16[16,16,8,128]{3,2,1,0:T(8,128)(2,1)S(1)} %bitcast.23), channel_id=1, replica_groups=mesh['groups'=2,'aux'=16] {'aux'}, dimensions={0} | all-to-all | bytes 1048576 | tf_op jit(solution)/shard_map/all_to_all | solution.py:270
  58.2 1.0 %exchange_rows.4 = (bf16[4,192,128]{2,1,0:T(8,128)(2,1)S(1)}, bf16[2048,128]{1,0:T(8,128)(2,1)S(1)}) custom-call(bf16[16,3072,128]{2,1,0:T(8,128)(2,1)S(1)} %bitcast.18, bf16[16,16,8,128]{3,2,1,0:T(8,128)(2,1)S(1)} %all_to_all.11.fitted_ref), custom_call_target="tpu_custom_call" | custom-call | flops 402653184 | bytes 3145728 | tf_op jit(solution)/shard_map/exchange_rows/pallas_call | solution.py:245
  59.2 0.1 collective-permute-start.1
  59.3 1.0 %exchange_rows.5 = bf16[4,192,128]{2,1,0:T(8,128)(2,1)S(1)} custom-call(bf16[16,3072,128]{2,1,0:T(8,128)(2,1)S(1)} %bitcast.19, bf16[2048,128]{1,0:T(8,128)(2,1)S(1)} %get-tuple-element.13.fitted_ref), custom_call_target="tpu_custom_call" | custom-call | flops 402653184 | bytes 3145728 | tf_op jit(solution)/shard_map/exchange_rows/pallas_call | solution.py:245
  60.3 0.6 collective-permute-start
  60.8 0.0 collective-permute-done.1.refs_0_
  60.8 1.0 %exchange_rows.7 = bf16[4,192,128]{2,1,0:T(8,128)(2,1)S(1)} custom-call(bf16[16,3072,128]{2,1,0:T(8,128)(2,1)S(1)} %bitcast.20, bf16[2048,128]{1,0:T(8,128)(2,1)S(1)} %get-tuple-element.13.fitted_ref, bf16[4,192,128]{2,1,0:T(8,128)(2,1)S(1)} %collective-permute-done.1.refs_0_), custom_call_target="tpu_custom_call" | custom-call | flops 402653184 | bytes 3145728 | tf_op jit(solution)/shard_map/exchange_rows/pallas_call | solution.py:245
  61.8 0.7 collective-permute-start.2
  62.6 0.0 collective-permute-done.refs_0_
  62.6 1.0 %exchange_rows.6 = f32[4,192,128]{2,1,0:T(8,128)S(1)} custom-call(bf16[16,3072,128]{2,1,0:T(8,128)(2,1)S(1)} %bitcast.21, bf16[2048,128]{1,0:T(8,128)(2,1)S(1)} %get-tuple-element.13.fitted_ref, bf16[4,192,128]{2,1,0:T(8,128)(2,1)S(1)} %collective-permute-done.refs_0_), custom_call_target="tpu_custom_call" | custom-call | flops 402653184 | bytes 3145728 | tf_op jit(solution)/shard_map/exchange_rows/pallas_call | solution.py:245
  63.6 5.2 %collective-permute-done.2 = bf16[4,192,128]{2,1,0:T(8,128)(2,1)S(1)} collective-permute-done((bf16[4,192,128]{2,1,0:T(8,128)(2,1)S(1)}, bf16[4,192,128]{2,1,0:T(8,128)(2,1)S(1)}, u32[]{:S(2)}, u32[]{:S(2)}) %collective-permute-start.2) | collective-permute-done | bytes 196640 | tf_op jit(solution)/shard_map/ppermute | solution.py:275
  68.7 0.1 fusion.3
  68.8 1.8 %collective-permute-start.3 = (bf16[192,128]{1,0:T(8,128)(2,1)S(1)}, bf16[192,128]{1,0:T(8,128)(2,1)S(1)}, u32[]{:S(2)}, u32[]{:S(2)}) collective-permute-start(bf16[192,128]{1,0:T(8,128)(2,1)S(1)} %get-tuple-element.17), channel_id=1, source_target_pairs={{0,4},{1,5},{2,6},{3,7},{4,0},{5,1},{6,2},{7,3},{8,12},{9,13},{10,... | collective-permute-start | bytes 147464 | tf_op jit(solution)/shard_map/ppermute | solution.py:275
  70.6 2.0 %collective-permute-start.5 = (bf16[192,128]{1,0:T(8,128)(2,1)S(1)}, bf16[192,128]{1,0:T(8,128)(2,1)S(1)}, u32[]{:S(2)}, u32[]{:S(2)}) collective-permute-start(bf16[192,128]{1,0:T(8,128)(2,1)S(1)} %get-tuple-element.18), channel_id=1, source_target_pairs={{0,12},{1,13},{2,14},{3,15},{4,8},{5,9},{6,10},{7,11},{8,4},{9,5},... | collective-permute-start | bytes 147464 | tf_op jit(solution)/shard_map/ppermute | solution.py:275
  72.6 0.0 collective-permute-start.4
  72.6 0.4 collective-permute-done.3
  73.0 3.5 %collective-permute-done.5 = bf16[192,128]{1,0:T(8,128)(2,1)S(1)} collective-permute-done((bf16[192,128]{1,0:T(8,128)(2,1)S(1)}, bf16[192,128]{1,0:T(8,128)(2,1)S(1)}, u32[]{:S(2)}, u32[]{:S(2)}) %collective-permute-start.5) | collective-permute-done | bytes 49184 | tf_op jit(solution)/shard_map/ppermute | solution.py:275
  76.5 1.2 %collective-permute-done.4 = bf16[192,128]{1,0:T(8,128)(2,1)S(1)} collective-permute-done((bf16[192,128]{1,0:T(8,128)(2,1)S(1)}, bf16[192,128]{1,0:T(8,128)(2,1)S(1)}, u32[]{:S(2)}, u32[]{:S(2)}) %collective-permute-start.4) | collective-permute-done | bytes 49184 | tf_op jit(solution)/shard_map/ppermute | solution.py:275
  77.7 0.7 fusion.2
  (1 shorter events, 0.0 us)
Async XLA Ops:
  59.2 1.6 %collective-permute-start.1 = (bf16[4,192,128]{2,1,0:T(8,128)(2,1)S(1)}, bf16[4,192,128]{2,1,0:T(8,128)(2,1)S(1)}, u32[]{:S(2)}, u32[]{:S(2)}) collective-permute-start(bf16[4,192,128]{2,1,0:T(8,128)(2,1)S(1)} %get-tuple-element.14), channel_id=1, source_target_pairs={{0,1},{1,0},{2,3},{3,2},{4,5},{5,4},{6,7},{7,6},{8,9},{9,8},{10,11... | collective-permute-start | bytes 589832 | tf_op jit(solution)/shard_map/ppermute | solution.py:275
  60.3 2.3 %collective-permute-start = (bf16[4,192,128]{2,1,0:T(8,128)(2,1)S(1)}, bf16[4,192,128]{2,1,0:T(8,128)(2,1)S(1)}, u32[]{:S(2)}, u32[]{:S(2)}) collective-permute-start(bf16[4,192,128]{2,1,0:T(8,128)(2,1)S(1)} %exchange_rows.5), channel_id=1, source_target_pairs={{0,1},{1,0},{2,3},{3,2},{4,5},{5,4},{6,7},{7,6},{8,9},{9,8},{10,11... | collective-permute-start | bytes 589832 | tf_op jit(solution)/shard_map/ppermute | solution.py:275
  61.8 6.9 %collective-permute-start.2 = (bf16[4,192,128]{2,1,0:T(8,128)(2,1)S(1)}, bf16[4,192,128]{2,1,0:T(8,128)(2,1)S(1)}, u32[]{:S(2)}, u32[]{:S(2)}) collective-permute-start(bf16[4,192,128]{2,1,0:T(8,128)(2,1)S(1)} %exchange_rows.7), channel_id=1, source_target_pairs={{0,2},{1,3},{2,0},{3,1},{4,6},{5,7},{6,4},{7,5},{8,10},{9,11},{10,... | collective-permute-start | bytes 589832 | tf_op jit(solution)/shard_map/ppermute | solution.py:275
  68.8 4.2 %collective-permute-start.3 = (bf16[192,128]{1,0:T(8,128)(2,1)S(1)}, bf16[192,128]{1,0:T(8,128)(2,1)S(1)}, u32[]{:S(2)}, u32[]{:S(2)}) collective-permute-start(bf16[192,128]{1,0:T(8,128)(2,1)S(1)} %get-tuple-element.17), channel_id=1, source_target_pairs={{0,4},{1,5},{2,6},{3,7},{4,0},{5,1},{6,2},{7,3},{8,12},{9,13},{10,... | collective-permute-start | bytes 147464 | tf_op jit(solution)/shard_map/ppermute | solution.py:275
  70.6 5.9 %collective-permute-start.5 = (bf16[192,128]{1,0:T(8,128)(2,1)S(1)}, bf16[192,128]{1,0:T(8,128)(2,1)S(1)}, u32[]{:S(2)}, u32[]{:S(2)}) collective-permute-start(bf16[192,128]{1,0:T(8,128)(2,1)S(1)} %get-tuple-element.18), channel_id=1, source_target_pairs={{0,12},{1,13},{2,14},{3,15},{4,8},{5,9},{6,10},{7,11},{8,4},{9,5},... | collective-permute-start | bytes 147464 | tf_op jit(solution)/shard_map/ppermute | solution.py:275
  72.6 5.1 %collective-permute-start.4 = (bf16[192,128]{1,0:T(8,128)(2,1)S(1)}, bf16[192,128]{1,0:T(8,128)(2,1)S(1)}, u32[]{:S(2)}, u32[]{:S(2)}) collective-permute-start(bf16[192,128]{1,0:T(8,128)(2,1)S(1)} %get-tuple-element.19), channel_id=1, source_target_pairs={{0,8},{1,9},{2,10},{3,11},{4,12},{5,13},{6,14},{7,15},{8,0},{9,1},... | collective-permute-start | bytes 147464 | tf_op jit(solution)/shard_map/ppermute | solution.py:275

commit v6 on v5

--- a/solution.py
+++ b/solution.py
@@ -7,7 +7,7 @@
 from jax.experimental.pallas import tpu as pltpu
 from jax.sharding import PartitionSpec as P
 
-UNROLL = 8
+UNROLL = 32
 CHUNK = 32
 F32 = jnp.float32
 BF16 = jnp.bfloat16
@@ -107,7 +107,7 @@
 
     lax.fori_loop(0, (live_ref[0] + UNROLL - 1) // UNROLL, step, jnp.zeros((size, occupied), F32))
 
-    @pl.loop(0, q_dev // 2, unroll=2)
+    @pl.loop(0, q_dev // 2, unroll=4)
     def _(t):
         block = jnp.concatenate(
             [slab[pl.ds((2 * t + u) * nblk, nblk)].reshape(nblk * size, occupied) for u in range(2)], axis=1

time: 77.4 us -> 72.7 us (0.939); the launches traced: 78.4 us -> 71.6 us
  blocking collectives: 48.3 us -> 40.9 us
    all_to_all x1, blocking collectives: 30 us -> 22.5 us  [body(): held = trade(pairs).reshape(naux, occupied // owners, occupied)]
where the time goes in v6:
time: 72.7 us; the launch traced here: 71.6 us
  blocking collectives  40.9 us (56%)
  Pallas kernels  13.8 us (19%)
  waiting for transfers between devices  10.3 us (14%)
  starting transfers between devices  5.17 us (7%)
    all_to_all x1, blocking collectives, body(): held = trade(pairs).reshape(naux, occupied // owners, occupied)  22.5 us
    all_to_all x1, blocking collectives, body(): fitted = trade(fitted.reshape(owners, q_dev, occupied // owners, occupied))  18.4 us
    ppermute x6, waiting for transfers between devices, swap(): return lax.ppermute(x, 'aux', [(d, d ^ bit) for d in range(owners)])  10.3 us
    pallas_call x1, Pallas kernels, half_transform(): pl.pallas_call(functools.partial(half_kernel, owners if split else 0, q_d...  9.16 us
    ppermute x6, starting transfers between devices, swap(): return lax.ppermute(x, 'aux', [(d, d ^ bit) for d in range(owners)])  5.17 us
    pallas_call x4, Pallas kernels, exchange_rows(): pl.pallas_call(functools.partial(exchange_kernel, start, 4 if parts % 4 =...  3.98 us
  transfers between devices with their start and end apart: 6, of which 4 were waited for; matrix products, arithmetic and copies ran while one was open for 0% of the time, Pallas kernels for 4%

profile of v6, /device:TPU:0, one launch (start us, length us, event | category | flops | bytes accessed | tf_op | source)
XLA Modules:
  0.0 71.6 jit_solution(18403364045399159420)
XLA Ops:
  0.7 9.2 %half_transform_pairs.1 = (bf16[384,128,128]{2,1,0:T(8,128)(2,1)S(1)}, bf16[16,16,8,128]{3,2,1,0:T(8,128)(2,1)S(1)}, bf16[512,256]{1,0:T(8,128)(2,1)S(1)}) custom-call(s32[1]{0:T(128)S(6)} %copy.6.live_ref, s32[3,320]{1,0:T(4,128)} %bitcast.24, bf16[320,128,128]{2,1,0:T(8,128)(2,1)} %blocks_hbm.1, bf16[3072,128]{1,0:T(8,128)(2,1)} %orb_hbm.1, ...), custom_call_target="tpu_custom_call" | custom-call | flops 2952790016 | bytes 23068672 | tf_op jit(solution)/shard_map/half_transform_pairs/pallas_call | solution.py:131
  9.8 22.5 %all_to_all.10 = bf16[16,16,8,128]{3,2,1,0:T(8,128)(2,1)S(1)} all-to-all(bf16[16,16,8,128]{3,2,1,0:T(8,128)(2,1)S(1)} %get-tuple-element.12), channel_id=1, replica_groups=mesh['groups'=2,'aux'=16] {'aux'}, dimensions={0} | all-to-all | bytes 1048576 | tf_op jit(solution)/shard_map/all_to_all | solution.py:268
  32.4 0.6 apply_metric.1
  33.0 18.4 %all_to_all.11.fitted_ref = bf16[16,16,8,128]{3,2,1,0:T(8,128)(2,1)S(1)} all-to-all(bf16[16,16,8,128]{3,2,1,0:T(8,128)(2,1)S(1)} %bitcast.23), channel_id=1, replica_groups=mesh['groups'=2,'aux'=16] {'aux'}, dimensions={0} | all-to-all | bytes 1048576 | tf_op jit(solution)/shard_map/all_to_all | solution.py:270
  51.3 1.0 %exchange_rows.4 = (bf16[4,192,128]{2,1,0:T(8,128)(2,1)S(1)}, bf16[2048,128]{1,0:T(8,128)(2,1)S(1)}) custom-call(bf16[16,3072,128]{2,1,0:T(8,128)(2,1)S(1)} %bitcast.18, bf16[16,16,8,128]{3,2,1,0:T(8,128)(2,1)S(1)} %all_to_all.11.fitted_ref), custom_call_target="tpu_custom_call" | custom-call | flops 402653184 | bytes 3145728 | tf_op jit(solution)/shard_map/exchange_rows/pallas_call | solution.py:245
  52.4 0.1 collective-permute-start.1
  52.5 1.0 %exchange_rows.5 = bf16[4,192,128]{2,1,0:T(8,128)(2,1)S(1)} custom-call(bf16[16,3072,128]{2,1,0:T(8,128)(2,1)S(1)} %bitcast.19, bf16[2048,128]{1,0:T(8,128)(2,1)S(1)} %get-tuple-element.13.fitted_ref), custom_call_target="tpu_custom_call" | custom-call | flops 402653184 | bytes 3145728 | tf_op jit(solution)/shard_map/exchange_rows/pallas_call | solution.py:245
  53.5 0.6 collective-permute-start
  54.0 0.0 collective-permute-done.1.refs_0_
  54.0 1.0 %exchange_rows.7 = bf16[4,192,128]{2,1,0:T(8,128)(2,1)S(1)} custom-call(bf16[16,3072,128]{2,1,0:T(8,128)(2,1)S(1)} %bitcast.20, bf16[2048,128]{1,0:T(8,128)(2,1)S(1)} %get-tuple-element.13.fitted_ref, bf16[4,192,128]{2,1,0:T(8,128)(2,1)S(1)} %collective-permute-done.1.refs_0_), custom_call_target="tpu_custom_call" | custom-call | flops 402653184 | bytes 3145728 | tf_op jit(solution)/shard_map/exchange_rows/pallas_call | solution.py:245
  55.0 0.7 %collective-permute-start.2 = (bf16[4,192,128]{2,1,0:T(8,128)(2,1)S(1)}, bf16[4,192,128]{2,1,0:T(8,128)(2,1)S(1)}, u32[]{:S(2)}, u32[]{:S(2)}) collective-permute-start(bf16[4,192,128]{2,1,0:T(8,128)(2,1)S(1)} %exchange_rows.7), channel_id=1, source_target_pairs={{0,2},{1,3},{2,0},{3,1},{4,6},{5,7},{6,4},{7,5},{8,10},{9,11},{10,... | collective-permute-start | bytes 589832 | tf_op jit(solution)/shard_map/ppermute | solution.py:275
  55.7 0.0 collective-permute-done.refs_0_
  55.8 1.0 %exchange_rows.6 = f32[4,192,128]{2,1,0:T(8,128)S(1)} custom-call(bf16[16,3072,128]{2,1,0:T(8,128)(2,1)S(1)} %bitcast.21, bf16[2048,128]{1,0:T(8,128)(2,1)S(1)} %get-tuple-element.13.fitted_ref, bf16[4,192,128]{2,1,0:T(8,128)(2,1)S(1)} %collective-permute-done.refs_0_), custom_call_target="tpu_custom_call" | custom-call | flops 402653184 | bytes 3145728 | tf_op jit(solution)/shard_map/exchange_rows/pallas_call | solution.py:245
  56.7 5.2 %collective-permute-done.2 = bf16[4,192,128]{2,1,0:T(8,128)(2,1)S(1)} collective-permute-done((bf16[4,192,128]{2,1,0:T(8,128)(2,1)S(1)}, bf16[4,192,128]{2,1,0:T(8,128)(2,1)S(1)}, u32[]{:S(2)}, u32[]{:S(2)}) %collective-permute-start.2) | collective-permute-done | bytes 196640 | tf_op jit(solution)/shard_map/ppermute | solution.py:275
  61.9 0.1 fusion.3
  62.0 1.8 %collective-permute-start.3 = (bf16[192,128]{1,0:T(8,128)(2,1)S(1)}, bf16[192,128]{1,0:T(8,128)(2,1)S(1)}, u32[]{:S(2)}, u32[]{:S(2)}) collective-permute-start(bf16[192,128]{1,0:T(8,128)(2,1)S(1)} %get-tuple-element.17), channel_id=1, source_target_pairs={{0,4},{1,5},{2,6},{3,7},{4,0},{5,1},{6,2},{7,3},{8,12},{9,13},{10,... | collective-permute-start | bytes 147464 | tf_op jit(solution)/shard_map/ppermute | solution.py:275
  63.8 2.0 %collective-permute-start.5 = (bf16[192,128]{1,0:T(8,128)(2,1)S(1)}, bf16[192,128]{1,0:T(8,128)(2,1)S(1)}, u32[]{:S(2)}, u32[]{:S(2)}) collective-permute-start(bf16[192,128]{1,0:T(8,128)(2,1)S(1)} %get-tuple-element.18), channel_id=1, source_target_pairs={{0,12},{1,13},{2,14},{3,15},{4,8},{5,9},{6,10},{7,11},{8,4},{9,5},... | collective-permute-start | bytes 147464 | tf_op jit(solution)/shard_map/ppermute | solution.py:275
  65.8 0.0 collective-permute-start.4
  65.8 0.4 collective-permute-done.3
  66.1 3.5 %collective-permute-done.5 = bf16[192,128]{1,0:T(8,128)(2,1)S(1)} collective-permute-done((bf16[192,128]{1,0:T(8,128)(2,1)S(1)}, bf16[192,128]{1,0:T(8,128)(2,1)S(1)}, u32[]{:S(2)}, u32[]{:S(2)}) %collective-permute-start.5) | collective-permute-done | bytes 49184 | tf_op jit(solution)/shard_map/ppermute | solution.py:275
  69.7 1.2 %collective-permute-done.4 = bf16[192,128]{1,0:T(8,128)(2,1)S(1)} collective-permute-done((bf16[192,128]{1,0:T(8,128)(2,1)S(1)}, bf16[192,128]{1,0:T(8,128)(2,1)S(1)}, u32[]{:S(2)}, u32[]{:S(2)}) %collective-permute-start.4) | collective-permute-done | bytes 49184 | tf_op jit(solution)/shard_map/ppermute | solution.py:275
  70.9 0.7 fusion.2
  (1 shorter events, 0.0 us)
Async XLA Ops:
  52.4 1.6 %collective-permute-start.1 = (bf16[4,192,128]{2,1,0:T(8,128)(2,1)S(1)}, bf16[4,192,128]{2,1,0:T(8,128)(2,1)S(1)}, u32[]{:S(2)}, u32[]{:S(2)}) collective-permute-start(bf16[4,192,128]{2,1,0:T(8,128)(2,1)S(1)} %get-tuple-element.14), channel_id=1, source_target_pairs={{0,1},{1,0},{2,3},{3,2},{4,5},{5,4},{6,7},{7,6},{8,9},{9,8},{10,11... | collective-permute-start | bytes 589832 | tf_op jit(solution)/shard_map/ppermute | solution.py:275
  53.5 2.3 %collective-permute-start = (bf16[4,192,128]{2,1,0:T(8,128)(2,1)S(1)}, bf16[4,192,128]{2,1,0:T(8,128)(2,1)S(1)}, u32[]{:S(2)}, u32[]{:S(2)}) collective-permute-start(bf16[4,192,128]{2,1,0:T(8,128)(2,1)S(1)} %exchange_rows.5), channel_id=1, source_target_pairs={{0,1},{1,0},{2,3},{3,2},{4,5},{5,4},{6,7},{7,6},{8,9},{9,8},{10,11... | collective-permute-start | bytes 589832 | tf_op jit(solution)/shard_map/ppermute | solution.py:275
  55.0 6.9 %collective-permute-start.2 = (bf16[4,192,128]{2,1,0:T(8,128)(2,1)S(1)}, bf16[4,192,128]{2,1,0:T(8,128)(2,1)S(1)}, u32[]{:S(2)}, u32[]{:S(2)}) collective-permute-start(bf16[4,192,128]{2,1,0:T(8,128)(2,1)S(1)} %exchange_rows.7), channel_id=1, source_target_pairs={{0,2},{1,3},{2,0},{3,1},{4,6},{5,7},{6,4},{7,5},{8,10},{9,11},{10,... | collective-permute-start | bytes 589832 | tf_op jit(solution)/shard_map/ppermute | solution.py:275
  62.0 4.2 %collective-permute-start.3 = (bf16[192,128]{1,0:T(8,128)(2,1)S(1)}, bf16[192,128]{1,0:T(8,128)(2,1)S(1)}, u32[]{:S(2)}, u32[]{:S(2)}) collective-permute-start(bf16[192,128]{1,0:T(8,128)(2,1)S(1)} %get-tuple-element.17), channel_id=1, source_target_pairs={{0,4},{1,5},{2,6},{3,7},{4,0},{5,1},{6,2},{7,3},{8,12},{9,13},{10,... | collective-permute-start | bytes 147464 | tf_op jit(solution)/shard_map/ppermute | solution.py:275
  63.8 5.9 %collective-permute-start.5 = (bf16[192,128]{1,0:T(8,128)(2,1)S(1)}, bf16[192,128]{1,0:T(8,128)(2,1)S(1)}, u32[]{:S(2)}, u32[]{:S(2)}) collective-permute-start(bf16[192,128]{1,0:T(8,128)(2,1)S(1)} %get-tuple-element.18), channel_id=1, source_target_pairs={{0,12},{1,13},{2,14},{3,15},{4,8},{5,9},{6,10},{7,11},{8,4},{9,5},... | collective-permute-start | bytes 147464 | tf_op jit(solution)/shard_map/ppermute | solution.py:275
  65.8 5.1 %collective-permute-start.4 = (bf16[192,128]{1,0:T(8,128)(2,1)S(1)}, bf16[192,128]{1,0:T(8,128)(2,1)S(1)}, u32[]{:S(2)}, u32[]{:S(2)}) collective-permute-start(bf16[192,128]{1,0:T(8,128)(2,1)S(1)} %get-tuple-element.19), channel_id=1, source_target_pairs={{0,8},{1,9},{2,10},{3,11},{4,12},{5,13},{6,14},{7,15},{8,0},{9,1},... | collective-permute-start | bytes 147464 | tf_op jit(solution)/shard_map/ppermute | solution.py:275

commit v7 on v6

--- a/solution.py
+++ b/solution.py
@@ -204,7 +204,7 @@
         fitted[q * occupied : (q + 1) * occupied, :] = block
 
 
-def exchange_kernel(start, together, more, slab, fitted_ref, *refs):
+def exchange_kernel(start, more, slab, fitted_ref, *refs):
     refs = list(refs)
     more_ref = refs.pop(0) if more else None
     out_ref = refs.pop(0)
@@ -216,12 +216,17 @@
     q_dev = slab.shape[0]
     parts, each, occupied = out_ref.shape
     me = lax.axis_index("aux").astype(jnp.int32)
-
-    @pl.loop(0, parts // together)
-    def _(g):
+    core = (me & 1) ^ (start & 1)
+    first, second = 2 + 2 * core, 4 - 2 * core
+    fixed = me ^ (start & 1) ^ (first if start & 2 else 0)
+    together = 4 if parts % 4 == 0 else 1
+
+    for g in range(parts // together):
         rows = []
-        for u in range(together):
-            owner = (4 * (g * together + u) + start) ^ me
+        for h in range(g * together, (g + 1) * together):
+            owner = fixed ^ (8 * (h % (parts // 2)))
+            if h >= parts // 2:
+                owner = owner ^ second
             rows.append(pl.ds(pl.multiple_of(owner * each, each), each))
         every = jnp.concatenate(
             [jnp.concatenate([slab[q, r, :] for r in rows], axis=0) for q in range(q_dev)], axis=1
@@ -243,7 +248,7 @@
         out.append(jax.ShapeDtypeStruct((q_dev * occupied, occupied), BF16))
     operands = [pltpu.with_memory_space_constraint(slab, pltpu.VMEM), fitted] + ([] if more is None else [more])
     return pl.pallas_call(
-        functools.partial(exchange_kernel, start, 4 if parts % 4 == 0 else 1, more is not None),
+        functools.partial(exchange_kernel, start, more is not None),
         out_shape=out,
         in_specs=[pl.BlockSpec(memory_space=pltpu.VMEM)] * len(operands),
         out_specs=[pl.BlockSpec(memory_space=pltpu.VMEM)] * len(out),
@@ -271,20 +276,23 @@
     if (occupied // owners) % 8:
         fitted = fitted.transpose(1, 0, 2, 3).reshape(q_dev, occupied, occupied)
 
-    def swap(x, bit):
-        return lax.ppermute(x, "aux", [(d, d ^ bit) for d in range(owners)])
+    def swap(x, even, odd):
+        return lax.ppermute(x, "aux", [(d, d ^ (odd if d % 2 else even)) for d in range(owners)])
 
     away, fitted = exchange_rows(slab, fitted, owners, 3, BF16)
-    far = swap(away, 1)
+    far = swap(away, 1, 1)
     (away,) = exchange_rows(slab, fitted, owners, 1, BF16)
-    near = swap(away, 1)
+    near = swap(away, 1, 1)
     (away,) = exchange_rows(slab, fitted, owners, 2, BF16, far)
-    far = swap(away, 2)
+    far = swap(away, 2, 4)
     (near,) = exchange_rows(slab, fitted, owners, 0, F32, near)
-    near = near + far.astype(F32)
+    half = owners // 8
+    away = (near[half:] + far[half:].astype(F32)).astype(BF16)
+    near = near[:half] + far[:half].astype(F32)
+    near = near + swap(away, 4, 2).astype(F32)
     total = near[0]
-    for k in range(1, owners // 4):
-        total = total + swap(near[k].astype(BF16), 4 * k).astype(F32)
+    for k in range(1, half):
+        total = total + swap(near[k].astype(BF16), 8 * k, 8 * k).astype(F32)
     return total
 
 

time: 72.7 us -> 72.3 us (level); the launches traced: 71.6 us -> 72 us
  Pallas kernels: 13.8 us -> 16.4 us
  blocking collectives: 40.9 us -> 39.1 us
    pallas_call x1, Pallas kernels: 9.16 us -> 11.8 us  [half_transform(): pl.pallas_call(functools.partial(half_kernel, owners if split else 0, q_d...]
    all_to_all x1, blocking collectives: 22.5 us -> 20.7 us  [body(): held = trade(pairs).reshape(naux, occupied // owners, occupied)]
    ppermute x6 -> x5, waiting for transfers between devices: 10.3 us -> 10.1 us  [swap(): lax.ppermute(x, 'aux', [(d, d ^ (odd if d % 2 else even)) for d in range(...]
    ppermute x6 -> x5, starting transfers between devices: 5.17 us -> 5.04 us  [swap(): lax.ppermute(x, 'aux', [(d, d ^ (odd if d % 2 else even)) for d in range(...]
  transfers between devices with their start and end apart: 6 -> 5, of which waited for: 4 -> 3; matrix products, arithmetic and copies ran while one was open for 0% -> 0% of each run, Pallas kernels for 4% -> 4%
where the time goes in v7:
time: 72.3 us; the launch traced here: 72 us
  blocking collectives  39.1 us (54%)
  Pallas kernels  16.4 us (23%)
  waiting for transfers between devices  10.1 us (14%)
  starting transfers between devices  5.04 us (7%)
    all_to_all x1, blocking collectives, body(): held = trade(pairs).reshape(naux, occupied // owners, occupied)  20.7 us
    all_to_all x1, blocking collectives, body(): fitted = trade(fitted.reshape(owners, q_dev, occupied // owners, occupied))  18.4 us
    pallas_call x1, Pallas kernels, half_transform(): pl.pallas_call(functools.partial(half_kernel, owners if split else 0, q_d...  11.8 us
    ppermute x5, waiting for transfers between devices, swap(): lax.ppermute(x, 'aux', [(d, d ^ (odd if d % 2 else even)) for d in range(...  10.1 us
    ppermute x5, starting transfers between devices, swap(): lax.ppermute(x, 'aux', [(d, d ^ (odd if d % 2 else even)) for d in range(...  5.04 us
    pallas_call x4, Pallas kernels, exchange_rows(): pl.pallas_call(functools.partial(exchange_kernel, start, more is not None...  3.97 us
  transfers between devices with their start and end apart: 5, of which 3 were waited for; matrix products, arithmetic and copies ran while one was open for 0% of the time, Pallas kernels for 4%

profile of v7, /device:TPU:0, one launch (start us, length us, event | category | flops | bytes accessed | tf_op | source)
XLA Modules:
  0.0 72.0 jit_solution(6112274751876033143)
XLA Ops:
  0.7 11.8 %half_transform_pairs.1 = (bf16[384,128,128]{2,1,0:T(8,128)(2,1)S(1)}, bf16[16,16,8,128]{3,2,1,0:T(8,128)(2,1)S(1)}, bf16[512,256]{1,0:T(8,128)(2,1)S(1)}) custom-call(s32[1]{0:T(128)S(6)} %copy.6.live_ref, s32[3,320]{1,0:T(4,128)} %bitcast.16, bf16[320,128,128]{2,1,0:T(8,128)(2,1)} %blocks_hbm.1, bf16[3072,128]{1,0:T(8,128)(2,1)} %orb_hbm.1, ...), custom_call_target="tpu_custom_call" | custom-call | flops 2952790016 | bytes 23068672 | tf_op jit(solution)/shard_map/half_transform_pairs/pallas_call | solution.py:131
  12.5 20.7 %all_to_all.10 = bf16[16,16,8,128]{3,2,1,0:T(8,128)(2,1)S(1)} all-to-all(bf16[16,16,8,128]{3,2,1,0:T(8,128)(2,1)S(1)} %get-tuple-element.12), channel_id=1, replica_groups=mesh['groups'=2,'aux'=16] {'aux'}, dimensions={0} | all-to-all | bytes 1048576 | tf_op jit(solution)/shard_map/all_to_all | solution.py:273
  33.2 0.6 apply_metric.1
  33.8 18.4 %all_to_all.11.fitted_ref = bf16[16,16,8,128]{3,2,1,0:T(8,128)(2,1)S(1)} all-to-all(bf16[16,16,8,128]{3,2,1,0:T(8,128)(2,1)S(1)} %bitcast.15), channel_id=1, replica_groups=mesh['groups'=2,'aux'=16] {'aux'}, dimensions={0} | all-to-all | bytes 1048576 | tf_op jit(solution)/shard_map/all_to_all | solution.py:275
  52.2 1.0 %exchange_rows.4 = (bf16[4,192,128]{2,1,0:T(8,128)(2,1)S(1)}, bf16[2048,128]{1,0:T(8,128)(2,1)S(1)}) custom-call(bf16[16,3072,128]{2,1,0:T(8,128)(2,1)S(1)} %bitcast.10, bf16[16,16,8,128]{3,2,1,0:T(8,128)(2,1)S(1)} %all_to_all.11.fitted_ref), custom_call_target="tpu_custom_call" | custom-call | flops 402653184 | bytes 3145728 | tf_op jit(solution)/shard_map/exchange_rows/pallas_call | solution.py:250
  53.2 0.1 collective-permute-start.1
  53.3 1.0 %exchange_rows.5 = bf16[4,192,128]{2,1,0:T(8,128)(2,1)S(1)} custom-call(bf16[16,3072,128]{2,1,0:T(8,128)(2,1)S(1)} %bitcast.11, bf16[2048,128]{1,0:T(8,128)(2,1)S(1)} %get-tuple-element.13.fitted_ref), custom_call_target="tpu_custom_call" | custom-call | flops 402653184 | bytes 3145728 | tf_op jit(solution)/shard_map/exchange_rows/pallas_call | solution.py:250
  54.3 0.6 collective-permute-start
  54.8 0.0 collective-permute-done.1.refs_0_
  54.8 1.0 %exchange_rows.7 = bf16[4,192,128]{2,1,0:T(8,128)(2,1)S(1)} custom-call(bf16[16,3072,128]{2,1,0:T(8,128)(2,1)S(1)} %bitcast.12, bf16[2048,128]{1,0:T(8,128)(2,1)S(1)} %get-tuple-element.13.fitted_ref, bf16[4,192,128]{2,1,0:T(8,128)(2,1)S(1)} %collective-permute-done.1.refs_0_), custom_call_target="tpu_custom_call" | custom-call | flops 402653184 | bytes 3145728 | tf_op jit(solution)/shard_map/exchange_rows/pallas_call | solution.py:250
  55.8 0.7 %collective-permute-start.2 = (bf16[4,192,128]{2,1,0:T(8,128)(2,1)S(1)}, bf16[4,192,128]{2,1,0:T(8,128)(2,1)S(1)}, u32[]{:S(2)}, u32[]{:S(2)}) collective-permute-start(bf16[4,192,128]{2,1,0:T(8,128)(2,1)S(1)} %exchange_rows.7), channel_id=1, source_target_pairs={{0,2},{1,5},{2,0},{3,7},{4,6},{5,1},{6,4},{7,3},{8,10},{9,13},{10,... | collective-permute-start | bytes 589832 | tf_op jit(solution)/shard_map/ppermute | solution.py:280
  56.6 0.0 collective-permute-done.refs_0_
  56.6 1.0 %exchange_rows.6 = f32[4,192,128]{2,1,0:T(8,128)S(1)} custom-call(bf16[16,3072,128]{2,1,0:T(8,128)(2,1)S(1)} %bitcast.13, bf16[2048,128]{1,0:T(8,128)(2,1)S(1)} %get-tuple-element.13.fitted_ref, bf16[4,192,128]{2,1,0:T(8,128)(2,1)S(1)} %collective-permute-done.refs_0_), custom_call_target="tpu_custom_call" | custom-call | flops 402653184 | bytes 3145728 | tf_op jit(solution)/shard_map/exchange_rows/pallas_call | solution.py:250
  57.6 4.0 %collective-permute-done.2 = bf16[4,192,128]{2,1,0:T(8,128)(2,1)S(1)} collective-permute-done((bf16[4,192,128]{2,1,0:T(8,128)(2,1)S(1)}, bf16[4,192,128]{2,1,0:T(8,128)(2,1)S(1)}, u32[]{:S(2)}, u32[]{:S(2)}) %collective-permute-start.2) | collective-permute-done | bytes 196640 | tf_op jit(solution)/shard_map/ppermute | solution.py:280
  61.6 1.3 %collective-permute-start.3 = (bf16[2,192,128]{2,1,0:T(8,128)(2,1)S(1)}, bf16[2,192,128]{2,1,0:T(8,128)(2,1)S(1)}, u32[]{:S(2)}, u32[]{:S(2)}) collective-permute-start(bf16[2,192,128]{2,1,0:T(8,128)(2,1)S(1)} %fusion), channel_id=1, source_target_pairs={{0,4},{1,3},{2,6},{3,1},{4,0},{5,7},{6,2},{7,5},{8,12},{9,11},{10,... | collective-permute-start | bytes 294920 | tf_op jit(solution)/shard_map/ppermute | solution.py:280
  62.9 3.4 %collective-permute-done.3 = bf16[2,192,128]{2,1,0:T(8,128)(2,1)S(1)} collective-permute-done((bf16[2,192,128]{2,1,0:T(8,128)(2,1)S(1)}, bf16[2,192,128]{2,1,0:T(8,128)(2,1)S(1)}, u32[]{:S(2)}, u32[]{:S(2)}) %collective-permute-start.3) | collective-permute-done | bytes 98336 | tf_op jit(solution)/shard_map/ppermute | solution.py:280
  66.3 2.3 %collective-permute-start.4 = (bf16[192,128]{1,0:T(8,128)(2,1)S(1)}, bf16[192,128]{1,0:T(8,128)(2,1)S(1)}, u32[]{:S(2)}, u32[]{:S(2)}) collective-permute-start(bf16[192,128]{1,0:T(8,128)(2,1)S(1)} %fusion.3), channel_id=1, source_target_pairs={{0,8},{1,9},{2,10},{3,11},{4,12},{5,13},{6,14},{7,15},{8,0},{9,1},... | collective-permute-start | bytes 147464 | tf_op jit(solution)/shard_map/ppermute | solution.py:280
  68.6 2.7 %collective-permute-done.4 = bf16[192,128]{1,0:T(8,128)(2,1)S(1)} collective-permute-done((bf16[192,128]{1,0:T(8,128)(2,1)S(1)}, bf16[192,128]{1,0:T(8,128)(2,1)S(1)}, u32[]{:S(2)}, u32[]{:S(2)}) %collective-permute-start.4) | collective-permute-done | bytes 49184 | tf_op jit(solution)/shard_map/ppermute | solution.py:280
  71.4 0.7 fusion.2
  (3 shorter events, 0.1 us)
Async XLA Ops:
  53.2 1.6 %collective-permute-start.1 = (bf16[4,192,128]{2,1,0:T(8,128)(2,1)S(1)}, bf16[4,192,128]{2,1,0:T(8,128)(2,1)S(1)}, u32[]{:S(2)}, u32[]{:S(2)}) collective-permute-start(bf16[4,192,128]{2,1,0:T(8,128)(2,1)S(1)} %get-tuple-element.14), channel_id=1, source_target_pairs={{0,1},{1,0},{2,3},{3,2},{4,5},{5,4},{6,7},{7,6},{8,9},{9,8},{10,11... | collective-permute-start | bytes 589832 | tf_op jit(solution)/shard_map/ppermute | solution.py:280
  54.3 2.3 %collective-permute-start = (bf16[4,192,128]{2,1,0:T(8,128)(2,1)S(1)}, bf16[4,192,128]{2,1,0:T(8,128)(2,1)S(1)}, u32[]{:S(2)}, u32[]{:S(2)}) collective-permute-start(bf16[4,192,128]{2,1,0:T(8,128)(2,1)S(1)} %exchange_rows.5), channel_id=1, source_target_pairs={{0,1},{1,0},{2,3},{3,2},{4,5},{5,4},{6,7},{7,6},{8,9},{9,8},{10,11... | collective-permute-start | bytes 589832 | tf_op jit(solution)/shard_map/ppermute | solution.py:280
  55.8 5.7 %collective-permute-start.2 = (bf16[4,192,128]{2,1,0:T(8,128)(2,1)S(1)}, bf16[4,192,128]{2,1,0:T(8,128)(2,1)S(1)}, u32[]{:S(2)}, u32[]{:S(2)}) collective-permute-start(bf16[4,192,128]{2,1,0:T(8,128)(2,1)S(1)} %exchange_rows.7), channel_id=1, source_target_pairs={{0,2},{1,5},{2,0},{3,7},{4,6},{5,1},{6,4},{7,3},{8,10},{9,13},{10,... | collective-permute-start | bytes 589832 | tf_op jit(solution)/shard_map/ppermute | solution.py:280
  61.6 4.7 %collective-permute-start.3 = (bf16[2,192,128]{2,1,0:T(8,128)(2,1)S(1)}, bf16[2,192,128]{2,1,0:T(8,128)(2,1)S(1)}, u32[]{:S(2)}, u32[]{:S(2)}) collective-permute-start(bf16[2,192,128]{2,1,0:T(8,128)(2,1)S(1)} %fusion), channel_id=1, source_target_pairs={{0,4},{1,3},{2,6},{3,1},{4,0},{5,7},{6,2},{7,5},{8,12},{9,11},{10,... | collective-permute-start | bytes 294920 | tf_op jit(solution)/shard_map/ppermute | solution.py:280
  66.3 5.1 %collective-permute-start.4 = (bf16[192,128]{1,0:T(8,128)(2,1)S(1)}, bf16[192,128]{1,0:T(8,128)(2,1)S(1)}, u32[]{:S(2)}, u32[]{:S(2)}) collective-permute-start(bf16[192,128]{1,0:T(8,128)(2,1)S(1)} %fusion.3), channel_id=1, source_target_pairs={{0,8},{1,9},{2,10},{3,11},{4,12},{5,13},{6,14},{7,15},{8,0},{9,1},... | collective-permute-start | bytes 147464 | tf_op jit(solution)/shard_map/ppermute | solution.py:280

commit v8 on v6

--- a/solution.py
+++ b/solution.py
@@ -204,53 +204,50 @@
         fitted[q * occupied : (q + 1) * occupied, :] = block
 
 
-def exchange_kernel(start, together, more, slab, fitted_ref, *refs):
+def exchange_kernel(blocks, gather, more, slab, fitted_ref, *refs):
     refs = list(refs)
     more_ref = refs.pop(0) if more else None
-    out_ref = refs.pop(0)
-    if start == 3:
+    out_refs = [refs.pop(0) for _ in blocks]
+    if gather:
         fitted = refs.pop(0)
         gather_fitted(fitted_ref, fitted)
     else:
         fitted = fitted_ref
     q_dev = slab.shape[0]
-    parts, each, occupied = out_ref.shape
+    each = out_refs[0].shape[1]
     me = lax.axis_index("aux").astype(jnp.int32)
-
-    @pl.loop(0, parts // together)
-    def _(g):
-        rows = []
-        for u in range(together):
-            owner = (4 * (g * together + u) + start) ^ me
-            rows.append(pl.ds(pl.multiple_of(owner * each, each), each))
+    todo = [(k, c, h) for c, part in enumerate(blocks) for h, k in enumerate(part)]
+    together = next(n for n in (4, 3, 2, 1) if len(todo) % n == 0)
+    for g in range(0, len(todo), together):
+        rows = [pl.ds(pl.multiple_of((me ^ k) * each, each), each) for k, _, _ in todo[g : g + together]]
         every = jnp.concatenate(
             [jnp.concatenate([slab[q, r, :] for r in rows], axis=0) for q in range(q_dev)], axis=1
         )
         sums = jnp.dot(every, fitted[...], preferred_element_type=F32)
-        for u in range(together):
+        for u, (_, c, h) in enumerate(todo[g : g + together]):
             part = sums[u * each : (u + 1) * each]
             if more:
-                part = part + more_ref[g * together + u].astype(F32)
-            out_ref[g * together + u] = part.astype(out_ref.dtype)
-
-
-def exchange_rows(slab, fitted, owners, start, dtype, more=None):
+                part = part + more_ref[g + u].astype(F32)
+            out_refs[c][h] = part.astype(out_refs[c].dtype)
+
+
+def exchange_rows(slab, fitted, owners, blocks, dtype, gather=False, more=None):
     q_dev, basis, occupied = slab.shape
     each = basis // owners
-    parts = owners // 4
-    out = [jax.ShapeDtypeStruct((parts, each, occupied), dtype)]
-    if start == 3:
+    count = sum(len(part) for part in blocks)
+    out = [jax.ShapeDtypeStruct((len(part), each, occupied), dtype) for part in blocks]
+    if gather:
         out.append(jax.ShapeDtypeStruct((q_dev * occupied, occupied), BF16))
     operands = [pltpu.with_memory_space_constraint(slab, pltpu.VMEM), fitted] + ([] if more is None else [more])
     return pl.pallas_call(
-        functools.partial(exchange_kernel, start, 4 if parts % 4 == 0 else 1, more is not None),
+        functools.partial(exchange_kernel, blocks, gather, more is not None),
         out_shape=out,
         in_specs=[pl.BlockSpec(memory_space=pltpu.VMEM)] * len(operands),
         out_specs=[pl.BlockSpec(memory_space=pltpu.VMEM)] * len(out),
         compiler_params=pltpu.CompilerParams(vmem_limit_bytes=24 * 2**20),
         cost_estimate=pl.CostEstimate(
-            flops=2 * q_dev * occupied * basis * occupied // 4,
-            bytes_accessed=q_dev * occupied * basis // 2,
+            flops=2 * q_dev * occupied * count * each * occupied,
+            bytes_accessed=2 * q_dev * occupied * count * each,
             transcendentals=0,
         ),
         name="exchange_rows",
@@ -271,20 +268,26 @@
     if (occupied // owners) % 8:
         fitted = fitted.transpose(1, 0, 2, 3).reshape(q_dev, occupied, occupied)
 
-    def swap(x, bit):
-        return lax.ppermute(x, "aux", [(d, d ^ bit) for d in range(owners)])
-
-    away, fitted = exchange_rows(slab, fitted, owners, 3, BF16)
-    far = swap(away, 1)
-    (away,) = exchange_rows(slab, fitted, owners, 1, BF16)
-    near = swap(away, 1)
-    (away,) = exchange_rows(slab, fitted, owners, 2, BF16, far)
-    far = swap(away, 2)
-    (near,) = exchange_rows(slab, fitted, owners, 0, F32, near)
-    near = near + far.astype(F32)
+    def swap(x, bits):
+        return lax.ppermute(x, "aux", [(d, d ^ bits) for d in range(owners)])
+
+    far = range(0, owners, 8)
+    leave = [tuple(x + k for k in far) for x in (2, 4, 6)]
+    stay = [tuple(far)]
+    flip = lambda parts: [tuple(k ^ 1 for k in part) for part in parts]
+    *away, fitted = exchange_rows(slab, fitted, owners, flip([sum(leave, ())]), BF16, gather=True)
+    from_core = swap(away[0], 1)
+    away = exchange_rows(slab, fitted, owners, flip(stay), BF16)
+    to_stay = swap(away[0], 1)
+    away = exchange_rows(slab, fitted, owners, leave, BF16, more=from_core)
+    arrived = [swap(x, bits) for x, bits in zip(away, (2, 4, 6))]
+    (near,) = exchange_rows(slab, fitted, owners, stay, F32, more=to_stay)
+    for x in arrived:
+        near = near + x.astype(F32)
     total = near[0]
-    for k in range(1, owners // 4):
-        total = total + swap(near[k].astype(BF16), 4 * k).astype(F32)
+    for c, k in enumerate(far):
+        if k:
+            total = total + swap(near[c].astype(BF16), k).astype(F32)
     return total
 
 

time: 72.7 us -> 71.4 us (0.982)
  waiting for transfers between devices: 10.3 us -> 7.34 us
  starting transfers between devices: 5.17 us -> 6.46 us
  Pallas kernels: 13.8 us -> 14.6 us
    ppermute x6, waiting for transfers between devices: 10.3 us -> 7.34 us  [swap(): return lax.ppermute(x, 'aux', [(d, d ^ bits) for d in range(owners)])]
    ppermute x6, starting transfers between devices: 5.17 us -> 6.46 us  [swap(): return lax.ppermute(x, 'aux', [(d, d ^ bits) for d in range(owners)])]
    pallas_call x1, Pallas kernels: 9.16 us -> 10.1 us  [half_transform(): pl.pallas_call(functools.partial(half_kernel, owners if split else 0, q_d...]
  transfers between devices with their start and end apart: 6 -> 6, of which waited for: 4 -> 5; matrix products, arithmetic and copies ran while one was open for 0% -> 0% of each run, Pallas kernels for 4% -> 4%
where the time goes in v8:
time: 71.4 us; the launch traced here: 70.7 us
  blocking collectives  40.8 us (57%)
  Pallas kernels  14.6 us (20%)
  waiting for transfers between devices  7.34 us (10%)
  starting transfers between devices  6.46 us (9%)
    all_to_all x1, blocking collectives, body(): held = trade(pairs).reshape(naux, occupied // owners, occupied)  22.5 us
    all_to_all x1, blocking collectives, body(): fitted = trade(fitted.reshape(owners, q_dev, occupied // owners, occupied))  18.4 us
    pallas_call x1, Pallas kernels, half_transform(): pl.pallas_call(functools.partial(half_kernel, owners if split else 0, q_d...  10.1 us
    ppermute x6, waiting for transfers between devices, swap(): return lax.ppermute(x, 'aux', [(d, d ^ bits) for d in range(owners)])  7.34 us
    ppermute x6, starting transfers between devices, swap(): return lax.ppermute(x, 'aux', [(d, d ^ bits) for d in range(owners)])  6.46 us
    pallas_call x4, Pallas kernels, exchange_rows(): pl.pallas_call(functools.partial(exchange_kernel, blocks, gather, more is...  3.97 us
  transfers between devices with their start and end apart: 6, of which 5 were waited for; matrix products, arithmetic and copies ran while one was open for 0% of the time, Pallas kernels for 4%

profile of v8, /device:TPU:0, one launch (start us, length us, event | category | flops | bytes accessed | tf_op | source)
XLA Modules:
  0.0 70.7 jit_solution(16143475815119026370)
XLA Ops:
  0.7 10.1 %half_transform_pairs.1 = (bf16[384,128,128]{2,1,0:T(8,128)(2,1)S(1)}, bf16[16,16,8,128]{3,2,1,0:T(8,128)(2,1)S(1)}, bf16[512,256]{1,0:T(8,128)(2,1)S(1)}) custom-call(s32[1]{0:T(128)S(6)} %copy.6.live_ref, s32[3,320]{1,0:T(4,128)} %bitcast.16, bf16[320,128,128]{2,1,0:T(8,128)(2,1)} %blocks_hbm.1, bf16[3072,128]{1,0:T(8,128)(2,1)} %orb_hbm.1, ...), custom_call_target="tpu_custom_call" | custom-call | flops 2952790016 | bytes 23068672 | tf_op jit(solution)/shard_map/half_transform_pairs/pallas_call | solution.py:131
  10.7 22.5 %all_to_all.10 = bf16[16,16,8,128]{3,2,1,0:T(8,128)(2,1)S(1)} all-to-all(bf16[16,16,8,128]{3,2,1,0:T(8,128)(2,1)S(1)} %get-tuple-element.15), channel_id=1, replica_groups=mesh['groups'=2,'aux'=16] {'aux'}, dimensions={0} | all-to-all | bytes 1048576 | tf_op jit(solution)/shard_map/all_to_all | solution.py:265
  33.2 0.6 apply_metric.1
  33.8 18.4 %all_to_all.11.fitted_ref = bf16[16,16,8,128]{3,2,1,0:T(8,128)(2,1)S(1)} all-to-all(bf16[16,16,8,128]{3,2,1,0:T(8,128)(2,1)S(1)} %bitcast.15), channel_id=1, replica_groups=mesh['groups'=2,'aux'=16] {'aux'}, dimensions={0} | all-to-all | bytes 1048576 | tf_op jit(solution)/shard_map/all_to_all | solution.py:267
  52.2 1.4 %exchange_rows.4 = (bf16[6,192,128]{2,1,0:T(8,128)(2,1)S(1)}, bf16[2048,128]{1,0:T(8,128)(2,1)S(1)}) custom-call(bf16[16,3072,128]{2,1,0:T(8,128)(2,1)S(1)} %bitcast.10, bf16[16,16,8,128]{3,2,1,0:T(8,128)(2,1)S(1)} %all_to_all.11.fitted_ref), custom_call_target="tpu_custom_call" | custom-call | flops 603979776 | bytes 4718592 | tf_op jit(solution)/shard_map/exchange_rows/pallas_call | solution.py:242
  53.6 0.1 collective-permute-start.1
  53.7 0.6 exchange_rows.5
  54.3 0.6 collective-permute-start
  54.8 0.4 collective-permute-done.1.refs_0_
  55.3 1.4 %exchange_rows.7 = (bf16[2,192,128]{2,1,0:T(8,128)(2,1)S(1)}, bf16[2,192,128]{2,1,0:T(8,128)(2,1)S(1)}, bf16[2,192,128]{2,1,0:T(8,128)(2,1)S(1)}) custom-call(bf16[16,3072,128]{2,1,0:T(8,128)(2,1)S(1)} %bitcast.12, bf16[2048,128]{1,0:T(8,128)(2,1)S(1)} %get-tuple-element.16.fitted_ref, bf16[6,192,128]{2,1,0:T(8,128)(2,1)S(1)} %collective-permute-done.1.refs_0_), custom_call_target="tpu_custom_call" | custom-call | flops 603979776 | bytes 4718592 | tf_op jit(solution)/shard_map/exchange_rows/pallas_call | solution.py:242
  56.7 0.9 %collective-permute-start.2 = (bf16[2,192,128]{2,1,0:T(8,128)(2,1)S(1)}, bf16[2,192,128]{2,1,0:T(8,128)(2,1)S(1)}, u32[]{:S(2)}, u32[]{:S(2)}) collective-permute-start(bf16[2,192,128]{2,1,0:T(8,128)(2,1)S(1)} %get-tuple-element.18), channel_id=1, source_target_pairs={{0,2},{1,3},{2,0},{3,1},{4,6},{5,7},{6,4},{7,5},{8,10},{9,11},{10,... | collective-permute-start | bytes 294920 | tf_op jit(solution)/shard_map/ppermute | solution.py:272
  57.5 1.6 %collective-permute-start.3 = (bf16[2,192,128]{2,1,0:T(8,128)(2,1)S(1)}, bf16[2,192,128]{2,1,0:T(8,128)(2,1)S(1)}, u32[]{:S(2)}, u32[]{:S(2)}) collective-permute-start(bf16[2,192,128]{2,1,0:T(8,128)(2,1)S(1)} %get-tuple-element.19), channel_id=1, source_target_pairs={{0,4},{1,5},{2,6},{3,7},{4,0},{5,1},{6,2},{7,3},{8,12},{9,13},{10,... | collective-permute-start | bytes 294920 | tf_op jit(solution)/shard_map/ppermute | solution.py:272
  59.1 1.1 %collective-permute-start.4 = (bf16[2,192,128]{2,1,0:T(8,128)(2,1)S(1)}, bf16[2,192,128]{2,1,0:T(8,128)(2,1)S(1)}, u32[]{:S(2)}, u32[]{:S(2)}) collective-permute-start(bf16[2,192,128]{2,1,0:T(8,128)(2,1)S(1)} %get-tuple-element.20), channel_id=1, source_target_pairs={{0,6},{1,7},{2,4},{3,5},{4,2},{5,3},{6,0},{7,1},{8,14},{9,15},{10,... | collective-permute-start | bytes 294920 | tf_op jit(solution)/shard_map/ppermute | solution.py:272
  60.2 0.0 collective-permute-done.refs_0_
  60.2 0.6 exchange_rows.6
  60.8 0.8 %collective-permute-done.2 = bf16[2,192,128]{2,1,0:T(8,128)(2,1)S(1)} collective-permute-done((bf16[2,192,128]{2,1,0:T(8,128)(2,1)S(1)}, bf16[2,192,128]{2,1,0:T(8,128)(2,1)S(1)}, u32[]{:S(2)}, u32[]{:S(2)}) %collective-permute-start.2) | collective-permute-done | bytes 98336 | tf_op jit(solution)/shard_map/ppermute | solution.py:272
  61.6 1.1 %collective-permute-done.3 = bf16[2,192,128]{2,1,0:T(8,128)(2,1)S(1)} collective-permute-done((bf16[2,192,128]{2,1,0:T(8,128)(2,1)S(1)}, bf16[2,192,128]{2,1,0:T(8,128)(2,1)S(1)}, u32[]{:S(2)}, u32[]{:S(2)}) %collective-permute-start.3) | collective-permute-done | bytes 98336 | tf_op jit(solution)/shard_map/ppermute | solution.py:272
  62.7 2.2 %collective-permute-done.4 = bf16[2,192,128]{2,1,0:T(8,128)(2,1)S(1)} collective-permute-done((bf16[2,192,128]{2,1,0:T(8,128)(2,1)S(1)}, bf16[2,192,128]{2,1,0:T(8,128)(2,1)S(1)}, u32[]{:S(2)}, u32[]{:S(2)}) %collective-permute-start.4) | collective-permute-done | bytes 98336 | tf_op jit(solution)/shard_map/ppermute | solution.py:272
  65.0 2.3 %collective-permute-start.5 = (bf16[192,128]{1,0:T(8,128)(2,1)S(1)}, bf16[192,128]{1,0:T(8,128)(2,1)S(1)}, u32[]{:S(2)}, u32[]{:S(2)}) collective-permute-start(bf16[192,128]{1,0:T(8,128)(2,1)S(1)} %fusion.1), channel_id=1, source_target_pairs={{0,8},{1,9},{2,10},{3,11},{4,12},{5,13},{6,14},{7,15},{8,0},{9,1},... | collective-permute-start | bytes 147464 | tf_op jit(solution)/shard_map/ppermute | solution.py:272
  67.2 2.8 %collective-permute-done.5 = bf16[192,128]{1,0:T(8,128)(2,1)S(1)} collective-permute-done((bf16[192,128]{1,0:T(8,128)(2,1)S(1)}, bf16[192,128]{1,0:T(8,128)(2,1)S(1)}, u32[]{:S(2)}, u32[]{:S(2)}) %collective-permute-start.5) | collective-permute-done | bytes 49184 | tf_op jit(solution)/shard_map/ppermute | solution.py:272
  70.0 0.7 fusion
  (2 shorter events, 0.1 us)
Async XLA Ops:
  53.6 1.6 %collective-permute-start.1 = (bf16[6,192,128]{2,1,0:T(8,128)(2,1)S(1)}, bf16[6,192,128]{2,1,0:T(8,128)(2,1)S(1)}, u32[]{:S(2)}, u32[]{:S(2)}) collective-permute-start(bf16[6,192,128]{2,1,0:T(8,128)(2,1)S(1)} %get-tuple-element.17), channel_id=1, source_target_pairs={{0,1},{1,0},{2,3},{3,2},{4,5},{5,4},{6,7},{7,6},{8,9},{9,8},{10,11... | collective-permute-start | bytes 884744 | tf_op jit(solution)/shard_map/ppermute | solution.py:272
  54.3 6.0 %collective-permute-start = (bf16[2,192,128]{2,1,0:T(8,128)(2,1)S(1)}, bf16[2,192,128]{2,1,0:T(8,128)(2,1)S(1)}, u32[]{:S(2)}, u32[]{:S(2)}) collective-permute-start(bf16[2,192,128]{2,1,0:T(8,128)(2,1)S(1)} %exchange_rows.5), channel_id=1, source_target_pairs={{0,1},{1,0},{2,3},{3,2},{4,5},{5,4},{6,7},{7,6},{8,9},{9,8},{10,11... | collective-permute-start | bytes 294920 | tf_op jit(solution)/shard_map/ppermute | solution.py:272
  56.7 4.9 %collective-permute-start.2 = (bf16[2,192,128]{2,1,0:T(8,128)(2,1)S(1)}, bf16[2,192,128]{2,1,0:T(8,128)(2,1)S(1)}, u32[]{:S(2)}, u32[]{:S(2)}) collective-permute-start(bf16[2,192,128]{2,1,0:T(8,128)(2,1)S(1)} %get-tuple-element.18), channel_id=1, source_target_pairs={{0,2},{1,3},{2,0},{3,1},{4,6},{5,7},{6,4},{7,5},{8,10},{9,11},{10,... | collective-permute-start | bytes 294920 | tf_op jit(solution)/shard_map/ppermute | solution.py:272
  57.5 5.1 %collective-permute-start.3 = (bf16[2,192,128]{2,1,0:T(8,128)(2,1)S(1)}, bf16[2,192,128]{2,1,0:T(8,128)(2,1)S(1)}, u32[]{:S(2)}, u32[]{:S(2)}) collective-permute-start(bf16[2,192,128]{2,1,0:T(8,128)(2,1)S(1)} %get-tuple-element.19), channel_id=1, source_target_pairs={{0,4},{1,5},{2,6},{3,7},{4,0},{5,1},{6,2},{7,3},{8,12},{9,13},{10,... | collective-permute-start | bytes 294920 | tf_op jit(solution)/shard_map/ppermute | solution.py:272
  59.1 5.8 %collective-permute-start.4 = (bf16[2,192,128]{2,1,0:T(8,128)(2,1)S(1)}, bf16[2,192,128]{2,1,0:T(8,128)(2,1)S(1)}, u32[]{:S(2)}, u32[]{:S(2)}) collective-permute-start(bf16[2,192,128]{2,1,0:T(8,128)(2,1)S(1)} %get-tuple-element.20), channel_id=1, source_target_pairs={{0,6},{1,7},{2,4},{3,5},{4,2},{5,3},{6,0},{7,1},{8,14},{9,15},{10,... | collective-permute-start | bytes 294920 | tf_op jit(solution)/shard_map/ppermute | solution.py:272
  65.0 5.1 %collective-permute-start.5 = (bf16[192,128]{1,0:T(8,128)(2,1)S(1)}, bf16[192,128]{1,0:T(8,128)(2,1)S(1)}, u32[]{:S(2)}, u32[]{:S(2)}) collective-permute-start(bf16[192,128]{1,0:T(8,128)(2,1)S(1)} %fusion.1), channel_id=1, source_target_pairs={{0,8},{1,9},{2,10},{3,11},{4,12},{5,13},{6,14},{7,15},{8,0},{9,1},... | collective-permute-start | bytes 147464 | tf_op jit(solution)/shard_map/ppermute | solution.py:272

commit v9 on v8

--- a/solution.py
+++ b/solution.py
@@ -13,32 +13,39 @@
 BF16 = jnp.bfloat16
 
 
-def rank_slots(live, index_ref, rows, meta, nblk, nkeys):
+def rank_slots(live, index_ref, rows, meta, nblk, nkeys, chunks):
     slots = index_ref.shape[1]
     wide = rows.shape[1]
     nothing = float(slots * 256)
+    never = float(chunks * nkeys)
     rows[...] = jnp.full(rows.shape, nkeys, F32)
     key = index_ref[0:1, :] * nblk + index_ref[1:2, :]
     slot = lax.broadcasted_iota(jnp.int32, (1, slots), 1)
     rows[0:1, 0:slots] = jnp.where(slot < live, key, nkeys).astype(F32)
     rows[1:2, 0:slots] = (slot * 256 + index_ref[2:3, :]).astype(F32)
+    rows[2:3, 0:slots] = (slot // CHUNK).astype(F32)
     row = rows[0:1, :]
-    column = rows[...].T[:, 0:1]
+    lives = row < nkeys
+    columns = rows[...].T
+    late = jnp.max(jnp.where(columns[:, 0:1] == row, columns[:, 2:3], 0.0), axis=0, keepdims=True)
+    order = jnp.where(lives, late * nkeys + row, never)
+    column = jnp.broadcast_to(order, (8, wide)).T[:, 0:1]
     before = lax.broadcasted_iota(jnp.int32, (wide, wide), 0) < lax.broadcasted_iota(jnp.int32, (wide, wide), 1)
-    same = (column == row) & before
+    same = (column == order) & before
     rank = jnp.sum(jnp.where(same, 1.0, 0.0), axis=0, keepdims=True)
-    place = jnp.sum(jnp.where(same | (column < row), 1.0, 0.0), axis=0, keepdims=True)
-    lives = row < nkeys
-    last = 2.0 * jnp.max(jnp.where(lives, row, 0.0), axis=1, keepdims=True)
+    place = jnp.sum(jnp.where(same | (column < order), 1.0, 0.0), axis=0, keepdims=True)
+    opens = jnp.where(rank == 0.0, 1.0, 0.0)
+    end = jnp.max(jnp.where(lives, order, 0.0), axis=1, keepdims=True)
+    last = 2.0 * jnp.max(jnp.where(lives & (order == end), row, 0.0), axis=1, keepdims=True)
     rows[1:2, :] = rows[1:2, :] - nothing
     rows[2:3, :] = jnp.where(lives, place, -1.0)
-    rows[3:4, :] = 2.0 * row + jnp.where(rank == 0.0, 1.0, 0.0) - last
+    rows[3:4, :] = 2.0 * row + opens - last
+    rows[4:5, :] = late - (chunks - 1)
     columns = rows[...].T
     found = columns[:, 2:3] == lax.broadcasted_iota(jnp.int32, (1, wide), 1).astype(F32)
-    members = jnp.sum(jnp.where(found, columns[:, 1:2], 0.0), axis=0, keepdims=True)
-    keys = jnp.sum(jnp.where(found, columns[:, 3:4], 0.0), axis=0, keepdims=True)
-    meta[0:1, :] = (members + nothing).astype(jnp.int32)
-    meta[1:2, :] = (keys + last).astype(jnp.int32)
+    for r, (c, rest) in enumerate([(1, nothing), (3, last), (4, float(chunks - 1))]):
+        facts = jnp.sum(jnp.where(found, columns[:, c : c + 1], 0.0), axis=0, keepdims=True) + rest
+        meta[r : r + 1, :] = facts.astype(jnp.int32)
 
 
 def half_kernel(
@@ -67,16 +74,17 @@
             [(index_hbm, index_ref), (orb_hbm, orb_ref), (metric_hbm, metric_ref)]
         )
     ]
-    for copy in small:
-        copy.start()
+    small[0].start()
+    small[1].start()
     for c in range(chunks):
         fetch(c).start()
+    small[2].start()
 
     held[slots] = jnp.zeros((size, size), BF16)
     clear(0, nkeys // 2)
 
     small[0].wait()
-    rank_slots(live_ref[0], index_ref, rows, meta, nblk, nkeys)
+    rank_slots(live_ref[0], index_ref, rows, meta, nblk, nkeys, chunks)
     copy = pltpu.make_async_copy(meta, facts, small_sem.at[0])
     copy.start()
 
@@ -85,6 +93,28 @@
     for b in range(nblk):
         part = slice(b * size, (b + 1) * size)
         orb_t[:, part] = orb_ref[part, :].T
+    copy.wait()
+
+    def arrive(c, nothing):
+        fetch(c).wait()
+        return nothing
+
+    def step(g, carry):
+        arrived, total = carry
+        needed = jnp.maximum(arrived, facts[2, g * UNROLL + UNROLL - 1] + 1)
+        lax.fori_loop(arrived, needed, arrive, 0)
+        for u in range(UNROLL):
+            slot, code = facts[0, g * UNROLL + u], facts[1, g * UNROLL + u]
+            orbs = orb_ref[pl.ds(pl.multiple_of((slot & 255) * size, size), size), :]
+            product = jnp.dot(held[slot >> 8], orbs, preferred_element_type=F32)
+            total = jnp.where((code & 1) == 1, product, total + product)
+            slab[code >> 1] = total.astype(BF16)
+        return needed, total
+
+    bodies = (live_ref[0] + UNROLL - 1) // UNROLL
+    arrived, _ = lax.fori_loop(0, bodies, step, (jnp.int32(0), jnp.zeros((size, occupied), F32)))
+    lax.fori_loop(arrived, chunks, arrive, 0)
+
     small[2].wait()
     metric = metric_ref[...]
     high = metric.astype(BF16)
@@ -92,22 +122,7 @@
     split_ref[0:naux, :] = high
     split_ref[naux : 2 * naux, :] = (metric - high.astype(F32)).astype(BF16)
 
-    copy.wait()
-    for c in range(chunks):
-        fetch(c).wait()
-
-    def step(g, total):
-        for u in range(UNROLL):
-            slot, code = facts[0, g * UNROLL + u], facts[1, g * UNROLL + u]
-            orbs = orb_ref[pl.ds(pl.multiple_of((slot & 255) * size, size), size), :]
-            product = jnp.dot(held[slot >> 8], orbs, preferred_element_type=F32)
-            total = jnp.where((code & 1) == 1, product, total + product)
-            slab[code >> 1] = total.astype(BF16)
-        return total
-
-    lax.fori_loop(0, (live_ref[0] + UNROLL - 1) // UNROLL, step, jnp.zeros((size, occupied), F32))
-
-    @pl.loop(0, q_dev // 2, unroll=4)
+    @pl.loop(0, q_dev // 2, unroll=8)
     def _(t):
         block = jnp.concatenate(
             [slab[pl.ds((2 * t + u) * nblk, nblk)].reshape(nblk * size, occupied) for u in range(2)], axis=1

time: 71.4 us -> 71.4 us (level)
  blocking collectives: 40.8 us -> 42.7 us
  Pallas kernels: 14.6 us -> 13.1 us
    all_to_all x1, blocking collectives: 22.5 us -> 24.4 us  [body(): held = trade(pairs).reshape(naux, occupied // owners, occupied)]
    pallas_call x1, Pallas kernels: 10.1 us -> 8.51 us  [half_transform(): pl.pallas_call(functools.partial(half_kernel, owners if split else 0, q_d...]
where the time goes in v9:
time: 71.4 us; the launch traced here: 71 us
  blocking collectives  42.7 us (60%)
  Pallas kernels  13.1 us (18%)
  waiting for transfers between devices  7.34 us (10%)
  starting transfers between devices  6.46 us (9%)
    all_to_all x1, blocking collectives, body(): held = trade(pairs).reshape(naux, occupied // owners, occupied)  24.4 us
    all_to_all x1, blocking collectives, body(): fitted = trade(fitted.reshape(owners, q_dev, occupied // owners, occupied))  18.4 us
    pallas_call x1, Pallas kernels, half_transform(): pl.pallas_call(functools.partial(half_kernel, owners if split else 0, q_d...  8.51 us
    ppermute x6, waiting for transfers between devices, swap(): return lax.ppermute(x, 'aux', [(d, d ^ bits) for d in range(owners)])  7.34 us
    ppermute x6, starting transfers between devices, swap(): return lax.ppermute(x, 'aux', [(d, d ^ bits) for d in range(owners)])  6.46 us
    pallas_call x4, Pallas kernels, exchange_rows(): pl.pallas_call(functools.partial(exchange_kernel, blocks, gather, more is...  3.97 us
  transfers between devices with their start and end apart: 6, of which 5 were waited for; matrix products, arithmetic and copies ran while one was open for 0% of the time, Pallas kernels for 4%

profile of v9, /device:TPU:0, one launch (start us, length us, event | category | flops | bytes accessed | tf_op | source)
XLA Modules:
  0.0 71.0 jit_solution(6409505321981304353)
XLA Ops:
  0.7 8.5 %half_transform_pairs.1 = (bf16[384,128,128]{2,1,0:T(8,128)(2,1)S(1)}, bf16[16,16,8,128]{3,2,1,0:T(8,128)(2,1)S(1)}, bf16[512,256]{1,0:T(8,128)(2,1)S(1)}) custom-call(s32[1]{0:T(128)S(6)} %copy.6.live_ref, s32[3,320]{1,0:T(4,128)} %bitcast.16, bf16[320,128,128]{2,1,0:T(8,128)(2,1)} %blocks_hbm.1, bf16[3072,128]{1,0:T(8,128)(2,1)} %orb_hbm.1, ...), custom_call_target="tpu_custom_call" | custom-call | flops 2952790016 | bytes 23068672 | tf_op jit(solution)/shard_map/half_transform_pairs/pallas_call | solution.py:146
  9.2 24.4 %all_to_all.10 = bf16[16,16,8,128]{3,2,1,0:T(8,128)(2,1)S(1)} all-to-all(bf16[16,16,8,128]{3,2,1,0:T(8,128)(2,1)S(1)} %get-tuple-element.15), channel_id=1, replica_groups=mesh['groups'=2,'aux'=16] {'aux'}, dimensions={0} | all-to-all | bytes 1048576 | tf_op jit(solution)/shard_map/all_to_all | solution.py:280
  33.5 0.6 apply_metric.1
  34.2 18.4 %all_to_all.11.fitted_ref = bf16[16,16,8,128]{3,2,1,0:T(8,128)(2,1)S(1)} all-to-all(bf16[16,16,8,128]{3,2,1,0:T(8,128)(2,1)S(1)} %bitcast.15), channel_id=1, replica_groups=mesh['groups'=2,'aux'=16] {'aux'}, dimensions={0} | all-to-all | bytes 1048576 | tf_op jit(solution)/shard_map/all_to_all | solution.py:282
  52.5 1.4 %exchange_rows.4 = (bf16[6,192,128]{2,1,0:T(8,128)(2,1)S(1)}, bf16[2048,128]{1,0:T(8,128)(2,1)S(1)}) custom-call(bf16[16,3072,128]{2,1,0:T(8,128)(2,1)S(1)} %bitcast.10, bf16[16,16,8,128]{3,2,1,0:T(8,128)(2,1)S(1)} %all_to_all.11.fitted_ref), custom_call_target="tpu_custom_call" | custom-call | flops 603979776 | bytes 4718592 | tf_op jit(solution)/shard_map/exchange_rows/pallas_call | solution.py:257
  54.0 0.1 collective-permute-start.1
  54.0 0.6 exchange_rows.5
  54.6 0.6 collective-permute-start
  55.2 0.4 collective-permute-done.1.refs_0_
  55.6 1.4 %exchange_rows.7 = (bf16[2,192,128]{2,1,0:T(8,128)(2,1)S(1)}, bf16[2,192,128]{2,1,0:T(8,128)(2,1)S(1)}, bf16[2,192,128]{2,1,0:T(8,128)(2,1)S(1)}) custom-call(bf16[16,3072,128]{2,1,0:T(8,128)(2,1)S(1)} %bitcast.12, bf16[2048,128]{1,0:T(8,128)(2,1)S(1)} %get-tuple-element.16.fitted_ref, bf16[6,192,128]{2,1,0:T(8,128)(2,1)S(1)} %collective-permute-done.1.refs_0_), custom_call_target="tpu_custom_call" | custom-call | flops 603979776 | bytes 4718592 | tf_op jit(solution)/shard_map/exchange_rows/pallas_call | solution.py:257
  57.0 0.9 %collective-permute-start.2 = (bf16[2,192,128]{2,1,0:T(8,128)(2,1)S(1)}, bf16[2,192,128]{2,1,0:T(8,128)(2,1)S(1)}, u32[]{:S(2)}, u32[]{:S(2)}) collective-permute-start(bf16[2,192,128]{2,1,0:T(8,128)(2,1)S(1)} %get-tuple-element.18), channel_id=1, source_target_pairs={{0,2},{1,3},{2,0},{3,1},{4,6},{5,7},{6,4},{7,5},{8,10},{9,11},{10,... | collective-permute-start | bytes 294920 | tf_op jit(solution)/shard_map/ppermute | solution.py:287
  57.9 1.6 %collective-permute-start.3 = (bf16[2,192,128]{2,1,0:T(8,128)(2,1)S(1)}, bf16[2,192,128]{2,1,0:T(8,128)(2,1)S(1)}, u32[]{:S(2)}, u32[]{:S(2)}) collective-permute-start(bf16[2,192,128]{2,1,0:T(8,128)(2,1)S(1)} %get-tuple-element.19), channel_id=1, source_target_pairs={{0,4},{1,5},{2,6},{3,7},{4,0},{5,1},{6,2},{7,3},{8,12},{9,13},{10,... | collective-permute-start | bytes 294920 | tf_op jit(solution)/shard_map/ppermute | solution.py:287
  59.4 1.1 %collective-permute-start.4 = (bf16[2,192,128]{2,1,0:T(8,128)(2,1)S(1)}, bf16[2,192,128]{2,1,0:T(8,128)(2,1)S(1)}, u32[]{:S(2)}, u32[]{:S(2)}) collective-permute-start(bf16[2,192,128]{2,1,0:T(8,128)(2,1)S(1)} %get-tuple-element.20), channel_id=1, source_target_pairs={{0,6},{1,7},{2,4},{3,5},{4,2},{5,3},{6,0},{7,1},{8,14},{9,15},{10,... | collective-permute-start | bytes 294920 | tf_op jit(solution)/shard_map/ppermute | solution.py:287
  60.6 0.0 collective-permute-done.refs_0_
  60.6 0.6 exchange_rows.6
  61.1 0.8 %collective-permute-done.2 = bf16[2,192,128]{2,1,0:T(8,128)(2,1)S(1)} collective-permute-done((bf16[2,192,128]{2,1,0:T(8,128)(2,1)S(1)}, bf16[2,192,128]{2,1,0:T(8,128)(2,1)S(1)}, u32[]{:S(2)}, u32[]{:S(2)}) %collective-permute-start.2) | collective-permute-done | bytes 98336 | tf_op jit(solution)/shard_map/ppermute | solution.py:287
  61.9 1.1 %collective-permute-done.3 = bf16[2,192,128]{2,1,0:T(8,128)(2,1)S(1)} collective-permute-done((bf16[2,192,128]{2,1,0:T(8,128)(2,1)S(1)}, bf16[2,192,128]{2,1,0:T(8,128)(2,1)S(1)}, u32[]{:S(2)}, u32[]{:S(2)}) %collective-permute-start.3) | collective-permute-done | bytes 98336 | tf_op jit(solution)/shard_map/ppermute | solution.py:287
  63.0 2.2 %collective-permute-done.4 = bf16[2,192,128]{2,1,0:T(8,128)(2,1)S(1)} collective-permute-done((bf16[2,192,128]{2,1,0:T(8,128)(2,1)S(1)}, bf16[2,192,128]{2,1,0:T(8,128)(2,1)S(1)}, u32[]{:S(2)}, u32[]{:S(2)}) %collective-permute-start.4) | collective-permute-done | bytes 98336 | tf_op jit(solution)/shard_map/ppermute | solution.py:287
  65.3 2.3 %collective-permute-start.5 = (bf16[192,128]{1,0:T(8,128)(2,1)S(1)}, bf16[192,128]{1,0:T(8,128)(2,1)S(1)}, u32[]{:S(2)}, u32[]{:S(2)}) collective-permute-start(bf16[192,128]{1,0:T(8,128)(2,1)S(1)} %fusion.1), channel_id=1, source_target_pairs={{0,8},{1,9},{2,10},{3,11},{4,12},{5,13},{6,14},{7,15},{8,0},{9,1},... | collective-permute-start | bytes 147464 | tf_op jit(solution)/shard_map/ppermute | solution.py:287
  67.6 2.8 %collective-permute-done.5 = bf16[192,128]{1,0:T(8,128)(2,1)S(1)} collective-permute-done((bf16[192,128]{1,0:T(8,128)(2,1)S(1)}, bf16[192,128]{1,0:T(8,128)(2,1)S(1)}, u32[]{:S(2)}, u32[]{:S(2)}) %collective-permute-start.5) | collective-permute-done | bytes 49184 | tf_op jit(solution)/shard_map/ppermute | solution.py:287
  70.4 0.7 fusion
  (2 shorter events, 0.1 us)
Async XLA Ops:
  54.0 1.6 %collective-permute-start.1 = (bf16[6,192,128]{2,1,0:T(8,128)(2,1)S(1)}, bf16[6,192,128]{2,1,0:T(8,128)(2,1)S(1)}, u32[]{:S(2)}, u32[]{:S(2)}) collective-permute-start(bf16[6,192,128]{2,1,0:T(8,128)(2,1)S(1)} %get-tuple-element.17), channel_id=1, source_target_pairs={{0,1},{1,0},{2,3},{3,2},{4,5},{5,4},{6,7},{7,6},{8,9},{9,8},{10,11... | collective-permute-start | bytes 884744 | tf_op jit(solution)/shard_map/ppermute | solution.py:287
  54.6 6.0 %collective-permute-start = (bf16[2,192,128]{2,1,0:T(8,128)(2,1)S(1)}, bf16[2,192,128]{2,1,0:T(8,128)(2,1)S(1)}, u32[]{:S(2)}, u32[]{:S(2)}) collective-permute-start(bf16[2,192,128]{2,1,0:T(8,128)(2,1)S(1)} %exchange_rows.5), channel_id=1, source_target_pairs={{0,1},{1,0},{2,3},{3,2},{4,5},{5,4},{6,7},{7,6},{8,9},{9,8},{10,11... | collective-permute-start | bytes 294920 | tf_op jit(solution)/shard_map/ppermute | solution.py:287
  57.0 4.9 %collective-permute-start.2 = (bf16[2,192,128]{2,1,0:T(8,128)(2,1)S(1)}, bf16[2,192,128]{2,1,0:T(8,128)(2,1)S(1)}, u32[]{:S(2)}, u32[]{:S(2)}) collective-permute-start(bf16[2,192,128]{2,1,0:T(8,128)(2,1)S(1)} %get-tuple-element.18), channel_id=1, source_target_pairs={{0,2},{1,3},{2,0},{3,1},{4,6},{5,7},{6,4},{7,5},{8,10},{9,11},{10,... | collective-permute-start | bytes 294920 | tf_op jit(solution)/shard_map/ppermute | solution.py:287
  57.9 5.1 %collective-permute-start.3 = (bf16[2,192,128]{2,1,0:T(8,128)(2,1)S(1)}, bf16[2,192,128]{2,1,0:T(8,128)(2,1)S(1)}, u32[]{:S(2)}, u32[]{:S(2)}) collective-permute-start(bf16[2,192,128]{2,1,0:T(8,128)(2,1)S(1)} %get-tuple-element.19), channel_id=1, source_target_pairs={{0,4},{1,5},{2,6},{3,7},{4,0},{5,1},{6,2},{7,3},{8,12},{9,13},{10,... | collective-permute-start | bytes 294920 | tf_op jit(solution)/shard_map/ppermute | solution.py:287
  59.4 5.8 %collective-permute-start.4 = (bf16[2,192,128]{2,1,0:T(8,128)(2,1)S(1)}, bf16[2,192,128]{2,1,0:T(8,128)(2,1)S(1)}, u32[]{:S(2)}, u32[]{:S(2)}) collective-permute-start(bf16[2,192,128]{2,1,0:T(8,128)(2,1)S(1)} %get-tuple-element.20), channel_id=1, source_target_pairs={{0,6},{1,7},{2,4},{3,5},{4,2},{5,3},{6,0},{7,1},{8,14},{9,15},{10,... | collective-permute-start | bytes 294920 | tf_op jit(solution)/shard_map/ppermute | solution.py:287
  65.3 5.1 %collective-permute-start.5 = (bf16[192,128]{1,0:T(8,128)(2,1)S(1)}, bf16[192,128]{1,0:T(8,128)(2,1)S(1)}, u32[]{:S(2)}, u32[]{:S(2)}) collective-permute-start(bf16[192,128]{1,0:T(8,128)(2,1)S(1)} %fusion.1), channel_id=1, source_target_pairs={{0,8},{1,9},{2,10},{3,11},{4,12},{5,13},{6,14},{7,15},{8,0},{9,1},... | collective-permute-start | bytes 147464 | tf_op jit(solution)/shard_map/ppermute | solution.py:287

commit v10 on v9

--- a/solution.py
+++ b/solution.py
@@ -9,6 +9,7 @@
 
 UNROLL = 32
 CHUNK = 32
+TURNS = 3
 F32 = jnp.float32
 BF16 = jnp.bfloat16
 
@@ -90,19 +91,22 @@
 
     clear(nkeys // 2, nkeys)
     small[1].wait()
-    for b in range(nblk):
-        part = slice(b * size, (b + 1) * size)
-        orb_t[:, part] = orb_ref[part, :].T
     copy.wait()
 
     def arrive(c, nothing):
         fetch(c).wait()
         return nothing
+
+    def turn(b):
+        part = pl.ds(pl.multiple_of(b * size, size), size)
+        orb_t[:, part] = orb_ref[part, :].T
 
     def step(g, carry):
         arrived, total = carry
         needed = jnp.maximum(arrived, facts[2, g * UNROLL + UNROLL - 1] + 1)
         lax.fori_loop(arrived, needed, arrive, 0)
+        for u in range(TURNS):
+            turn(jnp.minimum(g * TURNS + u, nblk - 1))
         for u in range(UNROLL):
             slot, code = facts[0, g * UNROLL + u], facts[1, g * UNROLL + u]
             orbs = orb_ref[pl.ds(pl.multiple_of((slot & 255) * size, size), size), :]
@@ -114,6 +118,10 @@
     bodies = (live_ref[0] + UNROLL - 1) // UNROLL
     arrived, _ = lax.fori_loop(0, bodies, step, (jnp.int32(0), jnp.zeros((size, occupied), F32)))
     lax.fori_loop(arrived, chunks, arrive, 0)
+
+    @pl.loop(jnp.minimum(bodies * TURNS, nblk), nblk)
+    def _(b):
+        turn(b)
 
     small[2].wait()
     metric = metric_ref[...]

time: 71.4 us -> 70.7 us (level)
  blocking collectives: 42.7 us -> 40.9 us
  Pallas kernels: 13.1 us -> 14.1 us
    all_to_all x1, blocking collectives: 24.4 us -> 22.5 us  [body(): held = trade(pairs).reshape(naux, occupied // owners, occupied)]
    pallas_call x1, Pallas kernels: 8.51 us -> 9.55 us  [half_transform(): pl.pallas_call(functools.partial(half_kernel, owners if split else 0, q_d...]
where the time goes in v10:
time: 70.7 us; the launch traced here: 70.2 us
  blocking collectives  40.9 us (58%)
  Pallas kernels  14.1 us (20%)
  waiting for transfers between devices  7.34 us (10%)
  starting transfers between devices  6.46 us (9%)
  between operations  0.71 us (1%)
    all_to_all x1, blocking collectives, body(): held = trade(pairs).reshape(naux, occupied // owners, occupied)  22.5 us
    all_to_all x1, blocking collectives, body(): fitted = trade(fitted.reshape(owners, q_dev, occupied // owners, occupied))  18.4 us
    pallas_call x1, Pallas kernels, half_transform(): pl.pallas_call(functools.partial(half_kernel, owners if split else 0, q_d...  9.55 us
    ppermute x6, waiting for transfers between devices, swap(): return lax.ppermute(x, 'aux', [(d, d ^ bits) for d in range(owners)])  7.34 us
    ppermute x6, starting transfers between devices, swap(): return lax.ppermute(x, 'aux', [(d, d ^ bits) for d in range(owners)])  6.46 us
    pallas_call x4, Pallas kernels, exchange_rows(): pl.pallas_call(functools.partial(exchange_kernel, blocks, gather, more is...  3.97 us
  transfers between devices with their start and end apart: 6, of which 5 were waited for; matrix products, arithmetic and copies ran while one was open for 0% of the time, Pallas kernels for 4%

profile of v10, /device:TPU:0, one launch (start us, length us, event | category | flops | bytes accessed | tf_op | source)
XLA Modules:
  0.0 70.2 jit_solution(916952781182545504)
XLA Ops:
  0.7 9.5 %half_transform_pairs.1 = (bf16[384,128,128]{2,1,0:T(8,128)(2,1)S(1)}, bf16[16,16,8,128]{3,2,1,0:T(8,128)(2,1)S(1)}, bf16[512,256]{1,0:T(8,128)(2,1)S(1)}) custom-call(s32[1]{0:T(128)S(6)} %copy.6.live_ref, s32[3,320]{1,0:T(4,128)} %bitcast.16, bf16[320,128,128]{2,1,0:T(8,128)(2,1)} %blocks_hbm.1, bf16[3072,128]{1,0:T(8,128)(2,1)} %orb_hbm.1, ...), custom_call_target="tpu_custom_call" | custom-call | flops 2952790016 | bytes 23068672 | tf_op jit(solution)/shard_map/half_transform_pairs/pallas_call | solution.py:154
  10.2 22.5 %all_to_all.10 = bf16[16,16,8,128]{3,2,1,0:T(8,128)(2,1)S(1)} all-to-all(bf16[16,16,8,128]{3,2,1,0:T(8,128)(2,1)S(1)} %get-tuple-element.15), channel_id=1, replica_groups=mesh['groups'=2,'aux'=16] {'aux'}, dimensions={0} | all-to-all | bytes 1048576 | tf_op jit(solution)/shard_map/all_to_all | solution.py:288
  32.7 0.6 apply_metric.1
  33.3 18.4 %all_to_all.11.fitted_ref = bf16[16,16,8,128]{3,2,1,0:T(8,128)(2,1)S(1)} all-to-all(bf16[16,16,8,128]{3,2,1,0:T(8,128)(2,1)S(1)} %bitcast.15), channel_id=1, replica_groups=mesh['groups'=2,'aux'=16] {'aux'}, dimensions={0} | all-to-all | bytes 1048576 | tf_op jit(solution)/shard_map/all_to_all | solution.py:290
  51.7 1.4 %exchange_rows.4 = (bf16[6,192,128]{2,1,0:T(8,128)(2,1)S(1)}, bf16[2048,128]{1,0:T(8,128)(2,1)S(1)}) custom-call(bf16[16,3072,128]{2,1,0:T(8,128)(2,1)S(1)} %bitcast.10, bf16[16,16,8,128]{3,2,1,0:T(8,128)(2,1)S(1)} %all_to_all.11.fitted_ref), custom_call_target="tpu_custom_call" | custom-call | flops 603979776 | bytes 4718592 | tf_op jit(solution)/shard_map/exchange_rows/pallas_call | solution.py:265
  53.1 0.1 collective-permute-start.1
  53.2 0.6 exchange_rows.5
  53.8 0.6 collective-permute-start
  54.3 0.4 collective-permute-done.1.refs_0_
  54.8 1.4 %exchange_rows.7 = (bf16[2,192,128]{2,1,0:T(8,128)(2,1)S(1)}, bf16[2,192,128]{2,1,0:T(8,128)(2,1)S(1)}, bf16[2,192,128]{2,1,0:T(8,128)(2,1)S(1)}) custom-call(bf16[16,3072,128]{2,1,0:T(8,128)(2,1)S(1)} %bitcast.12, bf16[2048,128]{1,0:T(8,128)(2,1)S(1)} %get-tuple-element.16.fitted_ref, bf16[6,192,128]{2,1,0:T(8,128)(2,1)S(1)} %collective-permute-done.1.refs_0_), custom_call_target="tpu_custom_call" | custom-call | flops 603979776 | bytes 4718592 | tf_op jit(solution)/shard_map/exchange_rows/pallas_call | solution.py:265
  56.2 0.9 %collective-permute-start.2 = (bf16[2,192,128]{2,1,0:T(8,128)(2,1)S(1)}, bf16[2,192,128]{2,1,0:T(8,128)(2,1)S(1)}, u32[]{:S(2)}, u32[]{:S(2)}) collective-permute-start(bf16[2,192,128]{2,1,0:T(8,128)(2,1)S(1)} %get-tuple-element.18), channel_id=1, source_target_pairs={{0,2},{1,3},{2,0},{3,1},{4,6},{5,7},{6,4},{7,5},{8,10},{9,11},{10,... | collective-permute-start | bytes 294920 | tf_op jit(solution)/shard_map/ppermute | solution.py:295
  57.1 1.6 %collective-permute-start.3 = (bf16[2,192,128]{2,1,0:T(8,128)(2,1)S(1)}, bf16[2,192,128]{2,1,0:T(8,128)(2,1)S(1)}, u32[]{:S(2)}, u32[]{:S(2)}) collective-permute-start(bf16[2,192,128]{2,1,0:T(8,128)(2,1)S(1)} %get-tuple-element.19), channel_id=1, source_target_pairs={{0,4},{1,5},{2,6},{3,7},{4,0},{5,1},{6,2},{7,3},{8,12},{9,13},{10,... | collective-permute-start | bytes 294920 | tf_op jit(solution)/shard_map/ppermute | solution.py:295
  58.6 1.1 %collective-permute-start.4 = (bf16[2,192,128]{2,1,0:T(8,128)(2,1)S(1)}, bf16[2,192,128]{2,1,0:T(8,128)(2,1)S(1)}, u32[]{:S(2)}, u32[]{:S(2)}) collective-permute-start(bf16[2,192,128]{2,1,0:T(8,128)(2,1)S(1)} %get-tuple-element.20), channel_id=1, source_target_pairs={{0,6},{1,7},{2,4},{3,5},{4,2},{5,3},{6,0},{7,1},{8,14},{9,15},{10,... | collective-permute-start | bytes 294920 | tf_op jit(solution)/shard_map/ppermute | solution.py:295
  59.7 0.0 collective-permute-done.refs_0_
  59.7 0.6 exchange_rows.6
  60.3 0.8 %collective-permute-done.2 = bf16[2,192,128]{2,1,0:T(8,128)(2,1)S(1)} collective-permute-done((bf16[2,192,128]{2,1,0:T(8,128)(2,1)S(1)}, bf16[2,192,128]{2,1,0:T(8,128)(2,1)S(1)}, u32[]{:S(2)}, u32[]{:S(2)}) %collective-permute-start.2) | collective-permute-done | bytes 98336 | tf_op jit(solution)/shard_map/ppermute | solution.py:295
  61.1 1.1 %collective-permute-done.3 = bf16[2,192,128]{2,1,0:T(8,128)(2,1)S(1)} collective-permute-done((bf16[2,192,128]{2,1,0:T(8,128)(2,1)S(1)}, bf16[2,192,128]{2,1,0:T(8,128)(2,1)S(1)}, u32[]{:S(2)}, u32[]{:S(2)}) %collective-permute-start.3) | collective-permute-done | bytes 98336 | tf_op jit(solution)/shard_map/ppermute | solution.py:295
  62.2 2.2 %collective-permute-done.4 = bf16[2,192,128]{2,1,0:T(8,128)(2,1)S(1)} collective-permute-done((bf16[2,192,128]{2,1,0:T(8,128)(2,1)S(1)}, bf16[2,192,128]{2,1,0:T(8,128)(2,1)S(1)}, u32[]{:S(2)}, u32[]{:S(2)}) %collective-permute-start.4) | collective-permute-done | bytes 98336 | tf_op jit(solution)/shard_map/ppermute | solution.py:295
  64.5 2.3 %collective-permute-start.5 = (bf16[192,128]{1,0:T(8,128)(2,1)S(1)}, bf16[192,128]{1,0:T(8,128)(2,1)S(1)}, u32[]{:S(2)}, u32[]{:S(2)}) collective-permute-start(bf16[192,128]{1,0:T(8,128)(2,1)S(1)} %fusion.1), channel_id=1, source_target_pairs={{0,8},{1,9},{2,10},{3,11},{4,12},{5,13},{6,14},{7,15},{8,0},{9,1},... | collective-permute-start | bytes 147464 | tf_op jit(solution)/shard_map/ppermute | solution.py:295
  66.8 2.8 %collective-permute-done.5 = bf16[192,128]{1,0:T(8,128)(2,1)S(1)} collective-permute-done((bf16[192,128]{1,0:T(8,128)(2,1)S(1)}, bf16[192,128]{1,0:T(8,128)(2,1)S(1)}, u32[]{:S(2)}, u32[]{:S(2)}) %collective-permute-start.5) | collective-permute-done | bytes 49184 | tf_op jit(solution)/shard_map/ppermute | solution.py:295
  69.5 0.7 fusion
  (2 shorter events, 0.1 us)
Async XLA Ops:
  53.1 1.6 %collective-permute-start.1 = (bf16[6,192,128]{2,1,0:T(8,128)(2,1)S(1)}, bf16[6,192,128]{2,1,0:T(8,128)(2,1)S(1)}, u32[]{:S(2)}, u32[]{:S(2)}) collective-permute-start(bf16[6,192,128]{2,1,0:T(8,128)(2,1)S(1)} %get-tuple-element.17), channel_id=1, source_target_pairs={{0,1},{1,0},{2,3},{3,2},{4,5},{5,4},{6,7},{7,6},{8,9},{9,8},{10,11... | collective-permute-start | bytes 884744 | tf_op jit(solution)/shard_map/ppermute | solution.py:295
  53.8 6.0 %collective-permute-start = (bf16[2,192,128]{2,1,0:T(8,128)(2,1)S(1)}, bf16[2,192,128]{2,1,0:T(8,128)(2,1)S(1)}, u32[]{:S(2)}, u32[]{:S(2)}) collective-permute-start(bf16[2,192,128]{2,1,0:T(8,128)(2,1)S(1)} %exchange_rows.5), channel_id=1, source_target_pairs={{0,1},{1,0},{2,3},{3,2},{4,5},{5,4},{6,7},{7,6},{8,9},{9,8},{10,11... | collective-permute-start | bytes 294920 | tf_op jit(solution)/shard_map/ppermute | solution.py:295
  56.2 4.9 %collective-permute-start.2 = (bf16[2,192,128]{2,1,0:T(8,128)(2,1)S(1)}, bf16[2,192,128]{2,1,0:T(8,128)(2,1)S(1)}, u32[]{:S(2)}, u32[]{:S(2)}) collective-permute-start(bf16[2,192,128]{2,1,0:T(8,128)(2,1)S(1)} %get-tuple-element.18), channel_id=1, source_target_pairs={{0,2},{1,3},{2,0},{3,1},{4,6},{5,7},{6,4},{7,5},{8,10},{9,11},{10,... | collective-permute-start | bytes 294920 | tf_op jit(solution)/shard_map/ppermute | solution.py:295
  57.1 5.1 %collective-permute-start.3 = (bf16[2,192,128]{2,1,0:T(8,128)(2,1)S(1)}, bf16[2,192,128]{2,1,0:T(8,128)(2,1)S(1)}, u32[]{:S(2)}, u32[]{:S(2)}) collective-permute-start(bf16[2,192,128]{2,1,0:T(8,128)(2,1)S(1)} %get-tuple-element.19), channel_id=1, source_target_pairs={{0,4},{1,5},{2,6},{3,7},{4,0},{5,1},{6,2},{7,3},{8,12},{9,13},{10,... | collective-permute-start | bytes 294920 | tf_op jit(solution)/shard_map/ppermute | solution.py:295
  58.6 5.8 %collective-permute-start.4 = (bf16[2,192,128]{2,1,0:T(8,128)(2,1)S(1)}, bf16[2,192,128]{2,1,0:T(8,128)(2,1)S(1)}, u32[]{:S(2)}, u32[]{:S(2)}) collective-permute-start(bf16[2,192,128]{2,1,0:T(8,128)(2,1)S(1)} %get-tuple-element.20), channel_id=1, source_target_pairs={{0,6},{1,7},{2,4},{3,5},{4,2},{5,3},{6,0},{7,1},{8,14},{9,15},{10,... | collective-permute-start | bytes 294920 | tf_op jit(solution)/shard_map/ppermute | solution.py:295
  64.5 5.1 %collective-permute-start.5 = (bf16[192,128]{1,0:T(8,128)(2,1)S(1)}, bf16[192,128]{1,0:T(8,128)(2,1)S(1)}, u32[]{:S(2)}, u32[]{:S(2)}) collective-permute-start(bf16[192,128]{1,0:T(8,128)(2,1)S(1)} %fusion.1), channel_id=1, source_target_pairs={{0,8},{1,9},{2,10},{3,11},{4,12},{5,13},{6,14},{7,15},{8,0},{9,1},... | collective-permute-start | bytes 147464 | tf_op jit(solution)/shard_map/ppermute | solution.py:295

commit v11 on v10

--- a/solution.py
+++ b/solution.py
@@ -17,36 +17,54 @@
 def rank_slots(live, index_ref, rows, meta, nblk, nkeys, chunks):
     slots = index_ref.shape[1]
     wide = rows.shape[1]
-    nothing = float(slots * 256)
     never = float(chunks * nkeys)
+    assert slots < 512 and nblk <= 32 and nkeys <= 512 and CHUNK % 8 == 0
     rows[...] = jnp.full(rows.shape, nkeys, F32)
     key = index_ref[0:1, :] * nblk + index_ref[1:2, :]
     slot = lax.broadcasted_iota(jnp.int32, (1, slots), 1)
     rows[0:1, 0:slots] = jnp.where(slot < live, key, nkeys).astype(F32)
-    rows[1:2, 0:slots] = (slot * 256 + index_ref[2:3, :]).astype(F32)
-    rows[2:3, 0:slots] = (slot // CHUNK).astype(F32)
+    rows[1:2, 0:slots] = (slot * 32768 + index_ref[2:3, :] * 1024).astype(F32)
     row = rows[0:1, :]
     lives = row < nkeys
+    tile = (8, wide)
+    zero = jnp.zeros(tile, F32)
+    lane = lax.broadcasted_iota(jnp.int32, tile, 1)
+    ahead = lane - lax.broadcasted_iota(jnp.int32, tile, 0)
+
+    every = jnp.broadcast_to(row, tile)
     columns = rows[...].T
-    late = jnp.max(jnp.where(columns[:, 0:1] == row, columns[:, 2:3], 0.0), axis=0, keepdims=True)
+    late = zero
+    for s in range(0, slots, 8):
+        late = jnp.where(columns[s : s + 8, 0:1] == every, float(s // CHUNK), late)
+    late = jnp.max(late, axis=0, keepdims=True)
     order = jnp.where(lives, late * nkeys + row, never)
-    column = jnp.broadcast_to(order, (8, wide)).T[:, 0:1]
-    before = lax.broadcasted_iota(jnp.int32, (wide, wide), 0) < lax.broadcasted_iota(jnp.int32, (wide, wide), 1)
-    same = (column == order) & before
-    rank = jnp.sum(jnp.where(same, 1.0, 0.0), axis=0, keepdims=True)
-    place = jnp.sum(jnp.where(same | (column < order), 1.0, 0.0), axis=0, keepdims=True)
-    opens = jnp.where(rank == 0.0, 1.0, 0.0)
+
+    every = jnp.broadcast_to(order, tile)
+    columns = every.T
+    rank, place = zero, zero
+    for s in range(0, slots, 8):
+        column = columns[s : s + 8, 0:1]
+        same = (column == every) & (ahead > s)
+        rank = rank + jnp.where(same, 1.0, 0.0)
+        place = place + jnp.where(same | (column < every), 1.0, 0.0)
+    rank = jnp.sum(rank, axis=0, keepdims=True)
+    place = jnp.sum(place, axis=0, keepdims=True)
     end = jnp.max(jnp.where(lives, order, 0.0), axis=1, keepdims=True)
-    last = 2.0 * jnp.max(jnp.where(lives & (order == end), row, 0.0), axis=1, keepdims=True)
-    rows[1:2, :] = rows[1:2, :] - nothing
+    last = jnp.max(jnp.where(lives & (order == end), row, 0.0), axis=1, keepdims=True)
+    nothing = 2.0 * last + slots * 32768.0
+    rows[1:2, :] = rows[1:2, :] + 2.0 * row + jnp.where(rank == 0.0, 1.0, 0.0) - nothing
     rows[2:3, :] = jnp.where(lives, place, -1.0)
-    rows[3:4, :] = 2.0 * row + opens - last
-    rows[4:5, :] = late - (chunks - 1)
+    rows[3:4, :] = late - (chunks - 1)
+
     columns = rows[...].T
-    found = columns[:, 2:3] == lax.broadcasted_iota(jnp.int32, (1, wide), 1).astype(F32)
-    for r, (c, rest) in enumerate([(1, nothing), (3, last), (4, float(chunks - 1))]):
-        facts = jnp.sum(jnp.where(found, columns[:, c : c + 1], 0.0), axis=0, keepdims=True) + rest
-        meta[r : r + 1, :] = facts.astype(jnp.int32)
+    spot = lane.astype(F32)
+    number, need = zero, zero
+    for s in range(0, slots, 8):
+        found = columns[s : s + 8, 2:3] == spot
+        number = number + jnp.where(found, columns[s : s + 8, 1:2], 0.0)
+        need = need + jnp.where(found, columns[s : s + 8, 3:4], 0.0)
+    meta[0:1, :] = (jnp.sum(number, axis=0, keepdims=True) + nothing).astype(jnp.int32)
+    meta[1:2, :] = (jnp.sum(need, axis=0, keepdims=True) + (chunks - 1)).astype(jnp.int32)
 
 
 def half_kernel(
@@ -103,16 +121,23 @@
 
     def step(g, carry):
         arrived, total = carry
-        needed = jnp.maximum(arrived, facts[2, g * UNROLL + UNROLL - 1] + 1)
+        needed = jnp.maximum(arrived, facts[1, g * UNROLL + UNROLL - 1] + 1)
         lax.fori_loop(arrived, needed, arrive, 0)
         for u in range(TURNS):
             turn(jnp.minimum(g * TURNS + u, nblk - 1))
-        for u in range(UNROLL):
-            slot, code = facts[0, g * UNROLL + u], facts[1, g * UNROLL + u]
-            orbs = orb_ref[pl.ds(pl.multiple_of((slot & 255) * size, size), size), :]
-            product = jnp.dot(held[slot >> 8], orbs, preferred_element_type=F32)
-            total = jnp.where((code & 1) == 1, product, total + product)
-            slab[code >> 1] = total.astype(BF16)
+        empty = jnp.zeros((size, occupied), BF16)
+        for u in range(0, UNROLL, 2):
+            pair = [facts[0, g * UNROLL + u + w] for w in range(2)]
+            orbs = [orb_ref[pl.ds(pl.multiple_of(((v >> 10) & 31) * size, size), size), :] for v in pair]
+            diagonal = jnp.concatenate(
+                [jnp.concatenate([orbs[0], empty], axis=1), jnp.concatenate([empty, orbs[1]], axis=1)], axis=0
+            )
+            blocks = jnp.concatenate([held[v >> 15] for v in pair], axis=1)
+            products = jnp.dot(blocks, diagonal, preferred_element_type=F32)
+            for w, v in enumerate(pair):
+                product = products[:, w * occupied : (w + 1) * occupied]
+                total = jnp.where((v & 1) == 1, product, total + product)
+                slab[(v & 1023) >> 1] = total.astype(BF16)
         return needed, total
 
     bodies = (live_ref[0] + UNROLL - 1) // UNROLL

time: 70.7 us -> 71.1 us (level)
  Pallas kernels: 14.1 us -> 16.5 us
  blocking collectives: 40.9 us -> 39 us
    pallas_call x1, Pallas kernels: 9.55 us -> 11.9 us  [half_transform(): pl.pallas_call(functools.partial(half_kernel, owners if split else 0, q_d...]
    all_to_all x1, blocking collectives: 22.5 us -> 20.7 us  [body(): held = trade(pairs).reshape(naux, occupied // owners, occupied)]
where the time goes in v11:
time: 71.1 us; the launch traced here: 70.7 us
  blocking collectives  39 us (55%)
  Pallas kernels  16.5 us (23%)
  waiting for transfers between devices  7.34 us (10%)
  starting transfers between devices  6.46 us (9%)
    all_to_all x1, blocking collectives, body(): held = trade(pairs).reshape(naux, occupied // owners, occupied)  20.7 us
    all_to_all x1, blocking collectives, body(): fitted = trade(fitted.reshape(owners, q_dev, occupied // owners, occupied))  18.4 us
    pallas_call x1, Pallas kernels, half_transform(): pl.pallas_call(functools.partial(half_kernel, owners if split else 0, q_d...  11.9 us
    ppermute x6, waiting for transfers between devices, swap(): return lax.ppermute(x, 'aux', [(d, d ^ bits) for d in range(owners)])  7.34 us
    ppermute x6, starting transfers between devices, swap(): return lax.ppermute(x, 'aux', [(d, d ^ bits) for d in range(owners)])  6.46 us
    pallas_call x4, Pallas kernels, exchange_rows(): pl.pallas_call(functools.partial(exchange_kernel, blocks, gather, more is...  3.97 us
  transfers between devices with their start and end apart: 6, of which 5 were waited for; matrix products, arithmetic and copies ran while one was open for 0% of the time, Pallas kernels for 4%

profile of v11, /device:TPU:0, one launch (start us, length us, event | category | flops | bytes accessed | tf_op | source)
XLA Modules:
  0.0 70.7 jit_solution(6136595778738105094)
XLA Ops:
  0.7 11.9 %half_transform_pairs.1 = (bf16[384,128,128]{2,1,0:T(8,128)(2,1)S(1)}, bf16[16,16,8,128]{3,2,1,0:T(8,128)(2,1)S(1)}, bf16[512,256]{1,0:T(8,128)(2,1)S(1)}) custom-call(s32[1]{0:T(128)S(6)} %copy.6.live_ref, s32[3,320]{1,0:T(4,128)} %bitcast.16, bf16[320,128,128]{2,1,0:T(8,128)(2,1)} %blocks_hbm.1, bf16[3072,128]{1,0:T(8,128)(2,1)} %orb_hbm.1, ...), custom_call_target="tpu_custom_call" | custom-call | flops 2952790016 | bytes 23068672 | tf_op jit(solution)/shard_map/half_transform_pairs/pallas_call | solution.py:179
  12.5 20.7 %all_to_all.10 = bf16[16,16,8,128]{3,2,1,0:T(8,128)(2,1)S(1)} all-to-all(bf16[16,16,8,128]{3,2,1,0:T(8,128)(2,1)S(1)} %get-tuple-element.15), channel_id=1, replica_groups=mesh['groups'=2,'aux'=16] {'aux'}, dimensions={0} | all-to-all | bytes 1048576 | tf_op jit(solution)/shard_map/all_to_all | solution.py:313
  33.2 0.6 apply_metric.1
  33.8 18.4 %all_to_all.11.fitted_ref = bf16[16,16,8,128]{3,2,1,0:T(8,128)(2,1)S(1)} all-to-all(bf16[16,16,8,128]{3,2,1,0:T(8,128)(2,1)S(1)} %bitcast.15), channel_id=1, replica_groups=mesh['groups'=2,'aux'=16] {'aux'}, dimensions={0} | all-to-all | bytes 1048576 | tf_op jit(solution)/shard_map/all_to_all | solution.py:315
  52.2 1.4 %exchange_rows.4 = (bf16[6,192,128]{2,1,0:T(8,128)(2,1)S(1)}, bf16[2048,128]{1,0:T(8,128)(2,1)S(1)}) custom-call(bf16[16,3072,128]{2,1,0:T(8,128)(2,1)S(1)} %bitcast.10, bf16[16,16,8,128]{3,2,1,0:T(8,128)(2,1)S(1)} %all_to_all.11.fitted_ref), custom_call_target="tpu_custom_call" | custom-call | flops 603979776 | bytes 4718592 | tf_op jit(solution)/shard_map/exchange_rows/pallas_call | solution.py:290
  53.6 0.1 collective-permute-start.1
  53.7 0.6 exchange_rows.5
  54.3 0.6 collective-permute-start
  54.8 0.4 collective-permute-done.1.refs_0_
  55.2 1.4 %exchange_rows.7 = (bf16[2,192,128]{2,1,0:T(8,128)(2,1)S(1)}, bf16[2,192,128]{2,1,0:T(8,128)(2,1)S(1)}, bf16[2,192,128]{2,1,0:T(8,128)(2,1)S(1)}) custom-call(bf16[16,3072,128]{2,1,0:T(8,128)(2,1)S(1)} %bitcast.12, bf16[2048,128]{1,0:T(8,128)(2,1)S(1)} %get-tuple-element.16.fitted_ref, bf16[6,192,128]{2,1,0:T(8,128)(2,1)S(1)} %collective-permute-done.1.refs_0_), custom_call_target="tpu_custom_call" | custom-call | flops 603979776 | bytes 4718592 | tf_op jit(solution)/shard_map/exchange_rows/pallas_call | solution.py:290
  56.7 0.9 %collective-permute-start.2 = (bf16[2,192,128]{2,1,0:T(8,128)(2,1)S(1)}, bf16[2,192,128]{2,1,0:T(8,128)(2,1)S(1)}, u32[]{:S(2)}, u32[]{:S(2)}) collective-permute-start(bf16[2,192,128]{2,1,0:T(8,128)(2,1)S(1)} %get-tuple-element.18), channel_id=1, source_target_pairs={{0,2},{1,3},{2,0},{3,1},{4,6},{5,7},{6,4},{7,5},{8,10},{9,11},{10,... | collective-permute-start | bytes 294920 | tf_op jit(solution)/shard_map/ppermute | solution.py:320
  57.5 1.6 %collective-permute-start.3 = (bf16[2,192,128]{2,1,0:T(8,128)(2,1)S(1)}, bf16[2,192,128]{2,1,0:T(8,128)(2,1)S(1)}, u32[]{:S(2)}, u32[]{:S(2)}) collective-permute-start(bf16[2,192,128]{2,1,0:T(8,128)(2,1)S(1)} %get-tuple-element.19), channel_id=1, source_target_pairs={{0,4},{1,5},{2,6},{3,7},{4,0},{5,1},{6,2},{7,3},{8,12},{9,13},{10,... | collective-permute-start | bytes 294920 | tf_op jit(solution)/shard_map/ppermute | solution.py:320
  59.1 1.1 %collective-permute-start.4 = (bf16[2,192,128]{2,1,0:T(8,128)(2,1)S(1)}, bf16[2,192,128]{2,1,0:T(8,128)(2,1)S(1)}, u32[]{:S(2)}, u32[]{:S(2)}) collective-permute-start(bf16[2,192,128]{2,1,0:T(8,128)(2,1)S(1)} %get-tuple-element.20), channel_id=1, source_target_pairs={{0,6},{1,7},{2,4},{3,5},{4,2},{5,3},{6,0},{7,1},{8,14},{9,15},{10,... | collective-permute-start | bytes 294920 | tf_op jit(solution)/shard_map/ppermute | solution.py:320
  60.2 0.0 collective-permute-done.refs_0_
  60.2 0.6 exchange_rows.6
  60.8 0.8 %collective-permute-done.2 = bf16[2,192,128]{2,1,0:T(8,128)(2,1)S(1)} collective-permute-done((bf16[2,192,128]{2,1,0:T(8,128)(2,1)S(1)}, bf16[2,192,128]{2,1,0:T(8,128)(2,1)S(1)}, u32[]{:S(2)}, u32[]{:S(2)}) %collective-permute-start.2) | collective-permute-done | bytes 98336 | tf_op jit(solution)/shard_map/ppermute | solution.py:320
  61.6 1.1 %collective-permute-done.3 = bf16[2,192,128]{2,1,0:T(8,128)(2,1)S(1)} collective-permute-done((bf16[2,192,128]{2,1,0:T(8,128)(2,1)S(1)}, bf16[2,192,128]{2,1,0:T(8,128)(2,1)S(1)}, u32[]{:S(2)}, u32[]{:S(2)}) %collective-permute-start.3) | collective-permute-done | bytes 98336 | tf_op jit(solution)/shard_map/ppermute | solution.py:320
  62.7 2.2 %collective-permute-done.4 = bf16[2,192,128]{2,1,0:T(8,128)(2,1)S(1)} collective-permute-done((bf16[2,192,128]{2,1,0:T(8,128)(2,1)S(1)}, bf16[2,192,128]{2,1,0:T(8,128)(2,1)S(1)}, u32[]{:S(2)}, u32[]{:S(2)}) %collective-permute-start.4) | collective-permute-done | bytes 98336 | tf_op jit(solution)/shard_map/ppermute | solution.py:320
  65.0 2.3 %collective-permute-start.5 = (bf16[192,128]{1,0:T(8,128)(2,1)S(1)}, bf16[192,128]{1,0:T(8,128)(2,1)S(1)}, u32[]{:S(2)}, u32[]{:S(2)}) collective-permute-start(bf16[192,128]{1,0:T(8,128)(2,1)S(1)} %fusion.1), channel_id=1, source_target_pairs={{0,8},{1,9},{2,10},{3,11},{4,12},{5,13},{6,14},{7,15},{8,0},{9,1},... | collective-permute-start | bytes 147464 | tf_op jit(solution)/shard_map/ppermute | solution.py:320
  67.2 2.8 %collective-permute-done.5 = bf16[192,128]{1,0:T(8,128)(2,1)S(1)} collective-permute-done((bf16[192,128]{1,0:T(8,128)(2,1)S(1)}, bf16[192,128]{1,0:T(8,128)(2,1)S(1)}, u32[]{:S(2)}, u32[]{:S(2)}) %collective-permute-start.5) | collective-permute-done | bytes 49184 | tf_op jit(solution)/shard_map/ppermute | solution.py:320
  70.0 0.7 fusion
  (2 shorter events, 0.1 us)
Async XLA Ops:
  53.6 1.6 %collective-permute-start.1 = (bf16[6,192,128]{2,1,0:T(8,128)(2,1)S(1)}, bf16[6,192,128]{2,1,0:T(8,128)(2,1)S(1)}, u32[]{:S(2)}, u32[]{:S(2)}) collective-permute-start(bf16[6,192,128]{2,1,0:T(8,128)(2,1)S(1)} %get-tuple-element.17), channel_id=1, source_target_pairs={{0,1},{1,0},{2,3},{3,2},{4,5},{5,4},{6,7},{7,6},{8,9},{9,8},{10,11... | collective-permute-start | bytes 884744 | tf_op jit(solution)/shard_map/ppermute | solution.py:320
  54.3 6.0 %collective-permute-start = (bf16[2,192,128]{2,1,0:T(8,128)(2,1)S(1)}, bf16[2,192,128]{2,1,0:T(8,128)(2,1)S(1)}, u32[]{:S(2)}, u32[]{:S(2)}) collective-permute-start(bf16[2,192,128]{2,1,0:T(8,128)(2,1)S(1)} %exchange_rows.5), channel_id=1, source_target_pairs={{0,1},{1,0},{2,3},{3,2},{4,5},{5,4},{6,7},{7,6},{8,9},{9,8},{10,11... | collective-permute-start | bytes 294920 | tf_op jit(solution)/shard_map/ppermute | solution.py:320
  56.7 4.9 %collective-permute-start.2 = (bf16[2,192,128]{2,1,0:T(8,128)(2,1)S(1)}, bf16[2,192,128]{2,1,0:T(8,128)(2,1)S(1)}, u32[]{:S(2)}, u32[]{:S(2)}) collective-permute-start(bf16[2,192,128]{2,1,0:T(8,128)(2,1)S(1)} %get-tuple-element.18), channel_id=1, source_target_pairs={{0,2},{1,3},{2,0},{3,1},{4,6},{5,7},{6,4},{7,5},{8,10},{9,11},{10,... | collective-permute-start | bytes 294920 | tf_op jit(solution)/shard_map/ppermute | solution.py:320
  57.5 5.1 %collective-permute-start.3 = (bf16[2,192,128]{2,1,0:T(8,128)(2,1)S(1)}, bf16[2,192,128]{2,1,0:T(8,128)(2,1)S(1)}, u32[]{:S(2)}, u32[]{:S(2)}) collective-permute-start(bf16[2,192,128]{2,1,0:T(8,128)(2,1)S(1)} %get-tuple-element.19), channel_id=1, source_target_pairs={{0,4},{1,5},{2,6},{3,7},{4,0},{5,1},{6,2},{7,3},{8,12},{9,13},{10,... | collective-permute-start | bytes 294920 | tf_op jit(solution)/shard_map/ppermute | solution.py:320
  59.1 5.8 %collective-permute-start.4 = (bf16[2,192,128]{2,1,0:T(8,128)(2,1)S(1)}, bf16[2,192,128]{2,1,0:T(8,128)(2,1)S(1)}, u32[]{:S(2)}, u32[]{:S(2)}) collective-permute-start(bf16[2,192,128]{2,1,0:T(8,128)(2,1)S(1)} %get-tuple-element.20), channel_id=1, source_target_pairs={{0,6},{1,7},{2,4},{3,5},{4,2},{5,3},{6,0},{7,1},{8,14},{9,15},{10,... | collective-permute-start | bytes 294920 | tf_op jit(solution)/shard_map/ppermute | solution.py:320
  65.0 5.1 %collective-permute-start.5 = (bf16[192,128]{1,0:T(8,128)(2,1)S(1)}, bf16[192,128]{1,0:T(8,128)(2,1)S(1)}, u32[]{:S(2)}, u32[]{:S(2)}) collective-permute-start(bf16[192,128]{1,0:T(8,128)(2,1)S(1)} %fusion.1), channel_id=1, source_target_pairs={{0,8},{1,9},{2,10},{3,11},{4,12},{5,13},{6,14},{7,15},{8,0},{9,1},... | collective-permute-start | bytes 147464 | tf_op jit(solution)/shard_map/ppermute | solution.py:320

commit v12 on v11

--- a/solution.py
+++ b/solution.py
@@ -10,11 +10,12 @@
 UNROLL = 32
 CHUNK = 32
 TURNS = 3
+FLIGHT = 4
 F32 = jnp.float32
 BF16 = jnp.bfloat16
 
 
-def rank_slots(live, index_ref, rows, meta, nblk, nkeys, chunks):
+def rank_slots(live, index_ref, rows, meta, nblk, nkeys, chunks, pump):
     slots = index_ref.shape[1]
     wide = rows.shape[1]
     never = float(chunks * nkeys)
@@ -37,6 +38,7 @@
     for s in range(0, slots, 8):
         late = jnp.where(columns[s : s + 8, 0:1] == every, float(s // CHUNK), late)
     late = jnp.max(late, axis=0, keepdims=True)
+    pump()
     order = jnp.where(lives, late * nkeys + row, never)
 
     every = jnp.broadcast_to(order, tile)
@@ -47,6 +49,7 @@
         same = (column == every) & (ahead > s)
         rank = rank + jnp.where(same, 1.0, 0.0)
         place = place + jnp.where(same | (column < every), 1.0, 0.0)
+    pump()
     rank = jnp.sum(rank, axis=0, keepdims=True)
     place = jnp.sum(place, axis=0, keepdims=True)
     end = jnp.max(jnp.where(lives, order, 0.0), axis=1, keepdims=True)
@@ -95,19 +98,33 @@
     ]
     small[0].start()
     small[1].start()
-    for c in range(chunks):
+    for c in range(min(FLIGHT, chunks)):
         fetch(c).start()
-    small[2].start()
+    came = [0]
+
+    def pump():
+        if came[0] + FLIGHT < chunks:
+            fetch(came[0]).wait()
+            fetch(came[0] + FLIGHT).start()
+            came[0] += 1
+
 
     held[slots] = jnp.zeros((size, size), BF16)
     clear(0, nkeys // 2)
 
     small[0].wait()
-    rank_slots(live_ref[0], index_ref, rows, meta, nblk, nkeys, chunks)
+    pump()
+    rank_slots(live_ref[0], index_ref, rows, meta, nblk, nkeys, chunks, pump)
+    pump()
     copy = pltpu.make_async_copy(meta, facts, small_sem.at[0])
     copy.start()
 
-    clear(nkeys // 2, nkeys)
+    clear(nkeys // 2, 3 * nkeys // 4)
+    pump()
+    clear(3 * nkeys // 4, nkeys)
+    while came[0] + FLIGHT < chunks:
+        pump()
+    small[2].start()
     small[1].wait()
     copy.wait()
 
@@ -141,7 +158,7 @@
         return needed, total
 
     bodies = (live_ref[0] + UNROLL - 1) // UNROLL
-    arrived, _ = lax.fori_loop(0, bodies, step, (jnp.int32(0), jnp.zeros((size, occupied), F32)))
+    arrived, _ = lax.fori_loop(0, bodies, step, (jnp.int32(came[0]), jnp.zeros((size, occupied), F32)))
     lax.fori_loop(arrived, chunks, arrive, 0)
 
     @pl.loop(jnp.minimum(bodies * TURNS, nblk), nblk)

time: 71.1 us -> 69.3 us (0.975)
  Pallas kernels: 16.5 us -> 13.6 us
  blocking collectives: 39 us -> 40 us
    pallas_call x1, Pallas kernels: 11.9 us -> 8.99 us  [half_transform(): pl.pallas_call(functools.partial(half_kernel, owners if split else 0, q_d...]
    all_to_all x1, blocking collectives: 20.7 us -> 21.7 us  [body(): held = trade(pairs).reshape(naux, occupied // owners, occupied)]
where the time goes in v12:
time: 69.3 us; the launch traced here: 68.8 us
  blocking collectives  40 us (58%)
  Pallas kernels  13.6 us (20%)
  waiting for transfers between devices  7.34 us (11%)
  starting transfers between devices  6.46 us (9%)
  between operations  0.71 us (1%)
    all_to_all x1, blocking collectives, body(): held = trade(pairs).reshape(naux, occupied // owners, occupied)  21.7 us
    all_to_all x1, blocking collectives, body(): fitted = trade(fitted.reshape(owners, q_dev, occupied // owners, occupied))  18.4 us
    pallas_call x1, Pallas kernels, half_transform(): pl.pallas_call(functools.partial(half_kernel, owners if split else 0, q_d...  8.99 us
    ppermute x6, waiting for transfers between devices, swap(): return lax.ppermute(x, 'aux', [(d, d ^ bits) for d in range(owners)])  7.34 us
    ppermute x6, starting transfers between devices, swap(): return lax.ppermute(x, 'aux', [(d, d ^ bits) for d in range(owners)])  6.46 us
    pallas_call x4, Pallas kernels, exchange_rows(): pl.pallas_call(functools.partial(exchange_kernel, blocks, gather, more is...  3.97 us
  transfers between devices with their start and end apart: 6, of which 5 were waited for; matrix products, arithmetic and copies ran while one was open for 0% of the time, Pallas kernels for 4%

profile of v12, /device:TPU:0, one launch (start us, length us, event | category | flops | bytes accessed | tf_op | source)
XLA Modules:
  0.0 68.8 jit_solution(3822810829894508741)
XLA Ops:
  0.7 9.0 %half_transform_pairs.1 = (bf16[384,128,128]{2,1,0:T(8,128)(2,1)S(1)}, bf16[16,16,8,128]{3,2,1,0:T(8,128)(2,1)S(1)}, bf16[512,256]{1,0:T(8,128)(2,1)S(1)}) custom-call(s32[1]{0:T(128)S(6)} %copy.6.live_ref, s32[3,320]{1,0:T(4,128)} %bitcast.16, bf16[320,128,128]{2,1,0:T(8,128)(2,1)} %blocks_hbm.1, bf16[3072,128]{1,0:T(8,128)(2,1)} %orb_hbm.1, ...), custom_call_target="tpu_custom_call" | custom-call | flops 2952790016 | bytes 23068672 | tf_op jit(solution)/shard_map/half_transform_pairs/pallas_call | solution.py:196
  9.6 21.7 %all_to_all.10 = bf16[16,16,8,128]{3,2,1,0:T(8,128)(2,1)S(1)} all-to-all(bf16[16,16,8,128]{3,2,1,0:T(8,128)(2,1)S(1)} %get-tuple-element.15), channel_id=1, replica_groups=mesh['groups'=2,'aux'=16] {'aux'}, dimensions={0} | all-to-all | bytes 1048576 | tf_op jit(solution)/shard_map/all_to_all | solution.py:330
  31.3 0.6 apply_metric.1
  31.9 18.4 %all_to_all.11.fitted_ref = bf16[16,16,8,128]{3,2,1,0:T(8,128)(2,1)S(1)} all-to-all(bf16[16,16,8,128]{3,2,1,0:T(8,128)(2,1)S(1)} %bitcast.15), channel_id=1, replica_groups=mesh['groups'=2,'aux'=16] {'aux'}, dimensions={0} | all-to-all | bytes 1048576 | tf_op jit(solution)/shard_map/all_to_all | solution.py:332
  50.3 1.4 %exchange_rows.4 = (bf16[6,192,128]{2,1,0:T(8,128)(2,1)S(1)}, bf16[2048,128]{1,0:T(8,128)(2,1)S(1)}) custom-call(bf16[16,3072,128]{2,1,0:T(8,128)(2,1)S(1)} %bitcast.10, bf16[16,16,8,128]{3,2,1,0:T(8,128)(2,1)S(1)} %all_to_all.11.fitted_ref), custom_call_target="tpu_custom_call" | custom-call | flops 603979776 | bytes 4718592 | tf_op jit(solution)/shard_map/exchange_rows/pallas_call | solution.py:307
  51.7 0.1 collective-permute-start.1
  51.8 0.6 exchange_rows.5
  52.4 0.6 collective-permute-start
  53.0 0.4 collective-permute-done.1.refs_0_
  53.4 1.4 %exchange_rows.7 = (bf16[2,192,128]{2,1,0:T(8,128)(2,1)S(1)}, bf16[2,192,128]{2,1,0:T(8,128)(2,1)S(1)}, bf16[2,192,128]{2,1,0:T(8,128)(2,1)S(1)}) custom-call(bf16[16,3072,128]{2,1,0:T(8,128)(2,1)S(1)} %bitcast.12, bf16[2048,128]{1,0:T(8,128)(2,1)S(1)} %get-tuple-element.16.fitted_ref, bf16[6,192,128]{2,1,0:T(8,128)(2,1)S(1)} %collective-permute-done.1.refs_0_), custom_call_target="tpu_custom_call" | custom-call | flops 603979776 | bytes 4718592 | tf_op jit(solution)/shard_map/exchange_rows/pallas_call | solution.py:307
  54.8 0.9 %collective-permute-start.2 = (bf16[2,192,128]{2,1,0:T(8,128)(2,1)S(1)}, bf16[2,192,128]{2,1,0:T(8,128)(2,1)S(1)}, u32[]{:S(2)}, u32[]{:S(2)}) collective-permute-start(bf16[2,192,128]{2,1,0:T(8,128)(2,1)S(1)} %get-tuple-element.18), channel_id=1, source_target_pairs={{0,2},{1,3},{2,0},{3,1},{4,6},{5,7},{6,4},{7,5},{8,10},{9,11},{10,... | collective-permute-start | bytes 294920 | tf_op jit(solution)/shard_map/ppermute | solution.py:337
  55.7 1.6 %collective-permute-start.3 = (bf16[2,192,128]{2,1,0:T(8,128)(2,1)S(1)}, bf16[2,192,128]{2,1,0:T(8,128)(2,1)S(1)}, u32[]{:S(2)}, u32[]{:S(2)}) collective-permute-start(bf16[2,192,128]{2,1,0:T(8,128)(2,1)S(1)} %get-tuple-element.19), channel_id=1, source_target_pairs={{0,4},{1,5},{2,6},{3,7},{4,0},{5,1},{6,2},{7,3},{8,12},{9,13},{10,... | collective-permute-start | bytes 294920 | tf_op jit(solution)/shard_map/ppermute | solution.py:337
  57.2 1.1 %collective-permute-start.4 = (bf16[2,192,128]{2,1,0:T(8,128)(2,1)S(1)}, bf16[2,192,128]{2,1,0:T(8,128)(2,1)S(1)}, u32[]{:S(2)}, u32[]{:S(2)}) collective-permute-start(bf16[2,192,128]{2,1,0:T(8,128)(2,1)S(1)} %get-tuple-element.20), channel_id=1, source_target_pairs={{0,6},{1,7},{2,4},{3,5},{4,2},{5,3},{6,0},{7,1},{8,14},{9,15},{10,... | collective-permute-start | bytes 294920 | tf_op jit(solution)/shard_map/ppermute | solution.py:337
  58.3 0.0 collective-permute-done.refs_0_
  58.3 0.6 exchange_rows.6
  58.9 0.8 %collective-permute-done.2 = bf16[2,192,128]{2,1,0:T(8,128)(2,1)S(1)} collective-permute-done((bf16[2,192,128]{2,1,0:T(8,128)(2,1)S(1)}, bf16[2,192,128]{2,1,0:T(8,128)(2,1)S(1)}, u32[]{:S(2)}, u32[]{:S(2)}) %collective-permute-start.2) | collective-permute-done | bytes 98336 | tf_op jit(solution)/shard_map/ppermute | solution.py:337
  59.7 1.1 %collective-permute-done.3 = bf16[2,192,128]{2,1,0:T(8,128)(2,1)S(1)} collective-permute-done((bf16[2,192,128]{2,1,0:T(8,128)(2,1)S(1)}, bf16[2,192,128]{2,1,0:T(8,128)(2,1)S(1)}, u32[]{:S(2)}, u32[]{:S(2)}) %collective-permute-start.3) | collective-permute-done | bytes 98336 | tf_op jit(solution)/shard_map/ppermute | solution.py:337
  60.8 2.2 %collective-permute-done.4 = bf16[2,192,128]{2,1,0:T(8,128)(2,1)S(1)} collective-permute-done((bf16[2,192,128]{2,1,0:T(8,128)(2,1)S(1)}, bf16[2,192,128]{2,1,0:T(8,128)(2,1)S(1)}, u32[]{:S(2)}, u32[]{:S(2)}) %collective-permute-start.4) | collective-permute-done | bytes 98336 | tf_op jit(solution)/shard_map/ppermute | solution.py:337
  63.1 2.3 %collective-permute-start.5 = (bf16[192,128]{1,0:T(8,128)(2,1)S(1)}, bf16[192,128]{1,0:T(8,128)(2,1)S(1)}, u32[]{:S(2)}, u32[]{:S(2)}) collective-permute-start(bf16[192,128]{1,0:T(8,128)(2,1)S(1)} %fusion.1), channel_id=1, source_target_pairs={{0,8},{1,9},{2,10},{3,11},{4,12},{5,13},{6,14},{7,15},{8,0},{9,1},... | collective-permute-start | bytes 147464 | tf_op jit(solution)/shard_map/ppermute | solution.py:337
  65.4 2.8 %collective-permute-done.5 = bf16[192,128]{1,0:T(8,128)(2,1)S(1)} collective-permute-done((bf16[192,128]{1,0:T(8,128)(2,1)S(1)}, bf16[192,128]{1,0:T(8,128)(2,1)S(1)}, u32[]{:S(2)}, u32[]{:S(2)}) %collective-permute-start.5) | collective-permute-done | bytes 49184 | tf_op jit(solution)/shard_map/ppermute | solution.py:337
  68.2 0.7 fusion
  (2 shorter events, 0.1 us)
Async XLA Ops:
  51.7 1.6 %collective-permute-start.1 = (bf16[6,192,128]{2,1,0:T(8,128)(2,1)S(1)}, bf16[6,192,128]{2,1,0:T(8,128)(2,1)S(1)}, u32[]{:S(2)}, u32[]{:S(2)}) collective-permute-start(bf16[6,192,128]{2,1,0:T(8,128)(2,1)S(1)} %get-tuple-element.17), channel_id=1, source_target_pairs={{0,1},{1,0},{2,3},{3,2},{4,5},{5,4},{6,7},{7,6},{8,9},{9,8},{10,11... | collective-permute-start | bytes 884744 | tf_op jit(solution)/shard_map/ppermute | solution.py:337
  52.4 6.0 %collective-permute-start = (bf16[2,192,128]{2,1,0:T(8,128)(2,1)S(1)}, bf16[2,192,128]{2,1,0:T(8,128)(2,1)S(1)}, u32[]{:S(2)}, u32[]{:S(2)}) collective-permute-start(bf16[2,192,128]{2,1,0:T(8,128)(2,1)S(1)} %exchange_rows.5), channel_id=1, source_target_pairs={{0,1},{1,0},{2,3},{3,2},{4,5},{5,4},{6,7},{7,6},{8,9},{9,8},{10,11... | collective-permute-start | bytes 294920 | tf_op jit(solution)/shard_map/ppermute | solution.py:337
  54.8 4.9 %collective-permute-start.2 = (bf16[2,192,128]{2,1,0:T(8,128)(2,1)S(1)}, bf16[2,192,128]{2,1,0:T(8,128)(2,1)S(1)}, u32[]{:S(2)}, u32[]{:S(2)}) collective-permute-start(bf16[2,192,128]{2,1,0:T(8,128)(2,1)S(1)} %get-tuple-element.18), channel_id=1, source_target_pairs={{0,2},{1,3},{2,0},{3,1},{4,6},{5,7},{6,4},{7,5},{8,10},{9,11},{10,... | collective-permute-start | bytes 294920 | tf_op jit(solution)/shard_map/ppermute | solution.py:337
  55.7 5.1 %collective-permute-start.3 = (bf16[2,192,128]{2,1,0:T(8,128)(2,1)S(1)}, bf16[2,192,128]{2,1,0:T(8,128)(2,1)S(1)}, u32[]{:S(2)}, u32[]{:S(2)}) collective-permute-start(bf16[2,192,128]{2,1,0:T(8,128)(2,1)S(1)} %get-tuple-element.19), channel_id=1, source_target_pairs={{0,4},{1,5},{2,6},{3,7},{4,0},{5,1},{6,2},{7,3},{8,12},{9,13},{10,... | collective-permute-start | bytes 294920 | tf_op jit(solution)/shard_map/ppermute | solution.py:337
  57.2 5.8 %collective-permute-start.4 = (bf16[2,192,128]{2,1,0:T(8,128)(2,1)S(1)}, bf16[2,192,128]{2,1,0:T(8,128)(2,1)S(1)}, u32[]{:S(2)}, u32[]{:S(2)}) collective-permute-start(bf16[2,192,128]{2,1,0:T(8,128)(2,1)S(1)} %get-tuple-element.20), channel_id=1, source_target_pairs={{0,6},{1,7},{2,4},{3,5},{4,2},{5,3},{6,0},{7,1},{8,14},{9,15},{10,... | collective-permute-start | bytes 294920 | tf_op jit(solution)/shard_map/ppermute | solution.py:337
  63.1 5.1 %collective-permute-start.5 = (bf16[192,128]{1,0:T(8,128)(2,1)S(1)}, bf16[192,128]{1,0:T(8,128)(2,1)S(1)}, u32[]{:S(2)}, u32[]{:S(2)}) collective-permute-start(bf16[192,128]{1,0:T(8,128)(2,1)S(1)} %fusion.1), channel_id=1, source_target_pairs={{0,8},{1,9},{2,10},{3,11},{4,12},{5,13},{6,14},{7,15},{8,0},{9,1},... | collective-permute-start | bytes 147464 | tf_op jit(solution)/shard_map/ppermute | solution.py:337

commit v13 on v12

--- a/solution.py
+++ b/solution.py
@@ -7,9 +7,9 @@
 from jax.experimental.pallas import tpu as pltpu
 from jax.sharding import PartitionSpec as P
 
-UNROLL = 32
+UNROLL = 64
 CHUNK = 32
-TURNS = 3
+TURNS = 5
 FLIGHT = 4
 F32 = jnp.float32
 BF16 = jnp.bfloat16

time: 69.3 us -> 69.3 us (level); the launches traced: 68.8 us -> 69.5 us
  no operation moved by 1% of the time
where the time goes in v13:
time: 69.3 us; the launch traced here: 69.5 us
  blocking collectives  40.6 us (59%)
  Pallas kernels  13.7 us (20%)
  waiting for transfers between devices  7.34 us (11%)
  starting transfers between devices  6.46 us (9%)
  between operations  0.71 us (1%)
    all_to_all x1, blocking collectives, body(): held = trade(pairs).reshape(naux, occupied // owners, occupied)  22.2 us
    all_to_all x1, blocking collectives, body(): fitted = trade(fitted.reshape(owners, q_dev, occupied // owners, occupied))  18.4 us
    pallas_call x1, Pallas kernels, half_transform(): pl.pallas_call(functools.partial(half_kernel, owners if split else 0, q_d...  9.17 us
    ppermute x6, waiting for transfers between devices, swap(): return lax.ppermute(x, 'aux', [(d, d ^ bits) for d in range(owners)])  7.34 us
    ppermute x6, starting transfers between devices, swap(): return lax.ppermute(x, 'aux', [(d, d ^ bits) for d in range(owners)])  6.46 us
    pallas_call x4, Pallas kernels, exchange_rows(): pl.pallas_call(functools.partial(exchange_kernel, blocks, gather, more is...  3.97 us
  transfers between devices with their start and end apart: 6, of which 5 were waited for; matrix products, arithmetic and copies ran while one was open for 0% of the time, Pallas kernels for 4%

profile of v13, /device:TPU:0, one launch (start us, length us, event | category | flops | bytes accessed | tf_op | source)
XLA Modules:
  0.0 69.5 jit_solution(15673874914322098958)
XLA Ops:
  0.7 9.2 %half_transform_pairs.1 = (bf16[384,128,128]{2,1,0:T(8,128)(2,1)S(1)}, bf16[16,16,8,128]{3,2,1,0:T(8,128)(2,1)S(1)}, bf16[512,256]{1,0:T(8,128)(2,1)S(1)}) custom-call(s32[1]{0:T(128)S(6)} %copy.6.live_ref, s32[3,320]{1,0:T(4,128)} %bitcast.16, bf16[320,128,128]{2,1,0:T(8,128)(2,1)} %blocks_hbm.1, bf16[3072,128]{1,0:T(8,128)(2,1)} %orb_hbm.1, ...), custom_call_target="tpu_custom_call" | custom-call | flops 2952790016 | bytes 23068672 | tf_op jit(solution)/shard_map/half_transform_pairs/pallas_call | solution.py:196
  9.8 22.2 %all_to_all.10 = bf16[16,16,8,128]{3,2,1,0:T(8,128)(2,1)S(1)} all-to-all(bf16[16,16,8,128]{3,2,1,0:T(8,128)(2,1)S(1)} %get-tuple-element.15), channel_id=1, replica_groups=mesh['groups'=2,'aux'=16] {'aux'}, dimensions={0} | all-to-all | bytes 1048576 | tf_op jit(solution)/shard_map/all_to_all | solution.py:330
  32.0 0.6 apply_metric.1
  32.6 18.4 %all_to_all.11.fitted_ref = bf16[16,16,8,128]{3,2,1,0:T(8,128)(2,1)S(1)} all-to-all(bf16[16,16,8,128]{3,2,1,0:T(8,128)(2,1)S(1)} %bitcast.15), channel_id=1, replica_groups=mesh['groups'=2,'aux'=16] {'aux'}, dimensions={0} | all-to-all | bytes 1048576 | tf_op jit(solution)/shard_map/all_to_all | solution.py:332
  51.0 1.4 %exchange_rows.4 = (bf16[6,192,128]{2,1,0:T(8,128)(2,1)S(1)}, bf16[2048,128]{1,0:T(8,128)(2,1)S(1)}) custom-call(bf16[16,3072,128]{2,1,0:T(8,128)(2,1)S(1)} %bitcast.10, bf16[16,16,8,128]{3,2,1,0:T(8,128)(2,1)S(1)} %all_to_all.11.fitted_ref), custom_call_target="tpu_custom_call" | custom-call | flops 603979776 | bytes 4718592 | tf_op jit(solution)/shard_map/exchange_rows/pallas_call | solution.py:307
  52.4 0.1 collective-permute-start.1
  52.5 0.6 exchange_rows.5
  53.1 0.6 collective-permute-start
  53.7 0.4 collective-permute-done.1.refs_0_
  54.1 1.4 %exchange_rows.7 = (bf16[2,192,128]{2,1,0:T(8,128)(2,1)S(1)}, bf16[2,192,128]{2,1,0:T(8,128)(2,1)S(1)}, bf16[2,192,128]{2,1,0:T(8,128)(2,1)S(1)}) custom-call(bf16[16,3072,128]{2,1,0:T(8,128)(2,1)S(1)} %bitcast.12, bf16[2048,128]{1,0:T(8,128)(2,1)S(1)} %get-tuple-element.16.fitted_ref, bf16[6,192,128]{2,1,0:T(8,128)(2,1)S(1)} %collective-permute-done.1.refs_0_), custom_call_target="tpu_custom_call" | custom-call | flops 603979776 | bytes 4718592 | tf_op jit(solution)/shard_map/exchange_rows/pallas_call | solution.py:307
  55.5 0.9 %collective-permute-start.2 = (bf16[2,192,128]{2,1,0:T(8,128)(2,1)S(1)}, bf16[2,192,128]{2,1,0:T(8,128)(2,1)S(1)}, u32[]{:S(2)}, u32[]{:S(2)}) collective-permute-start(bf16[2,192,128]{2,1,0:T(8,128)(2,1)S(1)} %get-tuple-element.18), channel_id=1, source_target_pairs={{0,2},{1,3},{2,0},{3,1},{4,6},{5,7},{6,4},{7,5},{8,10},{9,11},{10,... | collective-permute-start | bytes 294920 | tf_op jit(solution)/shard_map/ppermute | solution.py:337
  56.4 1.6 %collective-permute-start.3 = (bf16[2,192,128]{2,1,0:T(8,128)(2,1)S(1)}, bf16[2,192,128]{2,1,0:T(8,128)(2,1)S(1)}, u32[]{:S(2)}, u32[]{:S(2)}) collective-permute-start(bf16[2,192,128]{2,1,0:T(8,128)(2,1)S(1)} %get-tuple-element.19), channel_id=1, source_target_pairs={{0,4},{1,5},{2,6},{3,7},{4,0},{5,1},{6,2},{7,3},{8,12},{9,13},{10,... | collective-permute-start | bytes 294920 | tf_op jit(solution)/shard_map/ppermute | solution.py:337
  57.9 1.1 %collective-permute-start.4 = (bf16[2,192,128]{2,1,0:T(8,128)(2,1)S(1)}, bf16[2,192,128]{2,1,0:T(8,128)(2,1)S(1)}, u32[]{:S(2)}, u32[]{:S(2)}) collective-permute-start(bf16[2,192,128]{2,1,0:T(8,128)(2,1)S(1)} %get-tuple-element.20), channel_id=1, source_target_pairs={{0,6},{1,7},{2,4},{3,5},{4,2},{5,3},{6,0},{7,1},{8,14},{9,15},{10,... | collective-permute-start | bytes 294920 | tf_op jit(solution)/shard_map/ppermute | solution.py:337
  59.0 0.0 collective-permute-done.refs_0_
  59.1 0.6 exchange_rows.6
  59.6 0.8 %collective-permute-done.2 = bf16[2,192,128]{2,1,0:T(8,128)(2,1)S(1)} collective-permute-done((bf16[2,192,128]{2,1,0:T(8,128)(2,1)S(1)}, bf16[2,192,128]{2,1,0:T(8,128)(2,1)S(1)}, u32[]{:S(2)}, u32[]{:S(2)}) %collective-permute-start.2) | collective-permute-done | bytes 98336 | tf_op jit(solution)/shard_map/ppermute | solution.py:337
  60.4 1.1 %collective-permute-done.3 = bf16[2,192,128]{2,1,0:T(8,128)(2,1)S(1)} collective-permute-done((bf16[2,192,128]{2,1,0:T(8,128)(2,1)S(1)}, bf16[2,192,128]{2,1,0:T(8,128)(2,1)S(1)}, u32[]{:S(2)}, u32[]{:S(2)}) %collective-permute-start.3) | collective-permute-done | bytes 98336 | tf_op jit(solution)/shard_map/ppermute | solution.py:337
  61.5 2.2 %collective-permute-done.4 = bf16[2,192,128]{2,1,0:T(8,128)(2,1)S(1)} collective-permute-done((bf16[2,192,128]{2,1,0:T(8,128)(2,1)S(1)}, bf16[2,192,128]{2,1,0:T(8,128)(2,1)S(1)}, u32[]{:S(2)}, u32[]{:S(2)}) %collective-permute-start.4) | collective-permute-done | bytes 98336 | tf_op jit(solution)/shard_map/ppermute | solution.py:337
  63.8 2.3 %collective-permute-start.5 = (bf16[192,128]{1,0:T(8,128)(2,1)S(1)}, bf16[192,128]{1,0:T(8,128)(2,1)S(1)}, u32[]{:S(2)}, u32[]{:S(2)}) collective-permute-start(bf16[192,128]{1,0:T(8,128)(2,1)S(1)} %fusion.1), channel_id=1, source_target_pairs={{0,8},{1,9},{2,10},{3,11},{4,12},{5,13},{6,14},{7,15},{8,0},{9,1},... | collective-permute-start | bytes 147464 | tf_op jit(solution)/shard_map/ppermute | solution.py:337
  66.1 2.8 %collective-permute-done.5 = bf16[192,128]{1,0:T(8,128)(2,1)S(1)} collective-permute-done((bf16[192,128]{1,0:T(8,128)(2,1)S(1)}, bf16[192,128]{1,0:T(8,128)(2,1)S(1)}, u32[]{:S(2)}, u32[]{:S(2)}) %collective-permute-start.5) | collective-permute-done | bytes 49184 | tf_op jit(solution)/shard_map/ppermute | solution.py:337
  68.9 0.7 fusion
  (2 shorter events, 0.1 us)
Async XLA Ops:
  52.4 1.6 %collective-permute-start.1 = (bf16[6,192,128]{2,1,0:T(8,128)(2,1)S(1)}, bf16[6,192,128]{2,1,0:T(8,128)(2,1)S(1)}, u32[]{:S(2)}, u32[]{:S(2)}) collective-permute-start(bf16[6,192,128]{2,1,0:T(8,128)(2,1)S(1)} %get-tuple-element.17), channel_id=1, source_target_pairs={{0,1},{1,0},{2,3},{3,2},{4,5},{5,4},{6,7},{7,6},{8,9},{9,8},{10,11... | collective-permute-start | bytes 884744 | tf_op jit(solution)/shard_map/ppermute | solution.py:337
  53.1 6.0 %collective-permute-start = (bf16[2,192,128]{2,1,0:T(8,128)(2,1)S(1)}, bf16[2,192,128]{2,1,0:T(8,128)(2,1)S(1)}, u32[]{:S(2)}, u32[]{:S(2)}) collective-permute-start(bf16[2,192,128]{2,1,0:T(8,128)(2,1)S(1)} %exchange_rows.5), channel_id=1, source_target_pairs={{0,1},{1,0},{2,3},{3,2},{4,5},{5,4},{6,7},{7,6},{8,9},{9,8},{10,11... | collective-permute-start | bytes 294920 | tf_op jit(solution)/shard_map/ppermute | solution.py:337
  55.5 4.9 %collective-permute-start.2 = (bf16[2,192,128]{2,1,0:T(8,128)(2,1)S(1)}, bf16[2,192,128]{2,1,0:T(8,128)(2,1)S(1)}, u32[]{:S(2)}, u32[]{:S(2)}) collective-permute-start(bf16[2,192,128]{2,1,0:T(8,128)(2,1)S(1)} %get-tuple-element.18), channel_id=1, source_target_pairs={{0,2},{1,3},{2,0},{3,1},{4,6},{5,7},{6,4},{7,5},{8,10},{9,11},{10,... | collective-permute-start | bytes 294920 | tf_op jit(solution)/shard_map/ppermute | solution.py:337
  56.4 5.1 %collective-permute-start.3 = (bf16[2,192,128]{2,1,0:T(8,128)(2,1)S(1)}, bf16[2,192,128]{2,1,0:T(8,128)(2,1)S(1)}, u32[]{:S(2)}, u32[]{:S(2)}) collective-permute-start(bf16[2,192,128]{2,1,0:T(8,128)(2,1)S(1)} %get-tuple-element.19), channel_id=1, source_target_pairs={{0,4},{1,5},{2,6},{3,7},{4,0},{5,1},{6,2},{7,3},{8,12},{9,13},{10,... | collective-permute-start | bytes 294920 | tf_op jit(solution)/shard_map/ppermute | solution.py:337
  57.9 5.8 %collective-permute-start.4 = (bf16[2,192,128]{2,1,0:T(8,128)(2,1)S(1)}, bf16[2,192,128]{2,1,0:T(8,128)(2,1)S(1)}, u32[]{:S(2)}, u32[]{:S(2)}) collective-permute-start(bf16[2,192,128]{2,1,0:T(8,128)(2,1)S(1)} %get-tuple-element.20), channel_id=1, source_target_pairs={{0,6},{1,7},{2,4},{3,5},{4,2},{5,3},{6,0},{7,1},{8,14},{9,15},{10,... | collective-permute-start | bytes 294920 | tf_op jit(solution)/shard_map/ppermute | solution.py:337
  63.8 5.1 %collective-permute-start.5 = (bf16[192,128]{1,0:T(8,128)(2,1)S(1)}, bf16[192,128]{1,0:T(8,128)(2,1)S(1)}, u32[]{:S(2)}, u32[]{:S(2)}) collective-permute-start(bf16[192,128]{1,0:T(8,128)(2,1)S(1)} %fusion.1), channel_id=1, source_target_pairs={{0,8},{1,9},{2,10},{3,11},{4,12},{5,13},{6,14},{7,15},{8,0},{9,1},... | collective-permute-start | bytes 147464 | tf_op jit(solution)/shard_map/ppermute | solution.py:337

commit v14 on v13

--- a/solution.py
+++ b/solution.py
@@ -269,7 +269,7 @@
         fitted[q * occupied : (q + 1) * occupied, :] = block
 
 
-def exchange_kernel(blocks, gather, more, slab, fitted_ref, *refs):
+def exchange_kernel(blocks, gather, more, skip, slab, fitted_ref, *refs):
     refs = list(refs)
     more_ref = refs.pop(0) if more else None
     out_refs = [refs.pop(0) for _ in blocks]
@@ -292,11 +292,11 @@
         for u, (_, c, h) in enumerate(todo[g : g + together]):
             part = sums[u * each : (u + 1) * each]
             if more:
-                part = part + more_ref[g + u].astype(F32)
+                part = part + more_ref[skip + g + u].astype(F32)
             out_refs[c][h] = part.astype(out_refs[c].dtype)
 
 
-def exchange_rows(slab, fitted, owners, blocks, dtype, gather=False, more=None):
+def exchange_rows(slab, fitted, owners, blocks, dtype, gather=False, more=None, skip=0):
     q_dev, basis, occupied = slab.shape
     each = basis // owners
     count = sum(len(part) for part in blocks)
@@ -305,7 +305,7 @@
         out.append(jax.ShapeDtypeStruct((q_dev * occupied, occupied), BF16))
     operands = [pltpu.with_memory_space_constraint(slab, pltpu.VMEM), fitted] + ([] if more is None else [more])
     return pl.pallas_call(
-        functools.partial(exchange_kernel, blocks, gather, more is not None),
+        functools.partial(exchange_kernel, blocks, gather, more is not None, skip),
         out_shape=out,
         in_specs=[pl.BlockSpec(memory_space=pltpu.VMEM)] * len(operands),
         out_specs=[pl.BlockSpec(memory_space=pltpu.VMEM)] * len(out),
@@ -337,16 +337,17 @@
         return lax.ppermute(x, "aux", [(d, d ^ bits) for d in range(owners)])
 
     far = range(0, owners, 8)
-    leave = [tuple(x + k for k in far) for x in (2, 4, 6)]
-    stay = [tuple(far)]
-    flip = lambda parts: [tuple(k ^ 1 for k in part) for part in parts]
-    *away, fitted = exchange_rows(slab, fitted, owners, flip([sum(leave, ())]), BF16, gather=True)
-    from_core = swap(away[0], 1)
-    away = exchange_rows(slab, fitted, owners, flip(stay), BF16)
-    to_stay = swap(away[0], 1)
-    away = exchange_rows(slab, fitted, owners, leave, BF16, more=from_core)
-    arrived = [swap(x, bits) for x, bits in zip(away, (2, 4, 6))]
-    (near,) = exchange_rows(slab, fitted, owners, stay, F32, more=to_stay)
+    stay, out2, out4, out6 = (tuple(x + k for k in far) for x in (0, 2, 4, 6))
+    flip = lambda blocks: [tuple(k ^ 1 for k in blocks)]
+    away, fitted = exchange_rows(slab, fitted, owners, flip(out6 + out4), BF16, gather=True)
+    early = swap(away, 1)
+    (away,) = exchange_rows(slab, fitted, owners, flip(out2 + stay), BF16)
+    late = swap(away, 1)
+    away6, away4 = exchange_rows(slab, fitted, owners, [out6, out4], BF16, more=early)
+    arrived = [swap(away6, 6), swap(away4, 4)]
+    (away2,) = exchange_rows(slab, fitted, owners, [out2], BF16, more=late)
+    arrived.append(swap(away2, 2))
+    (near,) = exchange_rows(slab, fitted, owners, [stay], F32, more=late, skip=len(far))
     for x in arrived:
         near = near + x.astype(F32)
     total = near[0]

time: 69.3 us -> 69.5 us (level)
  blocking collectives: 40.6 us -> 39.1 us
  Pallas kernels: 13.7 us -> 14.5 us
    all_to_all x1, blocking collectives: 22.2 us -> 20.7 us  [body(): held = trade(pairs).reshape(naux, occupied // owners, occupied)]
    pallas_call x4 -> x5, Pallas kernels: 3.97 us -> 4.15 us  [exchange_rows(): pl.pallas_call(functools.partial(exchange_kernel, blocks, gather, more is...]
  transfers between devices with their start and end apart: 6 -> 6, of which waited for: 5 -> 4; matrix products, arithmetic and copies ran while one was open for 0% -> 0% of each run, Pallas kernels for 4% -> 3%
where the time goes in v14:
time: 69.5 us; the launch traced here: 69.2 us
  blocking collectives  39.1 us (56%)
  Pallas kernels  14.5 us (21%)
  waiting for transfers between devices  7.83 us (11%)
  starting transfers between devices  6.46 us (9%)
  between operations  0.72 us (1%)
    all_to_all x1, blocking collectives, body(): held = trade(pairs).reshape(naux, occupied // owners, occupied)  20.7 us
    all_to_all x1, blocking collectives, body(): fitted = trade(fitted.reshape(owners, q_dev, occupied // owners, occupied))  18.4 us
    pallas_call x1, Pallas kernels, half_transform(): pl.pallas_call(functools.partial(half_kernel, owners if split else 0, q_d...  9.7 us
    ppermute x6, waiting for transfers between devices, swap(): return lax.ppermute(x, 'aux', [(d, d ^ bits) for d in range(owners)])  7.83 us
    ppermute x6, starting transfers between devices, swap(): return lax.ppermute(x, 'aux', [(d, d ^ bits) for d in range(owners)])  6.46 us
    pallas_call x5, Pallas kernels, exchange_rows(): pl.pallas_call(functools.partial(exchange_kernel, blocks, gather, more is...  4.15 us
  transfers between devices with their start and end apart: 6, of which 4 were waited for; matrix products, arithmetic and copies ran while one was open for 0% of the time, Pallas kernels for 3%

profile of v14, /device:TPU:0, one launch (start us, length us, event | category | flops | bytes accessed | tf_op | source)
XLA Modules:
  0.0 69.2 jit_solution(7378510761549190860)
XLA Ops:
  0.7 9.7 %half_transform_pairs.1 = (bf16[384,128,128]{2,1,0:T(8,128)(2,1)S(1)}, bf16[16,16,8,128]{3,2,1,0:T(8,128)(2,1)S(1)}, bf16[512,256]{1,0:T(8,128)(2,1)S(1)}) custom-call(s32[1]{0:T(128)S(6)} %copy.6.live_ref, s32[3,320]{1,0:T(4,128)} %bitcast.17, bf16[320,128,128]{2,1,0:T(8,128)(2,1)} %blocks_hbm.1, bf16[3072,128]{1,0:T(8,128)(2,1)} %orb_hbm.1, ...), custom_call_target="tpu_custom_call" | custom-call | flops 2952790016 | bytes 23068672 | tf_op jit(solution)/shard_map/half_transform_pairs/pallas_call | solution.py:196
  10.4 20.7 %all_to_all.10 = bf16[16,16,8,128]{3,2,1,0:T(8,128)(2,1)S(1)} all-to-all(bf16[16,16,8,128]{3,2,1,0:T(8,128)(2,1)S(1)} %get-tuple-element.14), channel_id=1, replica_groups=mesh['groups'=2,'aux'=16] {'aux'}, dimensions={0} | all-to-all | bytes 1048576 | tf_op jit(solution)/shard_map/all_to_all | solution.py:330
  31.1 0.6 apply_metric.1
  31.7 18.4 %all_to_all.11.fitted_ref = bf16[16,16,8,128]{3,2,1,0:T(8,128)(2,1)S(1)} all-to-all(bf16[16,16,8,128]{3,2,1,0:T(8,128)(2,1)S(1)} %bitcast.16), channel_id=1, replica_groups=mesh['groups'=2,'aux'=16] {'aux'}, dimensions={0} | all-to-all | bytes 1048576 | tf_op jit(solution)/shard_map/all_to_all | solution.py:332
  50.1 1.0 %exchange_rows.5 = (bf16[4,192,128]{2,1,0:T(8,128)(2,1)S(1)}, bf16[2048,128]{1,0:T(8,128)(2,1)S(1)}) custom-call(bf16[16,3072,128]{2,1,0:T(8,128)(2,1)S(1)} %bitcast.10, bf16[16,16,8,128]{3,2,1,0:T(8,128)(2,1)S(1)} %all_to_all.11.fitted_ref), custom_call_target="tpu_custom_call" | custom-call | flops 402653184 | bytes 3145728 | tf_op jit(solution)/shard_map/exchange_rows/pallas_call | solution.py:307
  51.1 1.0 %exchange_rows.6 = bf16[4,192,128]{2,1,0:T(8,128)(2,1)S(1)} custom-call(bf16[16,3072,128]{2,1,0:T(8,128)(2,1)S(1)} %bitcast.11, bf16[2048,128]{1,0:T(8,128)(2,1)S(1)} %get-tuple-element.15.fitted_ref), custom_call_target="tpu_custom_call" | custom-call | flops 402653184 | bytes 3145728 | tf_op jit(solution)/shard_map/exchange_rows/pallas_call | solution.py:307
  52.1 0.1 collective-permute-start
  52.2 0.5 collective-permute-start.1
  52.7 0.9 %collective-permute-done.refs_0_ = bf16[4,192,128]{2,1,0:T(8,128)(2,1)S(1)} collective-permute-done((bf16[4,192,128]{2,1,0:T(8,128)(2,1)S(1)}, bf16[4,192,128]{2,1,0:T(8,128)(2,1)S(1)}, u32[]{:S(2)}, u32[]{:S(2)}) %collective-permute-start) | collective-permute-done | bytes 196640 | tf_op jit(solution)/shard_map/ppermute | solution.py:337
  53.6 0.6 exchange_rows.9
  54.2 0.9 %collective-permute-start.4 = (bf16[2,192,128]{2,1,0:T(8,128)(2,1)S(1)}, bf16[2,192,128]{2,1,0:T(8,128)(2,1)S(1)}, u32[]{:S(2)}, u32[]{:S(2)}) collective-permute-start(bf16[2,192,128]{2,1,0:T(8,128)(2,1)S(1)} %exchange_rows.9), channel_id=1, source_target_pairs={{0,2},{1,3},{2,0},{3,1},{4,6},{5,7},{6,4},{7,5},{8,10},{9,11},{10,... | collective-permute-start | bytes 294920 | tf_op jit(solution)/shard_map/ppermute | solution.py:337
  55.0 0.0 collective-permute-done.1.refs_0_
  55.0 1.0 %exchange_rows.8 = (bf16[2,192,128]{2,1,0:T(8,128)(2,1)S(1)}, bf16[2,192,128]{2,1,0:T(8,128)(2,1)S(1)}) custom-call(bf16[16,3072,128]{2,1,0:T(8,128)(2,1)S(1)} %bitcast.13, bf16[2048,128]{1,0:T(8,128)(2,1)S(1)} %get-tuple-element.15.fitted_ref, bf16[4,192,128]{2,1,0:T(8,128)(2,1)S(1)} %collective-permute-done.1.refs_0_), custom_call_target="tpu_custom_call" | custom-call | flops 402653184 | bytes 3145728 | tf_op jit(solution)/shard_map/exchange_rows/pallas_call | solution.py:307
  56.0 2.1 %collective-permute-start.2 = (bf16[2,192,128]{2,1,0:T(8,128)(2,1)S(1)}, bf16[2,192,128]{2,1,0:T(8,128)(2,1)S(1)}, u32[]{:S(2)}, u32[]{:S(2)}) collective-permute-start(bf16[2,192,128]{2,1,0:T(8,128)(2,1)S(1)} %get-tuple-element.17), channel_id=1, source_target_pairs={{0,6},{1,7},{2,4},{3,5},{4,2},{5,3},{6,0},{7,1},{8,14},{9,15},{10,... | collective-permute-start | bytes 294920 | tf_op jit(solution)/shard_map/ppermute | solution.py:337
  58.1 0.6 collective-permute-start.3
  58.8 0.6 exchange_rows.7
  59.4 0.0 collective-permute-done.4
  59.4 3.3 %collective-permute-done.2 = bf16[2,192,128]{2,1,0:T(8,128)(2,1)S(1)} collective-permute-done((bf16[2,192,128]{2,1,0:T(8,128)(2,1)S(1)}, bf16[2,192,128]{2,1,0:T(8,128)(2,1)S(1)}, u32[]{:S(2)}, u32[]{:S(2)}) %collective-permute-start.2) | collective-permute-done | bytes 98336 | tf_op jit(solution)/shard_map/ppermute | solution.py:337
  62.7 0.8 %collective-permute-done.3 = bf16[2,192,128]{2,1,0:T(8,128)(2,1)S(1)} collective-permute-done((bf16[2,192,128]{2,1,0:T(8,128)(2,1)S(1)}, bf16[2,192,128]{2,1,0:T(8,128)(2,1)S(1)}, u32[]{:S(2)}, u32[]{:S(2)}) %collective-permute-start.3) | collective-permute-done | bytes 98336 | tf_op jit(solution)/shard_map/ppermute | solution.py:337
  63.5 2.3 %collective-permute-start.5 = (bf16[192,128]{1,0:T(8,128)(2,1)S(1)}, bf16[192,128]{1,0:T(8,128)(2,1)S(1)}, u32[]{:S(2)}, u32[]{:S(2)}) collective-permute-start(bf16[192,128]{1,0:T(8,128)(2,1)S(1)} %fusion.1), channel_id=1, source_target_pairs={{0,8},{1,9},{2,10},{3,11},{4,12},{5,13},{6,14},{7,15},{8,0},{9,1},... | collective-permute-start | bytes 147464 | tf_op jit(solution)/shard_map/ppermute | solution.py:337
  65.8 2.8 %collective-permute-done.5 = bf16[192,128]{1,0:T(8,128)(2,1)S(1)} collective-permute-done((bf16[192,128]{1,0:T(8,128)(2,1)S(1)}, bf16[192,128]{1,0:T(8,128)(2,1)S(1)}, u32[]{:S(2)}, u32[]{:S(2)}) %collective-permute-start.5) | collective-permute-done | bytes 49184 | tf_op jit(solution)/shard_map/ppermute | solution.py:337
  68.6 0.7 fusion
  (2 shorter events, 0.1 us)
Async XLA Ops:
  52.1 1.5 %collective-permute-start = (bf16[4,192,128]{2,1,0:T(8,128)(2,1)S(1)}, bf16[4,192,128]{2,1,0:T(8,128)(2,1)S(1)}, u32[]{:S(2)}, u32[]{:S(2)}) collective-permute-start(bf16[4,192,128]{2,1,0:T(8,128)(2,1)S(1)} %exchange_rows.6), channel_id=1, source_target_pairs={{0,1},{1,0},{2,3},{3,2},{4,5},{5,4},{6,7},{7,6},{8,9},{9,8},{10,11... | collective-permute-start | bytes 589832 | tf_op jit(solution)/shard_map/ppermute | solution.py:337
  52.2 2.9 %collective-permute-start.1 = (bf16[4,192,128]{2,1,0:T(8,128)(2,1)S(1)}, bf16[4,192,128]{2,1,0:T(8,128)(2,1)S(1)}, u32[]{:S(2)}, u32[]{:S(2)}) collective-permute-start(bf16[4,192,128]{2,1,0:T(8,128)(2,1)S(1)} %get-tuple-element.16), channel_id=1, source_target_pairs={{0,1},{1,0},{2,3},{3,2},{4,5},{5,4},{6,7},{7,6},{8,9},{9,8},{10,11... | collective-permute-start | bytes 589832 | tf_op jit(solution)/shard_map/ppermute | solution.py:337
  54.2 5.2 %collective-permute-start.4 = (bf16[2,192,128]{2,1,0:T(8,128)(2,1)S(1)}, bf16[2,192,128]{2,1,0:T(8,128)(2,1)S(1)}, u32[]{:S(2)}, u32[]{:S(2)}) collective-permute-start(bf16[2,192,128]{2,1,0:T(8,128)(2,1)S(1)} %exchange_rows.9), channel_id=1, source_target_pairs={{0,2},{1,3},{2,0},{3,1},{4,6},{5,7},{6,4},{7,5},{8,10},{9,11},{10,... | collective-permute-start | bytes 294920 | tf_op jit(solution)/shard_map/ppermute | solution.py:337
  56.0 6.6 %collective-permute-start.2 = (bf16[2,192,128]{2,1,0:T(8,128)(2,1)S(1)}, bf16[2,192,128]{2,1,0:T(8,128)(2,1)S(1)}, u32[]{:S(2)}, u32[]{:S(2)}) collective-permute-start(bf16[2,192,128]{2,1,0:T(8,128)(2,1)S(1)} %get-tuple-element.17), channel_id=1, source_target_pairs={{0,6},{1,7},{2,4},{3,5},{4,2},{5,3},{6,0},{7,1},{8,14},{9,15},{10,... | collective-permute-start | bytes 294920 | tf_op jit(solution)/shard_map/ppermute | solution.py:337
  58.1 5.3 %collective-permute-start.3 = (bf16[2,192,128]{2,1,0:T(8,128)(2,1)S(1)}, bf16[2,192,128]{2,1,0:T(8,128)(2,1)S(1)}, u32[]{:S(2)}, u32[]{:S(2)}) collective-permute-start(bf16[2,192,128]{2,1,0:T(8,128)(2,1)S(1)} %get-tuple-element.18), channel_id=1, source_target_pairs={{0,4},{1,5},{2,6},{3,7},{4,0},{5,1},{6,2},{7,3},{8,12},{9,13},{10,... | collective-permute-start | bytes 294920 | tf_op jit(solution)/shard_map/ppermute | solution.py:337
  63.5 5.1 %collective-permute-start.5 = (bf16[192,128]{1,0:T(8,128)(2,1)S(1)}, bf16[192,128]{1,0:T(8,128)(2,1)S(1)}, u32[]{:S(2)}, u32[]{:S(2)}) collective-permute-start(bf16[192,128]{1,0:T(8,128)(2,1)S(1)} %fusion.1), channel_id=1, source_target_pairs={{0,8},{1,9},{2,10},{3,11},{4,12},{5,13},{6,14},{7,15},{8,0},{9,1},... | collective-permute-start | bytes 147464 | tf_op jit(solution)/shard_map/ppermute | solution.py:337

commit v15 on v14

--- a/solution.py
+++ b/solution.py
@@ -269,15 +269,18 @@
         fitted[q * occupied : (q + 1) * occupied, :] = block
 
 
-def exchange_kernel(blocks, gather, more, skip, slab, fitted_ref, *refs):
+def exchange_kernel(blocks, gather, more, skip, after, slab, fitted_ref, *refs):
     refs = list(refs)
     more_ref = refs.pop(0) if more else None
+    if after:
+        refs.pop(0)
     out_refs = [refs.pop(0) for _ in blocks]
     if gather:
         fitted = refs.pop(0)
         gather_fitted(fitted_ref, fitted)
     else:
         fitted = fitted_ref
+        refs.pop(0)[...] = jnp.zeros((8, 128), F32)
     q_dev = slab.shape[0]
     each = out_refs[0].shape[1]
     me = lax.axis_index("aux").astype(jnp.int32)
@@ -296,16 +299,18 @@
             out_refs[c][h] = part.astype(out_refs[c].dtype)
 
 
-def exchange_rows(slab, fitted, owners, blocks, dtype, gather=False, more=None, skip=0):
+def exchange_rows(slab, fitted, owners, blocks, dtype, gather=False, more=None, skip=0, after=None):
     q_dev, basis, occupied = slab.shape
     each = basis // owners
     count = sum(len(part) for part in blocks)
     out = [jax.ShapeDtypeStruct((len(part), each, occupied), dtype) for part in blocks]
     if gather:
         out.append(jax.ShapeDtypeStruct((q_dev * occupied, occupied), BF16))
-    operands = [pltpu.with_memory_space_constraint(slab, pltpu.VMEM), fitted] + ([] if more is None else [more])
+    else:
+        out.append(jax.ShapeDtypeStruct((8, 128), F32))
+    operands = [pltpu.with_memory_space_constraint(slab, pltpu.VMEM), fitted] + [x for x in (more, after) if x is not None]
     return pl.pallas_call(
-        functools.partial(exchange_kernel, blocks, gather, more is not None, skip),
+        functools.partial(exchange_kernel, blocks, gather, more is not None, skip, after is not None),
         out_shape=out,
         in_specs=[pl.BlockSpec(memory_space=pltpu.VMEM)] * len(operands),
         out_specs=[pl.BlockSpec(memory_space=pltpu.VMEM)] * len(out),
@@ -339,15 +344,15 @@
     far = range(0, owners, 8)
     stay, out2, out4, out6 = (tuple(x + k for k in far) for x in (0, 2, 4, 6))
     flip = lambda blocks: [tuple(k ^ 1 for k in blocks)]
-    away, fitted = exchange_rows(slab, fitted, owners, flip(out6 + out4), BF16, gather=True)
-    early = swap(away, 1)
-    (away,) = exchange_rows(slab, fitted, owners, flip(out2 + stay), BF16)
-    late = swap(away, 1)
-    away6, away4 = exchange_rows(slab, fitted, owners, [out6, out4], BF16, more=early)
+    away, fitted = exchange_rows(slab, fitted, owners, flip(out6 + out4 + out2), BF16, gather=True)
+    leave = swap(away, 1)
+    away, _ = exchange_rows(slab, fitted, owners, flip(stay), BF16)
+    keep = swap(away, 1)
+    away6, away4, tie = exchange_rows(slab, fitted, owners, [out6, out4], BF16, more=leave)
     arrived = [swap(away6, 6), swap(away4, 4)]
-    (away2,) = exchange_rows(slab, fitted, owners, [out2], BF16, more=late)
+    away2, tie = exchange_rows(slab, fitted, owners, [out2], BF16, more=leave, skip=2 * len(far), after=tie)
     arrived.append(swap(away2, 2))
-    (near,) = exchange_rows(slab, fitted, owners, [stay], F32, more=late, skip=len(far))
+    near, _ = exchange_rows(slab, fitted, owners, [stay], F32, more=keep, after=tie)
     for x in arrived:
         near = near + x.astype(F32)
     total = near[0]

time: 69.5 us -> 69.2 us (level)
  waiting for transfers between devices: 7.83 us -> 6.4 us
  blocking collectives: 39.1 us -> 40.1 us
    ppermute x6, waiting for transfers between devices: 7.83 us -> 6.4 us  [swap(): return lax.ppermute(x, 'aux', [(d, d ^ bits) for d in range(owners)])]
    pallas_call x5, Pallas kernels: 4.15 us -> 5.2 us  [exchange_rows(): pl.pallas_call(functools.partial(exchange_kernel, blocks, gather, more is...]
    all_to_all x1, blocking collectives: 20.7 us -> 21.7 us  [body(): held = trade(pairs).reshape(naux, occupied // owners, occupied)]
  transfers between devices with their start and end apart: 6 -> 6, of which waited for: 4 -> 4; matrix products, arithmetic and copies ran while one was open for 0% -> 0% of each run, Pallas kernels for 3% -> 5%
where the time goes in v15:
time: 69.2 us
  blocking collectives  40.1 us (58%)
  Pallas kernels  15 us (22%)
  waiting for transfers between devices  6.4 us (9%)
  starting transfers between devices  6.38 us (9%)
  between operations  0.7 us (1%)
    all_to_all x1, blocking collectives, body(): held = trade(pairs).reshape(naux, occupied // owners, occupied)  21.7 us
    all_to_all x1, blocking collectives, body(): fitted = trade(fitted.reshape(owners, q_dev, occupied // owners, occupied))  18.4 us
    pallas_call x1, Pallas kernels, half_transform(): pl.pallas_call(functools.partial(half_kernel, owners if split else 0, q_d...  9.17 us
    ppermute x6, waiting for transfers between devices, swap(): return lax.ppermute(x, 'aux', [(d, d ^ bits) for d in range(owners)])  6.4 us
    ppermute x6, starting transfers between devices, swap(): return lax.ppermute(x, 'aux', [(d, d ^ bits) for d in range(owners)])  6.38 us
    pallas_call x5, Pallas kernels, exchange_rows(): pl.pallas_call(functools.partial(exchange_kernel, blocks, gather, more is...  5.2 us
  transfers between devices with their start and end apart: 6, of which 4 were waited for; matrix products, arithmetic and copies ran while one was open for 0% of the time, Pallas kernels for 5%

profile of v15, /device:TPU:0, one launch (start us, length us, event | category | flops | bytes accessed | tf_op | source)
XLA Modules:
  0.0 69.2 jit_solution(2511571694115099432)
XLA Ops:
  0.7 9.2 %half_transform_pairs.1 = (bf16[384,128,128]{2,1,0:T(8,128)(2,1)S(1)}, bf16[16,16,8,128]{3,2,1,0:T(8,128)(2,1)S(1)}, bf16[512,256]{1,0:T(8,128)(2,1)S(1)}) custom-call(s32[1]{0:T(128)S(6)} %copy.6.live_ref, s32[3,320]{1,0:T(4,128)} %bitcast.17, bf16[320,128,128]{2,1,0:T(8,128)(2,1)} %blocks_hbm.1, bf16[3072,128]{1,0:T(8,128)(2,1)} %orb_hbm.1, ...), custom_call_target="tpu_custom_call" | custom-call | flops 2952790016 | bytes 23068672 | tf_op jit(solution)/shard_map/half_transform_pairs/pallas_call | solution.py:196
  9.8 21.7 %all_to_all.10 = bf16[16,16,8,128]{3,2,1,0:T(8,128)(2,1)S(1)} all-to-all(bf16[16,16,8,128]{3,2,1,0:T(8,128)(2,1)S(1)} %get-tuple-element.19), channel_id=1, replica_groups=mesh['groups'=2,'aux'=16] {'aux'}, dimensions={0} | all-to-all | bytes 1048576 | tf_op jit(solution)/shard_map/all_to_all | solution.py:335
  31.5 0.6 apply_metric.1
  32.1 18.4 %all_to_all.11.fitted_ref = bf16[16,16,8,128]{3,2,1,0:T(8,128)(2,1)S(1)} all-to-all(bf16[16,16,8,128]{3,2,1,0:T(8,128)(2,1)S(1)} %bitcast.16), channel_id=1, replica_groups=mesh['groups'=2,'aux'=16] {'aux'}, dimensions={0} | all-to-all | bytes 1048576 | tf_op jit(solution)/shard_map/all_to_all | solution.py:337
  50.5 1.5 %exchange_rows.5 = (bf16[6,192,128]{2,1,0:T(8,128)(2,1)S(1)}, bf16[2048,128]{1,0:T(8,128)(2,1)S(1)}) custom-call(bf16[16,3072,128]{2,1,0:T(8,128)(2,1)S(1)} %bitcast.10, bf16[16,16,8,128]{3,2,1,0:T(8,128)(2,1)S(1)} %all_to_all.11.fitted_ref), custom_call_target="tpu_custom_call" | custom-call | flops 603979776 | bytes 4718592 | tf_op jit(solution)/shard_map/exchange_rows/pallas_call | solution.py:312
  52.0 0.1 collective-permute-start.1
  52.0 1.1 %exchange_rows.6 = (bf16[2,192,128]{2,1,0:T(8,128)(2,1)S(1)}, f32[8,128]{1,0:T(8,128)}) custom-call(bf16[16,3072,128]{2,1,0:T(8,128)(2,1)S(1)} %bitcast.11, bf16[2048,128]{1,0:T(8,128)(2,1)S(1)} %get-tuple-element.20.fitted_ref), custom_call_target="tpu_custom_call" | custom-call | flops 201326592 | bytes 1572864 | tf_op jit(solution)/shard_map/exchange_rows/pallas_call | solution.py:312
  53.1 0.5 collective-permute-start
  53.6 0.0 collective-permute-done.1.refs_0_
  53.6 1.0 %exchange_rows.7 = (bf16[2,192,128]{2,1,0:T(8,128)(2,1)S(1)}, bf16[2,192,128]{2,1,0:T(8,128)(2,1)S(1)}, f32[8,128]{1,0:T(8,128)S(1)}) custom-call(bf16[16,3072,128]{2,1,0:T(8,128)(2,1)S(1)} %bitcast.12, bf16[2048,128]{1,0:T(8,128)(2,1)S(1)} %get-tuple-element.20.fitted_ref, bf16[6,192,128]{2,1,0:T(8,128)(2,1)S(1)} %collective-permute-done.1.refs_0_), custom_call_target="tpu_custom_call" | custom-call | flops 402653184 | bytes 3145728 | tf_op jit(solution)/shard_map/exchange_rows/pallas_call | solution.py:312
  54.6 0.6 exchange_rows.8
  55.2 0.9 %collective-permute-start.4 = (bf16[2,192,128]{2,1,0:T(8,128)(2,1)S(1)}, bf16[2,192,128]{2,1,0:T(8,128)(2,1)S(1)}, u32[]{:S(2)}, u32[]{:S(2)}) collective-permute-start(bf16[2,192,128]{2,1,0:T(8,128)(2,1)S(1)} %get-tuple-element.28), channel_id=1, source_target_pairs={{0,2},{1,3},{2,0},{3,1},{4,6},{5,7},{6,4},{7,5},{8,10},{9,11},{10,... | collective-permute-start | bytes 294920 | tf_op jit(solution)/shard_map/ppermute | solution.py:342
  56.1 2.0 %collective-permute-start.2 = (bf16[2,192,128]{2,1,0:T(8,128)(2,1)S(1)}, bf16[2,192,128]{2,1,0:T(8,128)(2,1)S(1)}, u32[]{:S(2)}, u32[]{:S(2)}) collective-permute-start(bf16[2,192,128]{2,1,0:T(8,128)(2,1)S(1)} %get-tuple-element.26), channel_id=1, source_target_pairs={{0,6},{1,7},{2,4},{3,5},{4,2},{5,3},{6,0},{7,1},{8,14},{9,15},{10,... | collective-permute-start | bytes 294920 | tf_op jit(solution)/shard_map/ppermute | solution.py:342
  58.1 0.6 collective-permute-start.3
  58.8 0.0 collective-permute-done.refs_0_
  58.8 1.1 %exchange_rows.9 = (f32[2,192,128]{2,1,0:T(8,128)S(1)}, f32[8,128]{1,0:T(8,128)}) custom-call(bf16[16,3072,128]{2,1,0:T(8,128)(2,1)S(1)} %bitcast.14, bf16[2048,128]{1,0:T(8,128)(2,1)S(1)} %get-tuple-element.20.fitted_ref, bf16[2,192,128]{2,1,0:T(8,128)(2,1)S(1)} %collective-permute-done.refs_0_, f32[8,128]{1,0:T(8,128)S(1)} %get-tuple-element.24.refs_1_), custom_call_target="tpu_custom_call" | custom-call | flops 201326592 | bytes 1572864 | tf_op jit(solution)/shard_map/exchange_rows/pallas_call | solution.py:312
  59.9 1.9 %collective-permute-done.4 = bf16[2,192,128]{2,1,0:T(8,128)(2,1)S(1)} collective-permute-done((bf16[2,192,128]{2,1,0:T(8,128)(2,1)S(1)}, bf16[2,192,128]{2,1,0:T(8,128)(2,1)S(1)}, u32[]{:S(2)}, u32[]{:S(2)}) %collective-permute-start.4) | collective-permute-done | bytes 98336 | tf_op jit(solution)/shard_map/ppermute | solution.py:342
  61.7 0.9 %collective-permute-done.2 = bf16[2,192,128]{2,1,0:T(8,128)(2,1)S(1)} collective-permute-done((bf16[2,192,128]{2,1,0:T(8,128)(2,1)S(1)}, bf16[2,192,128]{2,1,0:T(8,128)(2,1)S(1)}, u32[]{:S(2)}, u32[]{:S(2)}) %collective-permute-start.2) | collective-permute-done | bytes 98336 | tf_op jit(solution)/shard_map/ppermute | solution.py:342
  62.7 0.8 %collective-permute-done.3 = bf16[2,192,128]{2,1,0:T(8,128)(2,1)S(1)} collective-permute-done((bf16[2,192,128]{2,1,0:T(8,128)(2,1)S(1)}, bf16[2,192,128]{2,1,0:T(8,128)(2,1)S(1)}, u32[]{:S(2)}, u32[]{:S(2)}) %collective-permute-start.3) | collective-permute-done | bytes 98336 | tf_op jit(solution)/shard_map/ppermute | solution.py:342
  63.5 2.3 %collective-permute-start.5 = (bf16[192,128]{1,0:T(8,128)(2,1)S(1)}, bf16[192,128]{1,0:T(8,128)(2,1)S(1)}, u32[]{:S(2)}, u32[]{:S(2)}) collective-permute-start(bf16[192,128]{1,0:T(8,128)(2,1)S(1)} %fusion.1), channel_id=1, source_target_pairs={{0,8},{1,9},{2,10},{3,11},{4,12},{5,13},{6,14},{7,15},{8,0},{9,1},... | collective-permute-start | bytes 147464 | tf_op jit(solution)/shard_map/ppermute | solution.py:342
  65.8 2.8 %collective-permute-done.5 = bf16[192,128]{1,0:T(8,128)(2,1)S(1)} collective-permute-done((bf16[192,128]{1,0:T(8,128)(2,1)S(1)}, bf16[192,128]{1,0:T(8,128)(2,1)S(1)}, u32[]{:S(2)}, u32[]{:S(2)}) %collective-permute-start.5) | collective-permute-done | bytes 49184 | tf_op jit(solution)/shard_map/ppermute | solution.py:342
  68.6 0.7 fusion
  (2 shorter events, 0.1 us)
Async XLA Ops:
  52.0 1.7 %collective-permute-start.1 = (bf16[6,192,128]{2,1,0:T(8,128)(2,1)S(1)}, bf16[6,192,128]{2,1,0:T(8,128)(2,1)S(1)}, u32[]{:S(2)}, u32[]{:S(2)}) collective-permute-start(bf16[6,192,128]{2,1,0:T(8,128)(2,1)S(1)} %get-tuple-element.22), channel_id=1, source_target_pairs={{0,1},{1,0},{2,3},{3,2},{4,5},{5,4},{6,7},{7,6},{8,9},{9,8},{10,11... | collective-permute-start | bytes 884744 | tf_op jit(solution)/shard_map/ppermute | solution.py:342
  53.1 5.6 %collective-permute-start = (bf16[2,192,128]{2,1,0:T(8,128)(2,1)S(1)}, bf16[2,192,128]{2,1,0:T(8,128)(2,1)S(1)}, u32[]{:S(2)}, u32[]{:S(2)}) collective-permute-start(bf16[2,192,128]{2,1,0:T(8,128)(2,1)S(1)} %get-tuple-element.21), channel_id=1, source_target_pairs={{0,1},{1,0},{2,3},{3,2},{4,5},{5,4},{6,7},{7,6},{8,9},{9,8},{10,11... | collective-permute-start | bytes 294920 | tf_op jit(solution)/shard_map/ppermute | solution.py:342
  55.2 6.5 %collective-permute-start.4 = (bf16[2,192,128]{2,1,0:T(8,128)(2,1)S(1)}, bf16[2,192,128]{2,1,0:T(8,128)(2,1)S(1)}, u32[]{:S(2)}, u32[]{:S(2)}) collective-permute-start(bf16[2,192,128]{2,1,0:T(8,128)(2,1)S(1)} %get-tuple-element.28), channel_id=1, source_target_pairs={{0,2},{1,3},{2,0},{3,1},{4,6},{5,7},{6,4},{7,5},{8,10},{9,11},{10,... | collective-permute-start | bytes 294920 | tf_op jit(solution)/shard_map/ppermute | solution.py:342
  56.1 6.6 %collective-permute-start.2 = (bf16[2,192,128]{2,1,0:T(8,128)(2,1)S(1)}, bf16[2,192,128]{2,1,0:T(8,128)(2,1)S(1)}, u32[]{:S(2)}, u32[]{:S(2)}) collective-permute-start(bf16[2,192,128]{2,1,0:T(8,128)(2,1)S(1)} %get-tuple-element.26), channel_id=1, source_target_pairs={{0,6},{1,7},{2,4},{3,5},{4,2},{5,3},{6,0},{7,1},{8,14},{9,15},{10,... | collective-permute-start | bytes 294920 | tf_op jit(solution)/shard_map/ppermute | solution.py:342
  58.1 5.3 %collective-permute-start.3 = (bf16[2,192,128]{2,1,0:T(8,128)(2,1)S(1)}, bf16[2,192,128]{2,1,0:T(8,128)(2,1)S(1)}, u32[]{:S(2)}, u32[]{:S(2)}) collective-permute-start(bf16[2,192,128]{2,1,0:T(8,128)(2,1)S(1)} %get-tuple-element.27), channel_id=1, source_target_pairs={{0,4},{1,5},{2,6},{3,7},{4,0},{5,1},{6,2},{7,3},{8,12},{9,13},{10,... | collective-permute-start | bytes 294920 | tf_op jit(solution)/shard_map/ppermute | solution.py:342
  63.5 5.1 %collective-permute-start.5 = (bf16[192,128]{1,0:T(8,128)(2,1)S(1)}, bf16[192,128]{1,0:T(8,128)(2,1)S(1)}, u32[]{:S(2)}, u32[]{:S(2)}) collective-permute-start(bf16[192,128]{1,0:T(8,128)(2,1)S(1)} %fusion.1), channel_id=1, source_target_pairs={{0,8},{1,9},{2,10},{3,11},{4,12},{5,13},{6,14},{7,15},{8,0},{9,1},... | collective-permute-start | bytes 147464 | tf_op jit(solution)/shard_map/ppermute | solution.py:342

commit v16 on v15

--- a/solution.py
+++ b/solution.py
@@ -269,7 +269,7 @@
         fitted[q * occupied : (q + 1) * occupied, :] = block
 
 
-def exchange_kernel(blocks, gather, more, skip, after, slab, fitted_ref, *refs):
+def exchange_kernel(blocks, gather, more, skip, after, tie, slab, fitted_ref, *refs):
     refs = list(refs)
     more_ref = refs.pop(0) if more else None
     if after:
@@ -280,6 +280,7 @@
         gather_fitted(fitted_ref, fitted)
     else:
         fitted = fitted_ref
+    if tie:
         refs.pop(0)[...] = jnp.zeros((8, 128), F32)
     q_dev = slab.shape[0]
     each = out_refs[0].shape[1]
@@ -299,25 +300,25 @@
             out_refs[c][h] = part.astype(out_refs[c].dtype)
 
 
-def exchange_rows(slab, fitted, owners, blocks, dtype, gather=False, more=None, skip=0, after=None):
+def exchange_rows(slab, fitted, owners, blocks, dtype, gather=False, more=None, skip=0, after=None, tie=False):
     q_dev, basis, occupied = slab.shape
     each = basis // owners
     count = sum(len(part) for part in blocks)
     out = [jax.ShapeDtypeStruct((len(part), each, occupied), dtype) for part in blocks]
     if gather:
         out.append(jax.ShapeDtypeStruct((q_dev * occupied, occupied), BF16))
-    else:
+    if tie:
         out.append(jax.ShapeDtypeStruct((8, 128), F32))
     operands = [pltpu.with_memory_space_constraint(slab, pltpu.VMEM), fitted] + [x for x in (more, after) if x is not None]
     return pl.pallas_call(
-        functools.partial(exchange_kernel, blocks, gather, more is not None, skip, after is not None),
+        functools.partial(exchange_kernel, blocks, gather, more is not None, skip, after is not None, tie),
         out_shape=out,
         in_specs=[pl.BlockSpec(memory_space=pltpu.VMEM)] * len(operands),
         out_specs=[pl.BlockSpec(memory_space=pltpu.VMEM)] * len(out),
         compiler_params=pltpu.CompilerParams(vmem_limit_bytes=24 * 2**20),
         cost_estimate=pl.CostEstimate(
-            flops=2 * q_dev * occupied * count * each * occupied,
-            bytes_accessed=2 * q_dev * occupied * count * each,
+            flops=2 * q_dev * occupied * count * each * occupied if after is None else 1,
+            bytes_accessed=2 * q_dev * occupied * count * each if after is None else 1,
             transcendentals=0,
         ),
         name="exchange_rows",
@@ -346,13 +347,13 @@
     flip = lambda blocks: [tuple(k ^ 1 for k in blocks)]
     away, fitted = exchange_rows(slab, fitted, owners, flip(out6 + out4 + out2), BF16, gather=True)
     leave = swap(away, 1)
-    away, _ = exchange_rows(slab, fitted, owners, flip(stay), BF16)
+    (away,) = exchange_rows(slab, fitted, owners, flip(stay), BF16)
     keep = swap(away, 1)
-    away6, away4, tie = exchange_rows(slab, fitted, owners, [out6, out4], BF16, more=leave)
+    away6, away4, tie = exchange_rows(slab, fitted, owners, [out6, out4], BF16, more=leave, tie=True)
     arrived = [swap(away6, 6), swap(away4, 4)]
-    away2, tie = exchange_rows(slab, fitted, owners, [out2], BF16, more=leave, skip=2 * len(far), after=tie)
+    away2, tie = exchange_rows(slab, fitted, owners, [out2], BF16, more=leave, skip=2 * len(far), after=tie, tie=True)
     arrived.append(swap(away2, 2))
-    near, _ = exchange_rows(slab, fitted, owners, [stay], F32, more=keep, after=tie)
+    (near,) = exchange_rows(slab, fitted, owners, [stay], F32, more=keep, after=tie)
     for x in arrived:
         near = near + x.astype(F32)
     total = near[0]

time: 69.2 us -> 69.2 us (level)
  Pallas kernels: 15 us -> 13.9 us
  waiting for transfers between devices: 6.4 us -> 7.33 us
    pallas_call x5, Pallas kernels: 5.2 us -> 4.16 us  [exchange_rows(): pl.pallas_call(functools.partial(exchange_kernel, blocks, gather, more is...]
    ppermute x6, waiting for transfers between devices: 6.4 us -> 7.33 us  [swap(): return lax.ppermute(x, 'aux', [(d, d ^ bits) for d in range(owners)])]
  transfers between devices with their start and end apart: 6 -> 6, of which waited for: 4 -> 5; matrix products, arithmetic and copies ran while one was open for 0% -> 0% of each run, Pallas kernels for 5% -> 4%
where the time goes in v16:
time: 69.2 us
  blocking collectives  40 us (58%)
  Pallas kernels  13.9 us (20%)
  waiting for transfers between devices  7.33 us (11%)
  starting transfers between devices  6.46 us (9%)
  between operations  0.71 us (1%)
    all_to_all x1, blocking collectives, body(): held = trade(pairs).reshape(naux, occupied // owners, occupied)  21.7 us
    all_to_all x1, blocking collectives, body(): fitted = trade(fitted.reshape(owners, q_dev, occupied // owners, occupied))  18.4 us
    pallas_call x1, Pallas kernels, half_transform(): pl.pallas_call(functools.partial(half_kernel, owners if split else 0, q_d...  9.17 us
    ppermute x6, waiting for transfers between devices, swap(): return lax.ppermute(x, 'aux', [(d, d ^ bits) for d in range(owners)])  7.33 us
    ppermute x6, starting transfers between devices, swap(): return lax.ppermute(x, 'aux', [(d, d ^ bits) for d in range(owners)])  6.46 us
    pallas_call x5, Pallas kernels, exchange_rows(): pl.pallas_call(functools.partial(exchange_kernel, blocks, gather, more is...  4.16 us
  transfers between devices with their start and end apart: 6, of which 5 were waited for; matrix products, arithmetic and copies ran while one was open for 0% of the time, Pallas kernels for 4%

profile of v16, /device:TPU:0, one launch (start us, length us, event | category | flops | bytes accessed | tf_op | source)
XLA Modules:
  0.0 69.2 jit_solution(570345699005657354)
XLA Ops:
  0.7 9.2 %half_transform_pairs.1 = (bf16[384,128,128]{2,1,0:T(8,128)(2,1)S(1)}, bf16[16,16,8,128]{3,2,1,0:T(8,128)(2,1)S(1)}, bf16[512,256]{1,0:T(8,128)(2,1)S(1)}) custom-call(s32[1]{0:T(128)S(6)} %copy.6.live_ref, s32[3,320]{1,0:T(4,128)} %bitcast.17, bf16[320,128,128]{2,1,0:T(8,128)(2,1)} %blocks_hbm.1, bf16[3072,128]{1,0:T(8,128)(2,1)} %orb_hbm.1, ...), custom_call_target="tpu_custom_call" | custom-call | flops 2952790016 | bytes 23068672 | tf_op jit(solution)/shard_map/half_transform_pairs/pallas_call | solution.py:196
  9.8 21.7 %all_to_all.10 = bf16[16,16,8,128]{3,2,1,0:T(8,128)(2,1)S(1)} all-to-all(bf16[16,16,8,128]{3,2,1,0:T(8,128)(2,1)S(1)} %get-tuple-element.17), channel_id=1, replica_groups=mesh['groups'=2,'aux'=16] {'aux'}, dimensions={0} | all-to-all | bytes 1048576 | tf_op jit(solution)/shard_map/all_to_all | solution.py:336
  31.5 0.6 apply_metric.1
  32.1 18.4 %all_to_all.11.fitted_ref = bf16[16,16,8,128]{3,2,1,0:T(8,128)(2,1)S(1)} all-to-all(bf16[16,16,8,128]{3,2,1,0:T(8,128)(2,1)S(1)} %bitcast.16), channel_id=1, replica_groups=mesh['groups'=2,'aux'=16] {'aux'}, dimensions={0} | all-to-all | bytes 1048576 | tf_op jit(solution)/shard_map/all_to_all | solution.py:338
  50.5 1.4 %exchange_rows.5 = (bf16[6,192,128]{2,1,0:T(8,128)(2,1)S(1)}, bf16[2048,128]{1,0:T(8,128)(2,1)S(1)}) custom-call(bf16[16,3072,128]{2,1,0:T(8,128)(2,1)S(1)} %bitcast.10, bf16[16,16,8,128]{3,2,1,0:T(8,128)(2,1)S(1)} %all_to_all.11.fitted_ref), custom_call_target="tpu_custom_call" | custom-call | flops 603979776 | bytes 4718592 | tf_op jit(solution)/shard_map/exchange_rows/pallas_call | solution.py:313
  51.9 0.1 collective-permute-start.1
  52.0 0.6 exchange_rows.6
  52.6 0.6 collective-permute-start
  53.1 0.4 collective-permute-done.1.refs_0_
  53.6 1.0 %exchange_rows.7 = (bf16[2,192,128]{2,1,0:T(8,128)(2,1)S(1)}, bf16[2,192,128]{2,1,0:T(8,128)(2,1)S(1)}, f32[8,128]{1,0:T(8,128)S(1)}) custom-call(bf16[16,3072,128]{2,1,0:T(8,128)(2,1)S(1)} %bitcast.12, bf16[2048,128]{1,0:T(8,128)(2,1)S(1)} %get-tuple-element.18.fitted_ref, bf16[6,192,128]{2,1,0:T(8,128)(2,1)S(1)} %collective-permute-done.1.refs_0_), custom_call_target="tpu_custom_call" | custom-call | flops 402653184 | bytes 3145728 | tf_op jit(solution)/shard_map/exchange_rows/pallas_call | solution.py:313
  54.6 0.6 exchange_rows.8
  55.1 0.9 %collective-permute-start.4 = (bf16[2,192,128]{2,1,0:T(8,128)(2,1)S(1)}, bf16[2,192,128]{2,1,0:T(8,128)(2,1)S(1)}, u32[]{:S(2)}, u32[]{:S(2)}) collective-permute-start(bf16[2,192,128]{2,1,0:T(8,128)(2,1)S(1)} %get-tuple-element.24), channel_id=1, source_target_pairs={{0,2},{1,3},{2,0},{3,1},{4,6},{5,7},{6,4},{7,5},{8,10},{9,11},{10,... | collective-permute-start | bytes 294920 | tf_op jit(solution)/shard_map/ppermute | solution.py:343
  56.0 2.0 %collective-permute-start.2 = (bf16[2,192,128]{2,1,0:T(8,128)(2,1)S(1)}, bf16[2,192,128]{2,1,0:T(8,128)(2,1)S(1)}, u32[]{:S(2)}, u32[]{:S(2)}) collective-permute-start(bf16[2,192,128]{2,1,0:T(8,128)(2,1)S(1)} %get-tuple-element.22), channel_id=1, source_target_pairs={{0,6},{1,7},{2,4},{3,5},{4,2},{5,3},{6,0},{7,1},{8,14},{9,15},{10,... | collective-permute-start | bytes 294920 | tf_op jit(solution)/shard_map/ppermute | solution.py:343
  58.1 0.6 collective-permute-start.3
  58.7 0.0 collective-permute-done.refs_0_
  58.7 0.6 exchange_rows.9
  59.3 2.4 %collective-permute-done.4 = bf16[2,192,128]{2,1,0:T(8,128)(2,1)S(1)} collective-permute-done((bf16[2,192,128]{2,1,0:T(8,128)(2,1)S(1)}, bf16[2,192,128]{2,1,0:T(8,128)(2,1)S(1)}, u32[]{:S(2)}, u32[]{:S(2)}) %collective-permute-start.4) | collective-permute-done | bytes 98336 | tf_op jit(solution)/shard_map/ppermute | solution.py:343
  61.7 0.9 %collective-permute-done.2 = bf16[2,192,128]{2,1,0:T(8,128)(2,1)S(1)} collective-permute-done((bf16[2,192,128]{2,1,0:T(8,128)(2,1)S(1)}, bf16[2,192,128]{2,1,0:T(8,128)(2,1)S(1)}, u32[]{:S(2)}, u32[]{:S(2)}) %collective-permute-start.2) | collective-permute-done | bytes 98336 | tf_op jit(solution)/shard_map/ppermute | solution.py:343
  62.6 0.8 %collective-permute-done.3 = bf16[2,192,128]{2,1,0:T(8,128)(2,1)S(1)} collective-permute-done((bf16[2,192,128]{2,1,0:T(8,128)(2,1)S(1)}, bf16[2,192,128]{2,1,0:T(8,128)(2,1)S(1)}, u32[]{:S(2)}, u32[]{:S(2)}) %collective-permute-start.3) | collective-permute-done | bytes 98336 | tf_op jit(solution)/shard_map/ppermute | solution.py:343
  63.5 2.3 %collective-permute-start.5 = (bf16[192,128]{1,0:T(8,128)(2,1)S(1)}, bf16[192,128]{1,0:T(8,128)(2,1)S(1)}, u32[]{:S(2)}, u32[]{:S(2)}) collective-permute-start(bf16[192,128]{1,0:T(8,128)(2,1)S(1)} %fusion.1), channel_id=1, source_target_pairs={{0,8},{1,9},{2,10},{3,11},{4,12},{5,13},{6,14},{7,15},{8,0},{9,1},... | collective-permute-start | bytes 147464 | tf_op jit(solution)/shard_map/ppermute | solution.py:343
  65.7 2.8 %collective-permute-done.5 = bf16[192,128]{1,0:T(8,128)(2,1)S(1)} collective-permute-done((bf16[192,128]{1,0:T(8,128)(2,1)S(1)}, bf16[192,128]{1,0:T(8,128)(2,1)S(1)}, u32[]{:S(2)}, u32[]{:S(2)}) %collective-permute-start.5) | collective-permute-done | bytes 49184 | tf_op jit(solution)/shard_map/ppermute | solution.py:343
  68.5 0.7 fusion
  (2 shorter events, 0.1 us)
Async XLA Ops:
  51.9 1.6 %collective-permute-start.1 = (bf16[6,192,128]{2,1,0:T(8,128)(2,1)S(1)}, bf16[6,192,128]{2,1,0:T(8,128)(2,1)S(1)}, u32[]{:S(2)}, u32[]{:S(2)}) collective-permute-start(bf16[6,192,128]{2,1,0:T(8,128)(2,1)S(1)} %get-tuple-element.19), channel_id=1, source_target_pairs={{0,1},{1,0},{2,3},{3,2},{4,5},{5,4},{6,7},{7,6},{8,9},{9,8},{10,11... | collective-permute-start | bytes 884744 | tf_op jit(solution)/shard_map/ppermute | solution.py:343
  52.6 6.1 %collective-permute-start = (bf16[2,192,128]{2,1,0:T(8,128)(2,1)S(1)}, bf16[2,192,128]{2,1,0:T(8,128)(2,1)S(1)}, u32[]{:S(2)}, u32[]{:S(2)}) collective-permute-start(bf16[2,192,128]{2,1,0:T(8,128)(2,1)S(1)} %exchange_rows.6), channel_id=1, source_target_pairs={{0,1},{1,0},{2,3},{3,2},{4,5},{5,4},{6,7},{7,6},{8,9},{9,8},{10,11... | collective-permute-start | bytes 294920 | tf_op jit(solution)/shard_map/ppermute | solution.py:343
  55.1 6.5 %collective-permute-start.4 = (bf16[2,192,128]{2,1,0:T(8,128)(2,1)S(1)}, bf16[2,192,128]{2,1,0:T(8,128)(2,1)S(1)}, u32[]{:S(2)}, u32[]{:S(2)}) collective-permute-start(bf16[2,192,128]{2,1,0:T(8,128)(2,1)S(1)} %get-tuple-element.24), channel_id=1, source_target_pairs={{0,2},{1,3},{2,0},{3,1},{4,6},{5,7},{6,4},{7,5},{8,10},{9,11},{10,... | collective-permute-start | bytes 294920 | tf_op jit(solution)/shard_map/ppermute | solution.py:343
  56.0 6.6 %collective-permute-start.2 = (bf16[2,192,128]{2,1,0:T(8,128)(2,1)S(1)}, bf16[2,192,128]{2,1,0:T(8,128)(2,1)S(1)}, u32[]{:S(2)}, u32[]{:S(2)}) collective-permute-start(bf16[2,192,128]{2,1,0:T(8,128)(2,1)S(1)} %get-tuple-element.22), channel_id=1, source_target_pairs={{0,6},{1,7},{2,4},{3,5},{4,2},{5,3},{6,0},{7,1},{8,14},{9,15},{10,... | collective-permute-start | bytes 294920 | tf_op jit(solution)/shard_map/ppermute | solution.py:343
  58.1 5.3 %collective-permute-start.3 = (bf16[2,192,128]{2,1,0:T(8,128)(2,1)S(1)}, bf16[2,192,128]{2,1,0:T(8,128)(2,1)S(1)}, u32[]{:S(2)}, u32[]{:S(2)}) collective-permute-start(bf16[2,192,128]{2,1,0:T(8,128)(2,1)S(1)} %get-tuple-element.23), channel_id=1, source_target_pairs={{0,4},{1,5},{2,6},{3,7},{4,0},{5,1},{6,2},{7,3},{8,12},{9,13},{10,... | collective-permute-start | bytes 294920 | tf_op jit(solution)/shard_map/ppermute | solution.py:343
  63.5 5.1 %collective-permute-start.5 = (bf16[192,128]{1,0:T(8,128)(2,1)S(1)}, bf16[192,128]{1,0:T(8,128)(2,1)S(1)}, u32[]{:S(2)}, u32[]{:S(2)}) collective-permute-start(bf16[192,128]{1,0:T(8,128)(2,1)S(1)} %fusion.1), channel_id=1, source_target_pairs={{0,8},{1,9},{2,10},{3,11},{4,12},{5,13},{6,14},{7,15},{8,0},{9,1},... | collective-permute-start | bytes 147464 | tf_op jit(solution)/shard_map/ppermute | solution.py:343

commit v17 on v13

--- a/solution.py
+++ b/solution.py
@@ -142,19 +142,12 @@
         lax.fori_loop(arrived, needed, arrive, 0)
         for u in range(TURNS):
             turn(jnp.minimum(g * TURNS + u, nblk - 1))
-        empty = jnp.zeros((size, occupied), BF16)
-        for u in range(0, UNROLL, 2):
-            pair = [facts[0, g * UNROLL + u + w] for w in range(2)]
-            orbs = [orb_ref[pl.ds(pl.multiple_of(((v >> 10) & 31) * size, size), size), :] for v in pair]
-            diagonal = jnp.concatenate(
-                [jnp.concatenate([orbs[0], empty], axis=1), jnp.concatenate([empty, orbs[1]], axis=1)], axis=0
-            )
-            blocks = jnp.concatenate([held[v >> 15] for v in pair], axis=1)
-            products = jnp.dot(blocks, diagonal, preferred_element_type=F32)
-            for w, v in enumerate(pair):
-                product = products[:, w * occupied : (w + 1) * occupied]
-                total = jnp.where((v & 1) == 1, product, total + product)
-                slab[(v & 1023) >> 1] = total.astype(BF16)
+        for u in range(UNROLL):
+            v = facts[0, g * UNROLL + u]
+            orbs = orb_ref[pl.ds(pl.multiple_of(((v >> 10) & 31) * size, size), size), :]
+            product = jnp.dot(held[v >> 15], orbs, preferred_element_type=F32)
+            total = jnp.where((v & 1) == 1, product, total + product)
+            slab[(v & 1023) >> 1] = total.astype(BF16)
         return needed, total
 
     bodies = (live_ref[0] + UNROLL - 1) // UNROLL

time: 69.3 us -> 69.1 us (level)
  no operation moved by 1% of the time
where the time goes in v17:
time: 69.1 us; the launch traced here: 68.9 us
  blocking collectives  40.4 us (58%)
  Pallas kernels  13.4 us (19%)
  waiting for transfers between devices  7.34 us (11%)
  starting transfers between devices  6.46 us (9%)
  between operations  0.71 us (1%)
    all_to_all x1, blocking collectives, body(): held = trade(pairs).reshape(naux, occupied // owners, occupied)  22 us
    all_to_all x1, blocking collectives, body(): fitted = trade(fitted.reshape(owners, q_dev, occupied // owners, occupied))  18.4 us
    pallas_call x1, Pallas kernels, half_transform(): pl.pallas_call(functools.partial(half_kernel, owners if split else 0, q_d...  8.77 us
    ppermute x6, waiting for transfers between devices, swap(): return lax.ppermute(x, 'aux', [(d, d ^ bits) for d in range(owners)])  7.34 us
    ppermute x6, starting transfers between devices, swap(): return lax.ppermute(x, 'aux', [(d, d ^ bits) for d in range(owners)])  6.46 us
    pallas_call x4, Pallas kernels, exchange_rows(): pl.pallas_call(functools.partial(exchange_kernel, blocks, gather, more is...  3.97 us
  transfers between devices with their start and end apart: 6, of which 5 were waited for; matrix products, arithmetic and copies ran while one was open for 0% of the time, Pallas kernels for 4%

profile of v17, /device:TPU:0, one launch (start us, length us, event | category | flops | bytes accessed | tf_op | source)
XLA Modules:
  0.0 68.9 jit_solution(7885622414110270238)
XLA Ops:
  0.7 8.8 %half_transform_pairs.1 = (bf16[384,128,128]{2,1,0:T(8,128)(2,1)S(1)}, bf16[16,16,8,128]{3,2,1,0:T(8,128)(2,1)S(1)}, bf16[512,256]{1,0:T(8,128)(2,1)S(1)}) custom-call(s32[1]{0:T(128)S(6)} %copy.6.live_ref, s32[3,320]{1,0:T(4,128)} %bitcast.16, bf16[320,128,128]{2,1,0:T(8,128)(2,1)} %blocks_hbm.1, bf16[3072,128]{1,0:T(8,128)(2,1)} %orb_hbm.1, ...), custom_call_target="tpu_custom_call" | custom-call | flops 2952790016 | bytes 23068672 | tf_op jit(solution)/shard_map/half_transform_pairs/pallas_call | solution.py:189
  9.4 22.0 %all_to_all.10 = bf16[16,16,8,128]{3,2,1,0:T(8,128)(2,1)S(1)} all-to-all(bf16[16,16,8,128]{3,2,1,0:T(8,128)(2,1)S(1)} %get-tuple-element.15), channel_id=1, replica_groups=mesh['groups'=2,'aux'=16] {'aux'}, dimensions={0} | all-to-all | bytes 1048576 | tf_op jit(solution)/shard_map/all_to_all | solution.py:323
  31.4 0.6 apply_metric.1
  32.1 18.4 %all_to_all.11.fitted_ref = bf16[16,16,8,128]{3,2,1,0:T(8,128)(2,1)S(1)} all-to-all(bf16[16,16,8,128]{3,2,1,0:T(8,128)(2,1)S(1)} %bitcast.15), channel_id=1, replica_groups=mesh['groups'=2,'aux'=16] {'aux'}, dimensions={0} | all-to-all | bytes 1048576 | tf_op jit(solution)/shard_map/all_to_all | solution.py:325
  50.4 1.4 %exchange_rows.4 = (bf16[6,192,128]{2,1,0:T(8,128)(2,1)S(1)}, bf16[2048,128]{1,0:T(8,128)(2,1)S(1)}) custom-call(bf16[16,3072,128]{2,1,0:T(8,128)(2,1)S(1)} %bitcast.10, bf16[16,16,8,128]{3,2,1,0:T(8,128)(2,1)S(1)} %all_to_all.11.fitted_ref), custom_call_target="tpu_custom_call" | custom-call | flops 603979776 | bytes 4718592 | tf_op jit(solution)/shard_map/exchange_rows/pallas_call | solution.py:300
  51.9 0.1 collective-permute-start.1
  51.9 0.6 exchange_rows.5
  52.5 0.6 collective-permute-start
  53.1 0.4 collective-permute-done.1.refs_0_
  53.5 1.4 %exchange_rows.7 = (bf16[2,192,128]{2,1,0:T(8,128)(2,1)S(1)}, bf16[2,192,128]{2,1,0:T(8,128)(2,1)S(1)}, bf16[2,192,128]{2,1,0:T(8,128)(2,1)S(1)}) custom-call(bf16[16,3072,128]{2,1,0:T(8,128)(2,1)S(1)} %bitcast.12, bf16[2048,128]{1,0:T(8,128)(2,1)S(1)} %get-tuple-element.16.fitted_ref, bf16[6,192,128]{2,1,0:T(8,128)(2,1)S(1)} %collective-permute-done.1.refs_0_), custom_call_target="tpu_custom_call" | custom-call | flops 603979776 | bytes 4718592 | tf_op jit(solution)/shard_map/exchange_rows/pallas_call | solution.py:300
  54.9 0.9 %collective-permute-start.2 = (bf16[2,192,128]{2,1,0:T(8,128)(2,1)S(1)}, bf16[2,192,128]{2,1,0:T(8,128)(2,1)S(1)}, u32[]{:S(2)}, u32[]{:S(2)}) collective-permute-start(bf16[2,192,128]{2,1,0:T(8,128)(2,1)S(1)} %get-tuple-element.18), channel_id=1, source_target_pairs={{0,2},{1,3},{2,0},{3,1},{4,6},{5,7},{6,4},{7,5},{8,10},{9,11},{10,... | collective-permute-start | bytes 294920 | tf_op jit(solution)/shard_map/ppermute | solution.py:330
  55.8 1.6 %collective-permute-start.3 = (bf16[2,192,128]{2,1,0:T(8,128)(2,1)S(1)}, bf16[2,192,128]{2,1,0:T(8,128)(2,1)S(1)}, u32[]{:S(2)}, u32[]{:S(2)}) collective-permute-start(bf16[2,192,128]{2,1,0:T(8,128)(2,1)S(1)} %get-tuple-element.19), channel_id=1, source_target_pairs={{0,4},{1,5},{2,6},{3,7},{4,0},{5,1},{6,2},{7,3},{8,12},{9,13},{10,... | collective-permute-start | bytes 294920 | tf_op jit(solution)/shard_map/ppermute | solution.py:330
  57.3 1.1 %collective-permute-start.4 = (bf16[2,192,128]{2,1,0:T(8,128)(2,1)S(1)}, bf16[2,192,128]{2,1,0:T(8,128)(2,1)S(1)}, u32[]{:S(2)}, u32[]{:S(2)}) collective-permute-start(bf16[2,192,128]{2,1,0:T(8,128)(2,1)S(1)} %get-tuple-element.20), channel_id=1, source_target_pairs={{0,6},{1,7},{2,4},{3,5},{4,2},{5,3},{6,0},{7,1},{8,14},{9,15},{10,... | collective-permute-start | bytes 294920 | tf_op jit(solution)/shard_map/ppermute | solution.py:330
  58.5 0.0 collective-permute-done.refs_0_
  58.5 0.6 exchange_rows.6
  59.0 0.8 %collective-permute-done.2 = bf16[2,192,128]{2,1,0:T(8,128)(2,1)S(1)} collective-permute-done((bf16[2,192,128]{2,1,0:T(8,128)(2,1)S(1)}, bf16[2,192,128]{2,1,0:T(8,128)(2,1)S(1)}, u32[]{:S(2)}, u32[]{:S(2)}) %collective-permute-start.2) | collective-permute-done | bytes 98336 | tf_op jit(solution)/shard_map/ppermute | solution.py:330
  59.8 1.1 %collective-permute-done.3 = bf16[2,192,128]{2,1,0:T(8,128)(2,1)S(1)} collective-permute-done((bf16[2,192,128]{2,1,0:T(8,128)(2,1)S(1)}, bf16[2,192,128]{2,1,0:T(8,128)(2,1)S(1)}, u32[]{:S(2)}, u32[]{:S(2)}) %collective-permute-start.3) | collective-permute-done | bytes 98336 | tf_op jit(solution)/shard_map/ppermute | solution.py:330
  60.9 2.2 %collective-permute-done.4 = bf16[2,192,128]{2,1,0:T(8,128)(2,1)S(1)} collective-permute-done((bf16[2,192,128]{2,1,0:T(8,128)(2,1)S(1)}, bf16[2,192,128]{2,1,0:T(8,128)(2,1)S(1)}, u32[]{:S(2)}, u32[]{:S(2)}) %collective-permute-start.4) | collective-permute-done | bytes 98336 | tf_op jit(solution)/shard_map/ppermute | solution.py:330
  63.2 2.3 %collective-permute-start.5 = (bf16[192,128]{1,0:T(8,128)(2,1)S(1)}, bf16[192,128]{1,0:T(8,128)(2,1)S(1)}, u32[]{:S(2)}, u32[]{:S(2)}) collective-permute-start(bf16[192,128]{1,0:T(8,128)(2,1)S(1)} %fusion.1), channel_id=1, source_target_pairs={{0,8},{1,9},{2,10},{3,11},{4,12},{5,13},{6,14},{7,15},{8,0},{9,1},... | collective-permute-start | bytes 147464 | tf_op jit(solution)/shard_map/ppermute | solution.py:330
  65.5 2.8 %collective-permute-done.5 = bf16[192,128]{1,0:T(8,128)(2,1)S(1)} collective-permute-done((bf16[192,128]{1,0:T(8,128)(2,1)S(1)}, bf16[192,128]{1,0:T(8,128)(2,1)S(1)}, u32[]{:S(2)}, u32[]{:S(2)}) %collective-permute-start.5) | collective-permute-done | bytes 49184 | tf_op jit(solution)/shard_map/ppermute | solution.py:330
  68.3 0.7 fusion
  (2 shorter events, 0.1 us)
Async XLA Ops:
  51.9 1.6 %collective-permute-start.1 = (bf16[6,192,128]{2,1,0:T(8,128)(2,1)S(1)}, bf16[6,192,128]{2,1,0:T(8,128)(2,1)S(1)}, u32[]{:S(2)}, u32[]{:S(2)}) collective-permute-start(bf16[6,192,128]{2,1,0:T(8,128)(2,1)S(1)} %get-tuple-element.17), channel_id=1, source_target_pairs={{0,1},{1,0},{2,3},{3,2},{4,5},{5,4},{6,7},{7,6},{8,9},{9,8},{10,11... | collective-permute-start | bytes 884744 | tf_op jit(solution)/shard_map/ppermute | solution.py:330
  52.5 6.0 %collective-permute-start = (bf16[2,192,128]{2,1,0:T(8,128)(2,1)S(1)}, bf16[2,192,128]{2,1,0:T(8,128)(2,1)S(1)}, u32[]{:S(2)}, u32[]{:S(2)}) collective-permute-start(bf16[2,192,128]{2,1,0:T(8,128)(2,1)S(1)} %exchange_rows.5), channel_id=1, source_target_pairs={{0,1},{1,0},{2,3},{3,2},{4,5},{5,4},{6,7},{7,6},{8,9},{9,8},{10,11... | collective-permute-start | bytes 294920 | tf_op jit(solution)/shard_map/ppermute | solution.py:330
  54.9 4.9 %collective-permute-start.2 = (bf16[2,192,128]{2,1,0:T(8,128)(2,1)S(1)}, bf16[2,192,128]{2,1,0:T(8,128)(2,1)S(1)}, u32[]{:S(2)}, u32[]{:S(2)}) collective-permute-start(bf16[2,192,128]{2,1,0:T(8,128)(2,1)S(1)} %get-tuple-element.18), channel_id=1, source_target_pairs={{0,2},{1,3},{2,0},{3,1},{4,6},{5,7},{6,4},{7,5},{8,10},{9,11},{10,... | collective-permute-start | bytes 294920 | tf_op jit(solution)/shard_map/ppermute | solution.py:330
  55.8 5.1 %collective-permute-start.3 = (bf16[2,192,128]{2,1,0:T(8,128)(2,1)S(1)}, bf16[2,192,128]{2,1,0:T(8,128)(2,1)S(1)}, u32[]{:S(2)}, u32[]{:S(2)}) collective-permute-start(bf16[2,192,128]{2,1,0:T(8,128)(2,1)S(1)} %get-tuple-element.19), channel_id=1, source_target_pairs={{0,4},{1,5},{2,6},{3,7},{4,0},{5,1},{6,2},{7,3},{8,12},{9,13},{10,... | collective-permute-start | bytes 294920 | tf_op jit(solution)/shard_map/ppermute | solution.py:330
  57.3 5.8 %collective-permute-start.4 = (bf16[2,192,128]{2,1,0:T(8,128)(2,1)S(1)}, bf16[2,192,128]{2,1,0:T(8,128)(2,1)S(1)}, u32[]{:S(2)}, u32[]{:S(2)}) collective-permute-start(bf16[2,192,128]{2,1,0:T(8,128)(2,1)S(1)} %get-tuple-element.20), channel_id=1, source_target_pairs={{0,6},{1,7},{2,4},{3,5},{4,2},{5,3},{6,0},{7,1},{8,14},{9,15},{10,... | collective-permute-start | bytes 294920 | tf_op jit(solution)/shard_map/ppermute | solution.py:330
  63.2 5.1 %collective-permute-start.5 = (bf16[192,128]{1,0:T(8,128)(2,1)S(1)}, bf16[192,128]{1,0:T(8,128)(2,1)S(1)}, u32[]{:S(2)}, u32[]{:S(2)}) collective-permute-start(bf16[192,128]{1,0:T(8,128)(2,1)S(1)} %fusion.1), channel_id=1, source_target_pairs={{0,8},{1,9},{2,10},{3,11},{4,12},{5,13},{6,14},{7,15},{8,0},{9,1},... | collective-permute-start | bytes 147464 | tf_op jit(solution)/shard_map/ppermute | solution.py:330

commit v18 on v13

--- a/solution.py
+++ b/solution.py
@@ -10,7 +10,7 @@
 UNROLL = 64
 CHUNK = 32
 TURNS = 5
-FLIGHT = 4
+FLIGHT = 3
 F32 = jnp.float32
 BF16 = jnp.bfloat16
 

time: 69.3 us -> 69.7 us (level)
  Pallas kernels: 13.7 us -> 14.8 us
  blocking collectives: 40.6 us -> 39.5 us
    all_to_all x1, blocking collectives: 22.2 us -> 21.1 us  [body(): held = trade(pairs).reshape(naux, occupied // owners, occupied)]
    pallas_call x1, Pallas kernels: 9.17 us -> 10.2 us  [half_transform(): pl.pallas_call(functools.partial(half_kernel, owners if split else 0, q_d...]
where the time goes in v18:
time: 69.7 us; the launch traced here: 69.5 us
  blocking collectives  39.5 us (57%)
  Pallas kernels  14.8 us (21%)
  waiting for transfers between devices  7.34 us (11%)
  starting transfers between devices  6.46 us (9%)
  between operations  0.71 us (1%)
    all_to_all x1, blocking collectives, body(): held = trade(pairs).reshape(naux, occupied // owners, occupied)  21.1 us
    all_to_all x1, blocking collectives, body(): fitted = trade(fitted.reshape(owners, q_dev, occupied // owners, occupied))  18.4 us
    pallas_call x1, Pallas kernels, half_transform(): pl.pallas_call(functools.partial(half_kernel, owners if split else 0, q_d...  10.2 us
    ppermute x6, waiting for transfers between devices, swap(): return lax.ppermute(x, 'aux', [(d, d ^ bits) for d in range(owners)])  7.34 us
    ppermute x6, starting transfers between devices, swap(): return lax.ppermute(x, 'aux', [(d, d ^ bits) for d in range(owners)])  6.46 us
    pallas_call x4, Pallas kernels, exchange_rows(): pl.pallas_call(functools.partial(exchange_kernel, blocks, gather, more is...  3.97 us
  transfers between devices with their start and end apart: 6, of which 5 were waited for; matrix products, arithmetic and copies ran while one was open for 0% of the time, Pallas kernels for 4%

profile of v18, /device:TPU:0, one launch (start us, length us, event | category | flops | bytes accessed | tf_op | source)
XLA Modules:
  0.0 69.5 jit_solution(3143277883748453238)
XLA Ops:
  0.7 10.2 %half_transform_pairs.1 = (bf16[384,128,128]{2,1,0:T(8,128)(2,1)S(1)}, bf16[16,16,8,128]{3,2,1,0:T(8,128)(2,1)S(1)}, bf16[512,256]{1,0:T(8,128)(2,1)S(1)}) custom-call(s32[1]{0:T(128)S(6)} %copy.6.live_ref, s32[3,320]{1,0:T(4,128)} %bitcast.16, bf16[320,128,128]{2,1,0:T(8,128)(2,1)} %blocks_hbm.1, bf16[3072,128]{1,0:T(8,128)(2,1)} %orb_hbm.1, ...), custom_call_target="tpu_custom_call" | custom-call | flops 2952790016 | bytes 23068672 | tf_op jit(solution)/shard_map/half_transform_pairs/pallas_call | solution.py:196
  10.9 21.1 %all_to_all.10 = bf16[16,16,8,128]{3,2,1,0:T(8,128)(2,1)S(1)} all-to-all(bf16[16,16,8,128]{3,2,1,0:T(8,128)(2,1)S(1)} %get-tuple-element.15), channel_id=1, replica_groups=mesh['groups'=2,'aux'=16] {'aux'}, dimensions={0} | all-to-all | bytes 1048576 | tf_op jit(solution)/shard_map/all_to_all | solution.py:330
  32.0 0.6 apply_metric.1
  32.6 18.4 %all_to_all.11.fitted_ref = bf16[16,16,8,128]{3,2,1,0:T(8,128)(2,1)S(1)} all-to-all(bf16[16,16,8,128]{3,2,1,0:T(8,128)(2,1)S(1)} %bitcast.15), channel_id=1, replica_groups=mesh['groups'=2,'aux'=16] {'aux'}, dimensions={0} | all-to-all | bytes 1048576 | tf_op jit(solution)/shard_map/all_to_all | solution.py:332
  51.0 1.4 %exchange_rows.4 = (bf16[6,192,128]{2,1,0:T(8,128)(2,1)S(1)}, bf16[2048,128]{1,0:T(8,128)(2,1)S(1)}) custom-call(bf16[16,3072,128]{2,1,0:T(8,128)(2,1)S(1)} %bitcast.10, bf16[16,16,8,128]{3,2,1,0:T(8,128)(2,1)S(1)} %all_to_all.11.fitted_ref), custom_call_target="tpu_custom_call" | custom-call | flops 603979776 | bytes 4718592 | tf_op jit(solution)/shard_map/exchange_rows/pallas_call | solution.py:307
  52.4 0.1 collective-permute-start.1
  52.5 0.6 exchange_rows.5
  53.1 0.6 collective-permute-start
  53.6 0.4 collective-permute-done.1.refs_0_
  54.1 1.4 %exchange_rows.7 = (bf16[2,192,128]{2,1,0:T(8,128)(2,1)S(1)}, bf16[2,192,128]{2,1,0:T(8,128)(2,1)S(1)}, bf16[2,192,128]{2,1,0:T(8,128)(2,1)S(1)}) custom-call(bf16[16,3072,128]{2,1,0:T(8,128)(2,1)S(1)} %bitcast.12, bf16[2048,128]{1,0:T(8,128)(2,1)S(1)} %get-tuple-element.16.fitted_ref, bf16[6,192,128]{2,1,0:T(8,128)(2,1)S(1)} %collective-permute-done.1.refs_0_), custom_call_target="tpu_custom_call" | custom-call | flops 603979776 | bytes 4718592 | tf_op jit(solution)/shard_map/exchange_rows/pallas_call | solution.py:307
  55.5 0.9 %collective-permute-start.2 = (bf16[2,192,128]{2,1,0:T(8,128)(2,1)S(1)}, bf16[2,192,128]{2,1,0:T(8,128)(2,1)S(1)}, u32[]{:S(2)}, u32[]{:S(2)}) collective-permute-start(bf16[2,192,128]{2,1,0:T(8,128)(2,1)S(1)} %get-tuple-element.18), channel_id=1, source_target_pairs={{0,2},{1,3},{2,0},{3,1},{4,6},{5,7},{6,4},{7,5},{8,10},{9,11},{10,... | collective-permute-start | bytes 294920 | tf_op jit(solution)/shard_map/ppermute | solution.py:337
  56.3 1.6 %collective-permute-start.3 = (bf16[2,192,128]{2,1,0:T(8,128)(2,1)S(1)}, bf16[2,192,128]{2,1,0:T(8,128)(2,1)S(1)}, u32[]{:S(2)}, u32[]{:S(2)}) collective-permute-start(bf16[2,192,128]{2,1,0:T(8,128)(2,1)S(1)} %get-tuple-element.19), channel_id=1, source_target_pairs={{0,4},{1,5},{2,6},{3,7},{4,0},{5,1},{6,2},{7,3},{8,12},{9,13},{10,... | collective-permute-start | bytes 294920 | tf_op jit(solution)/shard_map/ppermute | solution.py:337
  57.9 1.1 %collective-permute-start.4 = (bf16[2,192,128]{2,1,0:T(8,128)(2,1)S(1)}, bf16[2,192,128]{2,1,0:T(8,128)(2,1)S(1)}, u32[]{:S(2)}, u32[]{:S(2)}) collective-permute-start(bf16[2,192,128]{2,1,0:T(8,128)(2,1)S(1)} %get-tuple-element.20), channel_id=1, source_target_pairs={{0,6},{1,7},{2,4},{3,5},{4,2},{5,3},{6,0},{7,1},{8,14},{9,15},{10,... | collective-permute-start | bytes 294920 | tf_op jit(solution)/shard_map/ppermute | solution.py:337
  59.0 0.0 collective-permute-done.refs_0_
  59.0 0.6 exchange_rows.6
  59.6 0.8 %collective-permute-done.2 = bf16[2,192,128]{2,1,0:T(8,128)(2,1)S(1)} collective-permute-done((bf16[2,192,128]{2,1,0:T(8,128)(2,1)S(1)}, bf16[2,192,128]{2,1,0:T(8,128)(2,1)S(1)}, u32[]{:S(2)}, u32[]{:S(2)}) %collective-permute-start.2) | collective-permute-done | bytes 98336 | tf_op jit(solution)/shard_map/ppermute | solution.py:337
  60.4 1.1 %collective-permute-done.3 = bf16[2,192,128]{2,1,0:T(8,128)(2,1)S(1)} collective-permute-done((bf16[2,192,128]{2,1,0:T(8,128)(2,1)S(1)}, bf16[2,192,128]{2,1,0:T(8,128)(2,1)S(1)}, u32[]{:S(2)}, u32[]{:S(2)}) %collective-permute-start.3) | collective-permute-done | bytes 98336 | tf_op jit(solution)/shard_map/ppermute | solution.py:337
  61.5 2.2 %collective-permute-done.4 = bf16[2,192,128]{2,1,0:T(8,128)(2,1)S(1)} collective-permute-done((bf16[2,192,128]{2,1,0:T(8,128)(2,1)S(1)}, bf16[2,192,128]{2,1,0:T(8,128)(2,1)S(1)}, u32[]{:S(2)}, u32[]{:S(2)}) %collective-permute-start.4) | collective-permute-done | bytes 98336 | tf_op jit(solution)/shard_map/ppermute | solution.py:337
  63.8 2.3 %collective-permute-start.5 = (bf16[192,128]{1,0:T(8,128)(2,1)S(1)}, bf16[192,128]{1,0:T(8,128)(2,1)S(1)}, u32[]{:S(2)}, u32[]{:S(2)}) collective-permute-start(bf16[192,128]{1,0:T(8,128)(2,1)S(1)} %fusion.1), channel_id=1, source_target_pairs={{0,8},{1,9},{2,10},{3,11},{4,12},{5,13},{6,14},{7,15},{8,0},{9,1},... | collective-permute-start | bytes 147464 | tf_op jit(solution)/shard_map/ppermute | solution.py:337
  66.0 2.8 %collective-permute-done.5 = bf16[192,128]{1,0:T(8,128)(2,1)S(1)} collective-permute-done((bf16[192,128]{1,0:T(8,128)(2,1)S(1)}, bf16[192,128]{1,0:T(8,128)(2,1)S(1)}, u32[]{:S(2)}, u32[]{:S(2)}) %collective-permute-start.5) | collective-permute-done | bytes 49184 | tf_op jit(solution)/shard_map/ppermute | solution.py:337
  68.8 0.7 fusion
  (2 shorter events, 0.1 us)
Async XLA Ops:
  52.4 1.6 %collective-permute-start.1 = (bf16[6,192,128]{2,1,0:T(8,128)(2,1)S(1)}, bf16[6,192,128]{2,1,0:T(8,128)(2,1)S(1)}, u32[]{:S(2)}, u32[]{:S(2)}) collective-permute-start(bf16[6,192,128]{2,1,0:T(8,128)(2,1)S(1)} %get-tuple-element.17), channel_id=1, source_target_pairs={{0,1},{1,0},{2,3},{3,2},{4,5},{5,4},{6,7},{7,6},{8,9},{9,8},{10,11... | collective-permute-start | bytes 884744 | tf_op jit(solution)/shard_map/ppermute | solution.py:337
  53.1 6.0 %collective-permute-start = (bf16[2,192,128]{2,1,0:T(8,128)(2,1)S(1)}, bf16[2,192,128]{2,1,0:T(8,128)(2,1)S(1)}, u32[]{:S(2)}, u32[]{:S(2)}) collective-permute-start(bf16[2,192,128]{2,1,0:T(8,128)(2,1)S(1)} %exchange_rows.5), channel_id=1, source_target_pairs={{0,1},{1,0},{2,3},{3,2},{4,5},{5,4},{6,7},{7,6},{8,9},{9,8},{10,11... | collective-permute-start | bytes 294920 | tf_op jit(solution)/shard_map/ppermute | solution.py:337
  55.5 4.9 %collective-permute-start.2 = (bf16[2,192,128]{2,1,0:T(8,128)(2,1)S(1)}, bf16[2,192,128]{2,1,0:T(8,128)(2,1)S(1)}, u32[]{:S(2)}, u32[]{:S(2)}) collective-permute-start(bf16[2,192,128]{2,1,0:T(8,128)(2,1)S(1)} %get-tuple-element.18), channel_id=1, source_target_pairs={{0,2},{1,3},{2,0},{3,1},{4,6},{5,7},{6,4},{7,5},{8,10},{9,11},{10,... | collective-permute-start | bytes 294920 | tf_op jit(solution)/shard_map/ppermute | solution.py:337
  56.3 5.1 %collective-permute-start.3 = (bf16[2,192,128]{2,1,0:T(8,128)(2,1)S(1)}, bf16[2,192,128]{2,1,0:T(8,128)(2,1)S(1)}, u32[]{:S(2)}, u32[]{:S(2)}) collective-permute-start(bf16[2,192,128]{2,1,0:T(8,128)(2,1)S(1)} %get-tuple-element.19), channel_id=1, source_target_pairs={{0,4},{1,5},{2,6},{3,7},{4,0},{5,1},{6,2},{7,3},{8,12},{9,13},{10,... | collective-permute-start | bytes 294920 | tf_op jit(solution)/shard_map/ppermute | solution.py:337
  57.9 5.8 %collective-permute-start.4 = (bf16[2,192,128]{2,1,0:T(8,128)(2,1)S(1)}, bf16[2,192,128]{2,1,0:T(8,128)(2,1)S(1)}, u32[]{:S(2)}, u32[]{:S(2)}) collective-permute-start(bf16[2,192,128]{2,1,0:T(8,128)(2,1)S(1)} %get-tuple-element.20), channel_id=1, source_target_pairs={{0,6},{1,7},{2,4},{3,5},{4,2},{5,3},{6,0},{7,1},{8,14},{9,15},{10,... | collective-permute-start | bytes 294920 | tf_op jit(solution)/shard_map/ppermute | solution.py:337
  63.8 5.1 %collective-permute-start.5 = (bf16[192,128]{1,0:T(8,128)(2,1)S(1)}, bf16[192,128]{1,0:T(8,128)(2,1)S(1)}, u32[]{:S(2)}, u32[]{:S(2)}) collective-permute-start(bf16[192,128]{1,0:T(8,128)(2,1)S(1)} %fusion.1), channel_id=1, source_target_pairs={{0,8},{1,9},{2,10},{3,11},{4,12},{5,13},{6,14},{7,15},{8,0},{9,1},... | collective-permute-start | bytes 147464 | tf_op jit(solution)/shard_map/ppermute | solution.py:337
